TPU v7x, 512 devices: a whole 4x8x8 slice. The times are simulated.
512 devices in a mesh: section: 2 (over core), row: 8 (over y), col: 32 (over x, z).
Axes of the slice: x: 4, y: 8, z: 8, core: 2. Of those that a mesh axis runs over, the one named last changes fastest.
Arguments:
- x_stash: bfloat16 [2, 1, 128, 16384], P('section', None, 'col', 'row'), may hold values from -6 to 6
- out_grad: bfloat16 [1, 128, 16384], P(None, 'col', 'row'), may hold values from -6 to 6
- in_values: bfloat16 [2, 8, 32, 64, 64, 128], P('section', 'row', 'col'), as said below
- in_index: int32 [2, 8, 32, 2, 128], P('section', 'row', 'col'), may hold values from 0 to 31, as said below
- out_values: bfloat16 [2, 8, 32, 64, 64, 128], P('section', 'row', 'col'), as said below
- out_index: int32 [2, 8, 32, 2, 128], P('section', 'row', 'col'), may hold values from 0 to 31, as said below
Outputs:
- in_grad: bfloat16 [2, 1, 128, 16384], P('section', None, 'col', 'row')
Inputs may be any that keep to these rules, and one draw needn't show every extreme that they name: `in_index`: the slots of one tile name distinct blocks. Each tile holds between 32 and 128 nonzero blocks in its first slots, and its later slots of in_values (out_values) are zero; in every draw one tile of each layer's matrix fills all 128 slots, and which one is drawn. `out_index`: same law as in_index, drawn apart. `in_values`: slots past a tile's count of nonzero blocks are zero. `out_values`: slots past a tile's count of nonzero blocks are zero.
All inputs are finite; a program needn't handle non-finite values.
Results may differ from a plain program's by a relative error of at most 0.034.
Values may be sent and summed in bfloat16 or wider, within the bound.
No kernel may reach another device: no remote copies, remote signals or barrier semaphores. Data moves between devices by JAX's collectives and lax.ppermute only.
A program may use at most 64 MiB of HBM per device.

v0:
```python
import jax
import jax.numpy as jnp
from jax import lax
from jax.sharding import PartitionSpec as P

FF = 65536


forward_form = "tnk,nkj->tnj"
backward_form = "tnj,nkj->tnk"


def passed_along(x, axis, by):
    size = lax.axis_size(axis)
    pairs = [(i, i + by) for i in range(size) if 0 <= i + by < size]
    return lax.ppermute(x, axis, pairs)


def unpair(values):
    pairs = values.shape[0]
    block_size = values.shape[1]
    split = values.reshape(pairs, block_size, 2, block_size)
    moved = jnp.swapaxes(split, 1, 2)
    return moved.reshape(pairs * 2, block_size, block_size)


def tile_product(operand, values, source, target, blocks_out, pattern):
    block_size = values.shape[-1]
    picked = operand.reshape(operand.shape[0], -1, block_size)[:, source]
    products = jnp.einsum(pattern, picked, values, preferred_element_type=jnp.float32)
    summed = (
        jnp.zeros((operand.shape[0], blocks_out, block_size), jnp.float32)
        .at[:, target]
        .add(products)
    )
    return summed.reshape(operand.shape[0], blocks_out * block_size)


def gelu_slope(hidden):
    return (
        0.5 * (1.0 + lax.erf(hidden * 0.7071067811865476))
        + hidden * jnp.exp(-0.5 * hidden * hidden) * 0.3989422804014327
    )


def local(x_stash, out_grad, in_values, in_index, out_values, out_index):
    section_id = lax.axis_index("section")
    is_last = section_id == 1
    micro_total = x_stash.shape[1]
    tok_share = x_stash.shape[2]
    width_share = x_stash.shape[3]
    block_size = in_values.shape[-2]
    side_cols = FF // lax.axis_size("col") // block_size
    side_rows = width_share // block_size
    in_v = unpair(in_values[0, 0, 0])
    in_rows = in_index[0, 0, 0, 0]
    in_cols = in_index[0, 0, 0, 1]
    out_v = unpair(out_values[0, 0, 0])
    out_rows = out_index[0, 0, 0, 0]
    out_cols = out_index[0, 0, 0, 1]

    def hidden_of(shard_rows):
        return tile_product(shard_rows, in_v, in_rows, in_cols, side_cols, forward_form)

    def gate_of(shard_rows):
        return tile_product(shard_rows, out_v, out_rows, out_cols, side_cols, forward_form)

    def advance(tick_now, state_pair):
        outgoing, result = state_pair
        incoming = passed_along(outgoing, "section", -1)
        micro_idx = jnp.where(is_last, tick_now, tick_now - 1)
        active = (micro_idx >= 0) & (micro_idx < micro_total)
        micro_safe = jnp.clip(micro_idx, 0, micro_total - 1)
        upstream = jnp.where(
            is_last, lax.dynamic_index_in_dim(out_grad, micro_safe, 0, False), incoming
        )
        stash_now = lax.dynamic_index_in_dim(x_stash[0], micro_safe, 0, False)
        hidden_part = hidden_of(lax.all_gather(stash_now, "col", axis=0, tiled=True))
        gate_part = gate_of(lax.all_gather(upstream, "col", axis=0, tiled=True))
        hidden, gate_grad = (
            lax.psum(hidden_part.astype(jnp.bfloat16), "row").astype(jnp.float32),
            lax.psum(gate_part.astype(jnp.bfloat16), "row").astype(jnp.float32),
        )
        hidden_grad = (gate_grad * gelu_slope(hidden)).astype(jnp.bfloat16)
        input_part = lax.psum_scatter(
            tile_product(hidden_grad, in_v, in_cols, in_rows, side_rows, backward_form).astype(
                jnp.bfloat16
            ),
            "col",
            scatter_dimension=0,
            tiled=True,
        ).astype(jnp.float32)
        fresh = (upstream.astype(jnp.float32) + input_part).astype(jnp.bfloat16)
        updated = lax.dynamic_update_index_in_dim(result, fresh, micro_safe, 0)
        result = jnp.where(active, updated, result)
        return (fresh, result)

    outgoing = jnp.zeros((tok_share, width_share), jnp.bfloat16)
    result = jnp.zeros((micro_total, tok_share, width_share), jnp.bfloat16)
    outgoing, result = lax.fori_loop(0, micro_total + 1, advance, (outgoing, result))
    return result[None]


def solution(mesh):
    in_specs = (
        P("section", None, "col", "row"),
        P(None, "col", "row"),
        P("section", "row", "col", None, None, None),
        P("section", "row", "col", None, None),
        P("section", "row", "col", None, None, None),
        P("section", "row", "col", None, None),
    )
    out_specs = P("section", None, "col", "row")
    return jax.shard_map(local, mesh=mesh, in_specs=in_specs, out_specs=out_specs, check_vma=False)
```

profile of v0, /device:TPU:1, one launch (start us, length us, event | category | flops | bytes accessed | tf_op | source)
XLA Modules:
  0.0 825.7 jit_solution(8945706175971660869)
XLA Ops:
  7.3 3.9 reshape_squeeze.7
  11.2 1.9 copy.23
  13.1 2.8 copy.26
  15.9 802.6 %while.18 = (s32[]{:T(128)}, bf16[4,2048]{1,0:T(4,128)(2,1)S(1)}, bf16[1,4,2048]{2,1,0:T(4,128)(2,1)S(1)}, pred[]{:T(512)}, bf16[1,4,2048]{2,1,0:T(4,128)(2,1)S(...) while((s32[]{:T(128)}, bf16[4,2048]{1,0:T(4,128)(2,1)S(1)}, ...), condition=%wide.region_7.8_spmd.clone, body=%wide.region_0.7_spmd.clone.sunk | while | flops 410595840 | bytes 96768936 | solution.py:100
  16.2 8.8 %collective-permute-start = (bf16[4,2048]{1,0:T(4,128)(2,1)S(1)}, bf16[4,2048]{1,0:T(4,128)(2,1)S(1)}, u32[]{:S(2)}, u32[]{:S(2)}) collective-permute-start(bf16[4,2048]{1,0:T(4,128)(2,1)S(1)} %broadcast_select_fusion.2), channel_id=1, source_target_pairs={{256,0},{257,1},{258,2},{259,3},{260,4},{261,5},{262,6},{263,7},{2... | collective-permute-start | bytes 49160 | tf_op jit(solution)/shard_map/while/body/eval_jaxpr/ppermute | solution.py:16
  25.0 39.6 %all-gather.6 = bf16[1,1,128,2048]{3,1,0,2:T(2,128)(2,1)S(1)} all-gather(bf16[1,1,4,2048]{3,1,0,2:T(2,128)(2,1)S(1)} %get-tuple-element.542), channel_id=2, replica_groups=mesh['section'=2,'row'=8,'col'=32] {'col'}, dimensions={2}, use_global_device_ids=true | all-gather | bytes 540672 | tf_op jit(solution)/shard_map/while/body/eval_jaxpr/all_gather | solution.py:78
  64.6 0.9 copy.30
  65.5 1.0 gather_fusion
  66.5 4.4 fusion.43
  71.0 13.5 %scatter_fusion = f32[128,32,64]{0,2,1:T(8,128)S(1)} fusion(f32[128,32,64]{0,2,1:T(8,128)S(1)} %broadcast.250.clone, s32[128]{0:T(128)S(1)} %get-tuple-element.487, f32[128,128,64]{1,2,0:T(8,128)} %fusion.43), kind=kCustom, calls=%fused_computation.4.clone.clone.1 | custom fusion | flops 1048576 | bytes 12583424 | tf_op jit(solution)/shard_map/while/body/eval_jaxpr/scatter-add | solution.py:34
  84.5 0.9 convert_element_type.156
  85.4 36.1 %all-gather.7 = bf16[32,4,2048]{2,1,0:T(4,128)(2,1)S(1)} all-gather(bf16[1,4,2048]{2,1,0:T(4,128)(2,1)S(1)} %fusion.44), channel_id=1, replica_groups=mesh['section'=2,'row'=8,'col'=32] {'col'}, dimensions={0}, use_global_device_ids=true | all-gather | bytes 540672 | tf_op jit(solution)/shard_map/while/body/eval_jaxpr/all_gather | solution.py:79
  121.5 0.8 reshape.249
  122.4 1.1 copy.31
  123.5 1.0 gather_fusion.1
  124.5 4.2 fusion.45
  128.8 13.5 %scatter_fusion.1 = f32[128,32,64]{0,2,1:T(8,128)S(1)} fusion(f32[128,32,64]{0,2,1:T(8,128)S(1)} %broadcast.250.clone.1, s32[128]{0:T(128)S(1)} %get-tuple-element.488, f32[128,128,64]{1,2,0:T(8,128)} %fusion.45), kind=kCustom, calls=%fused_computation.3.clone.clone.1 | custom fusion | flops 1048576 | bytes 12583424 | tf_op jit(solution)/shard_map/while/body/eval_jaxpr/scatter-add | solution.py:34
  142.3 0.9 convert_element_type.157
  143.3 95.6 %all-reduce.9.cloned.1.call-done = (bf16[128,2048]{0,1:T(8,128)(2,1)}, bf16[128,2048]{0,1:T(8,128)(2,1)}) async-done(((bf16[128,2048]{0,1:T(8,128)(2,1)}, bf16[128,2048]{0,1:T(8,128)(2,1)}), (bf16[128,2048]{0,1:T(8,128)(2,1)}, bf16[128,2048]{0,1:T(8,128)(2,1)})) %all-reduce.9.cloned.1.call-update) | async-done | bytes 1048592 | tf_op jit(solution)/shard_map/while/body/eval_jaxpr/psum | solution.py:81
  238.8 1.7 fusion.46
  240.5 1.0 gather_fusion.2
  241.5 4.2 fusion.47
  245.8 13.5 %scatter_fusion.2 = f32[128,32,64]{0,2,1:T(8,128)S(1)} fusion(f32[128,32,64]{0,2,1:T(8,128)S(1)} %broadcast.250, s32[128]{0:T(128)S(1)} %get-tuple-element.486, f32[128,128,64]{1,2,0:T(8,128)} %fusion.47), kind=kCustom, calls=%fused_computation.5.clone.clone.1 | custom fusion | flops 1048576 | bytes 12583424 | tf_op jit(solution)/shard_map/while/body/eval_jaxpr/scatter-add | solution.py:34
  259.4 1.0 copy.32
  260.5 1.3 dynamic-slice.5
  262.4 156.1 %all-reduce.11.cloned.1.call-done = bf16[128,2048]{1,0:T(8,128)(2,1)} async-done(((bf16[128,2048]{1,0:T(8,128)(2,1)}), bf16[128,2048]{1,0:T(8,128)(2,1)}) %all-reduce.11.cloned.1.call-update) | async-done | bytes 524304 | tf_op jit(solution)/shard_map/while
  419.3 7.0 collective-permute-start
  426.4 37.6 %all-gather.6 = bf16[1,1,128,2048]{3,1,0,2:T(2,128)(2,1)S(1)} all-gather(bf16[1,1,4,2048]{3,1,0,2:T(2,128)(2,1)S(1)} %get-tuple-element.542), channel_id=2, replica_groups=mesh['section'=2,'row'=8,'col'=32] {'col'}, dimensions={2}, use_global_device_ids=true | all-gather | bytes 540672 | tf_op jit(solution)/shard_map/while/body/eval_jaxpr/all_gather | solution.py:78
  464.0 0.9 copy.30
  464.9 1.0 gather_fusion
  465.9 4.4 fusion.43
  470.4 13.5 %scatter_fusion = f32[128,32,64]{0,2,1:T(8,128)S(1)} fusion(f32[128,32,64]{0,2,1:T(8,128)S(1)} %broadcast.250.clone, s32[128]{0:T(128)S(1)} %get-tuple-element.487, f32[128,128,64]{1,2,0:T(8,128)} %fusion.43), kind=kCustom, calls=%fused_computation.4.clone.clone.1 | custom fusion | flops 1048576 | bytes 12583424 | tf_op jit(solution)/shard_map/while/body/eval_jaxpr/scatter-add | solution.py:34
  483.9 0.9 convert_element_type.156
  484.8 34.8 %all-gather.7 = bf16[32,4,2048]{2,1,0:T(4,128)(2,1)S(1)} all-gather(bf16[1,4,2048]{2,1,0:T(4,128)(2,1)S(1)} %fusion.44), channel_id=1, replica_groups=mesh['section'=2,'row'=8,'col'=32] {'col'}, dimensions={0}, use_global_device_ids=true | all-gather | bytes 540672 | tf_op jit(solution)/shard_map/while/body/eval_jaxpr/all_gather | solution.py:79
  519.7 0.8 reshape.249
  520.5 1.1 copy.31
  521.6 1.0 gather_fusion.1
  522.6 4.2 fusion.45
  526.9 13.5 %scatter_fusion.1 = f32[128,32,64]{0,2,1:T(8,128)S(1)} fusion(f32[128,32,64]{0,2,1:T(8,128)S(1)} %broadcast.250.clone.1, s32[128]{0:T(128)S(1)} %get-tuple-element.488, f32[128,128,64]{1,2,0:T(8,128)} %fusion.45), kind=kCustom, calls=%fused_computation.3.clone.clone.1 | custom fusion | flops 1048576 | bytes 12583424 | tf_op jit(solution)/shard_map/while/body/eval_jaxpr/scatter-add | solution.py:34
  540.4 0.9 convert_element_type.157
  541.4 96.7 %all-reduce.9.cloned.1.call-done = (bf16[128,2048]{0,1:T(8,128)(2,1)}, bf16[128,2048]{0,1:T(8,128)(2,1)}) async-done(((bf16[128,2048]{0,1:T(8,128)(2,1)}, bf16[128,2048]{0,1:T(8,128)(2,1)}), (bf16[128,2048]{0,1:T(8,128)(2,1)}, bf16[128,2048]{0,1:T(8,128)(2,1)})) %all-reduce.9.cloned.1.call-update) | async-done | bytes 1048592 | tf_op jit(solution)/shard_map/while/body/eval_jaxpr/psum | solution.py:81
  638.1 1.7 fusion.46
  639.8 1.0 gather_fusion.2
  640.8 4.2 fusion.47
  645.1 13.5 %scatter_fusion.2 = f32[128,32,64]{0,2,1:T(8,128)S(1)} fusion(f32[128,32,64]{0,2,1:T(8,128)S(1)} %broadcast.250, s32[128]{0:T(128)S(1)} %get-tuple-element.486, f32[128,128,64]{1,2,0:T(8,128)} %fusion.47), kind=kCustom, calls=%fused_computation.5.clone.clone.1 | custom fusion | flops 1048576 | bytes 12583424 | tf_op jit(solution)/shard_map/while/body/eval_jaxpr/scatter-add | solution.py:34
  658.7 1.0 copy.32
  659.7 1.3 dynamic-slice.5
  661.7 156.1 %all-reduce.11.cloned.1.call-done = bf16[128,2048]{1,0:T(8,128)(2,1)} async-done(((bf16[128,2048]{1,0:T(8,128)(2,1)}), bf16[128,2048]{1,0:T(8,128)(2,1)}) %all-reduce.11.cloned.1.call-update) | async-done | bytes 524304 | tf_op jit(solution)/shard_map/while
  (44 shorter events, 4.1 us)
Async XLA Ops:
  13.1 2.8 copy-start.2
  13.1 2.8 copy-start
  16.1 222.7 %all-reduce.9.cloned.1.call-start = ((), (), s32[]{:S(2)}) async-start(), calls=%async_computation | async-start | bytes 2097152 | tf_op jit(solution)/shard_map/while/body/eval_jaxpr/psum | solution.py:81
  16.2 69.2 %collective-permute-start = (bf16[4,2048]{1,0:T(4,128)(2,1)S(1)}, bf16[4,2048]{1,0:T(4,128)(2,1)S(1)}, u32[]{:S(2)}, u32[]{:S(2)}) collective-permute-start(bf16[4,2048]{1,0:T(4,128)(2,1)S(1)} %broadcast_select_fusion.2), channel_id=1, source_target_pairs={{256,0},{257,1},{258,2},{259,3},{260,4},{261,5},{262,6},{263,7},{2... | collective-permute-start | bytes 49160 | tf_op jit(solution)/shard_map/while/body/eval_jaxpr/ppermute | solution.py:16
  143.2 275.3 %all-reduce.11.cloned.1.call-start = ((), (), s32[]{:S(2)}) async-start(), calls=%async_computation.1 | async-start | bytes 1048576 | tf_op jit(solution)/shard_map/while
  419.3 218.8 %all-reduce.9.cloned.1.call-start = ((), (), s32[]{:S(2)}) async-start(), calls=%async_computation | async-start | bytes 2097152 | tf_op jit(solution)/shard_map/while/body/eval_jaxpr/psum | solution.py:81
  419.3 65.5 %collective-permute-start = (bf16[4,2048]{1,0:T(4,128)(2,1)S(1)}, bf16[4,2048]{1,0:T(4,128)(2,1)S(1)}, u32[]{:S(2)}, u32[]{:S(2)}) collective-permute-start(bf16[4,2048]{1,0:T(4,128)(2,1)S(1)} %broadcast_select_fusion.2), channel_id=1, source_target_pairs={{256,0},{257,1},{258,2},{259,3},{260,4},{261,5},{262,6},{263,7},{2... | collective-permute-start | bytes 49160 | tf_op jit(solution)/shard_map/while/body/eval_jaxpr/ppermute | solution.py:16
  541.3 276.4 %all-reduce.11.cloned.1.call-start = ((), (), s32[]{:S(2)}) async-start(), calls=%async_computation.1 | async-start | bytes 1048576 | tf_op jit(solution)/shard_map/while
  818.5 0.6 copy-start.1
Sparse Core Ops, SparseCore 0:
  143.3 95.4 all-reduce.8
  260.6 157.8 all-reduce.10
  541.4 96.6 all-reduce.8
  659.9 157.8 all-reduce.10
where the time goes:
time: 832 us; the launch traced here: 826 us
  waiting for transfers between devices  505 us (61%)
  blocking collectives  148 us (18%)
  other arithmetic  89.9 us (11%)
  local copies, waits for them, and re-layouts  26.5 us (3%)
  matrix products  25.6 us (3%)
  starting transfers between devices  16 us (2%)
  between operations  13.1 us (2%)
    while x6, waiting for transfers between devices  312 us
    psum x2, waiting for transfers between devices, advance(): lax.psum(hidden_part.astype(jnp.bfloat16), 'row').astype(jnp.float32)  192 us
    scatter-add x6, other arithmetic, tile_product(): summed = jnp.zeros((operand.shape[0], blocks_out, block_size), jnp.float3...  80.9 us
    all_gather x2, blocking collectives, advance(): lax.all_gather(stash_now, 'col', axis=0, tiled=True)  77.2 us
    all_gather x2, blocking collectives, advance(): gate_part = gate_of(lax.all_gather(upstream, 'col', axis=0, tiled=True))  71 us
    dot_general x6, matrix products, tile_product(): jnp.einsum(pattern, picked, values, preferred_element_type=jnp.float32)  25.6 us
  transfers between devices with their start and end apart: 6, of which 4 were waited for; matrix products, arithmetic and copies ran while one was open for 5% of the time, Pallas kernels for 0%

commit v1 on v0

v1 whole, which is shorter than its diff:
```python
import functools

import jax
import jax.numpy as jnp
from jax import lax
from jax.experimental import pallas as pl
from jax.experimental.pallas import tpu as pltpu
from jax.sharding import PartitionSpec as P

LANES = 128
BLK = 64
PER_COL = 2
SWAP = [(0, 1), (1, 0)]
UNROLL = 16
SMEM = pl.BlockSpec(memory_space=pltpu.SMEM)
VMEM = pl.BlockSpec(memory_space=pltpu.VMEM)


def left_half(rows):
    return lax.broadcasted_iota(jnp.int32, (rows, LANES), 1) < BLK


def forward_kernel(count, *refs):
    index, x_ref, values = refs[:count], refs[count], refs[count + 1 : 2 * count + 1]
    out_ref, rows, blocks, even, odd = refs[2 * count + 1 :]
    tokens = blocks.shape[1]
    subs = blocks.shape[0] // 2
    left = left_half(tokens)
    for i in range(count):
        rows[...] = x_ref[:, i].reshape(rows.shape).astype(jnp.float32)
        for w in range(subs):
            both = rows[pl.ds(w, tokens, stride=subs), :]
            blocks[2 * w] = both.astype(jnp.bfloat16)
            blocks[2 * w + 1] = pltpu.roll(both, BLK, 1).astype(jnp.bfloat16)
        even[...] = jnp.zeros_like(even)
        odd[...] = jnp.zeros_like(odd)

        def multiply(pair, carry):
            first, second = 2 * pair, 2 * pair + 1
            picked = [blocks[index[i][0, n]][:, :BLK] for n in (first, second)]
            product = jnp.dot(
                jnp.concatenate(picked), values[i][pair], preferred_element_type=jnp.float32
            )
            even[index[i][1, first]] += product[:tokens]
            odd[index[i][1, second]] += product[tokens:]
            return carry

        lax.fori_loop(0, values[i].shape[0], multiply, 0, unroll=UNROLL)
        chunk = out_ref.shape[3] // LANES
        for j in range(even.shape[0] // 2):
            a, b = 2 * j, 2 * j + 1
            straight = jnp.where(left, even[a], odd[b])
            crossed = jnp.where(left, even[b], odd[a])
            total = straight + pltpu.roll(crossed, BLK, 1)
            lanes = slice((j % chunk) * LANES, (j % chunk + 1) * LANES)
            out_ref[j // chunk, i, :, lanes] = total.astype(jnp.bfloat16)


def forward(x, weights, n_row, ff_tile):
    count = len(weights)
    n_col, _, per, _ = x.shape
    tokens = n_col * PER_COL
    subs = per // PER_COL
    blocks_out = ff_tile // BLK
    return pl.pallas_call(
        functools.partial(forward_kernel, count),
        out_shape=jax.ShapeDtypeStruct((n_row, count, tokens, ff_tile // n_row), jnp.bfloat16),
        in_specs=[SMEM] * count + [VMEM] * (1 + count),
        out_specs=VMEM,
        scratch_shapes=[
            pltpu.VMEM((n_col * per, LANES), jnp.float32),
            pltpu.VMEM((2 * subs, tokens, LANES), jnp.bfloat16),
            pltpu.VMEM((blocks_out, tokens, LANES), jnp.float32),
            pltpu.VMEM((blocks_out, tokens, LANES), jnp.float32),
        ],
        compiler_params=pltpu.CompilerParams(vmem_limit_bytes=16 * 2**20),
        cost_estimate=pl.CostEstimate(
            flops=count * 10**9, bytes_accessed=count * 2 * 2**20, transcendentals=0
        ),
    )(*[w[0] for w in weights], x, *[w[1] for w in weights])


def backward_kernel(index, hidden_ref, values, out_ref, rows, lower, upper, total):
    tokens = lower.shape[1]
    subs = total.shape[0] // 2
    chunk = hidden_ref.shape[2] // LANES
    left = left_half(tokens)
    for j in range(lower.shape[0] // 2):
        lanes = slice((j % chunk) * LANES, (j % chunk + 1) * LANES)
        both = hidden_ref[j // chunk, :, lanes].astype(jnp.float32)
        turned = pltpu.roll(both, BLK, 1)
        lower[2 * j] = jnp.where(left, both, 0.0).astype(jnp.bfloat16)
        upper[2 * j + 1] = jnp.where(left, 0.0, both).astype(jnp.bfloat16)
        lower[2 * j + 1] = jnp.where(left, turned, 0.0).astype(jnp.bfloat16)
        upper[2 * j] = jnp.where(left, 0.0, turned).astype(jnp.bfloat16)
    total[...] = jnp.zeros_like(total)

    def multiply(pair, carry):
        first, second = 2 * pair, 2 * pair + 1
        picked = jnp.concatenate([lower[index[1, first]], upper[index[1, second]]])
        product = lax.dot_general(
            picked, values[pair], (((1,), (1,)), ((), ())), preferred_element_type=jnp.float32
        )
        total[index[0, first]] += product[:tokens]
        total[index[0, second]] += product[tokens:]
        return carry

    lax.fori_loop(0, values.shape[0], multiply, 0, unroll=UNROLL)
    for w in range(subs):
        both = jnp.concatenate([total[2 * w], total[2 * w + 1]], axis=1)
        rows[pl.ds(w, tokens, stride=subs), :] = both
    out_ref[...] = rows[...].astype(jnp.bfloat16).reshape(out_ref.shape)


def backward(hidden_grad, weights, n_col, width):
    tokens = hidden_grad.shape[1]
    ff_tile = hidden_grad.shape[0] * hidden_grad.shape[2]
    per = PER_COL * width // LANES
    return pl.pallas_call(
        backward_kernel,
        out_shape=jax.ShapeDtypeStruct((n_col, per, LANES), jnp.bfloat16),
        in_specs=[SMEM, VMEM, VMEM],
        out_specs=VMEM,
        scratch_shapes=[
            pltpu.VMEM((n_col * per, LANES), jnp.float32),
            pltpu.VMEM((ff_tile // BLK, tokens, LANES), jnp.bfloat16),
            pltpu.VMEM((ff_tile // BLK, tokens, LANES), jnp.bfloat16),
            pltpu.VMEM((width // BLK, tokens, BLK), jnp.float32),
        ],
        compiler_params=pltpu.CompilerParams(vmem_limit_bytes=16 * 2**20),
        cost_estimate=pl.CostEstimate(flops=10**9, bytes_accessed=2 * 2**20, transcendentals=0),
    )(weights[0], hidden_grad, weights[1])


def gelu_slope(hidden):
    return (
        0.5 * (1.0 + lax.erf(hidden * 0.7071067811865476))
        + hidden * jnp.exp(-0.5 * hidden * hidden) * 0.3989422804014327
    )


def local(n_row, n_col, ff, x_stash, out_grad, in_values, in_index, out_values, out_index):
    section = lax.axis_index("section")
    is_last = section == 1
    width = x_stash.shape[3]
    ff_tile = ff // n_col
    per = PER_COL * width // LANES

    def exchange(v, axis):
        return lax.all_to_all(v, axis, 0, 0)

    def gather(v, axis):
        return exchange(jnp.broadcast_to(v[None], (lax.axis_size(axis),) + v.shape), axis)

    def products(x, weights):
        return forward(x, weights, n_row, ff_tile)

    def row_sums(parts):
        return jnp.sum(exchange(parts, "row").astype(jnp.float32), axis=0)

    def finish(hidden, gate_grad, g, w_in):
        hidden_grad = (gate_grad * gelu_slope(hidden)).astype(jnp.bfloat16)
        part = exchange(backward(gather(hidden_grad, "row"), w_in, n_col, width), "col")
        return (g.astype(jnp.float32) + jnp.sum(part.astype(jnp.float32), axis=0)).astype(jnp.bfloat16)

    def swap(v):
        return lax.ppermute(v, "section", SWAP)

    def shard_of(v, start):
        return lax.dynamic_slice_in_dim(v, start, PER_COL, 0).reshape(per, LANES)

    in_own, out_own = in_values[0, 0, 0], out_values[0, 0, 0]
    in_at, out_at = in_index[0, 0, 0], out_index[0, 0, 0]
    places = jnp.concatenate([in_at, out_at]).astype(jnp.bfloat16)
    places = jnp.pad(places, ((0, 12), (0, 0)))
    mine = shard_of(x_stash[0, 0], PER_COL * section)
    came = swap(jnp.concatenate([shard_of(x_stash[0, 0], PER_COL - PER_COL * section), places]))
    other = came[:per]
    at_oth = came[per : per + 4].astype(jnp.int32)
    g1 = shard_of(out_grad[0], PER_COL * section)
    shards = jnp.stack([jnp.where(is_last, mine, other), g1, jnp.where(is_last, other, mine)])
    shards, in_sent, out_sent = lax.optimization_barrier((shards, in_own, out_own))
    first = gather(shards, "col")
    in_oth, out_oth = swap(in_sent), swap(out_sent)
    own = ((in_at, in_own), (out_at, out_own))
    oth = ((at_oth[:2], in_oth), (at_oth[2:], out_oth))

    def later_core(own, oth, first, g1):
        w1, w0 = own, oth
        sums = row_sums(products(first[:, :2], w1))
        g0 = finish(sums[0], sums[1], g1, w1[0])
        hidden0 = products(first[:, 2:], w0[:1])
        gate0 = products(gather(g0[None], "col"), w0[1:])
        sums = row_sums(jnp.concatenate([hidden0, gate0], axis=1))
        return g0, finish(sums[0], sums[1], g0, w0[0])

    def earlier_core(own, oth, first, g1):
        w1, w0 = oth, own
        sums = row_sums(products(first, w1 + w0[:1]))
        g0 = finish(sums[0], sums[1], g1, w1[0])
        gate0 = row_sums(products(gather(g0[None], "col"), w0[1:]))[0]
        return g0, finish(sums[2], gate0, g0, w0[0])

    g0, last = lax.cond(is_last, later_core, earlier_core, own, oth, first, g1)

    kept = jnp.where(is_last, g0, last)
    came = swap(jnp.where(is_last, last, g0))
    result = jnp.where(is_last, jnp.stack([came, kept]), jnp.stack([kept, came]))
    return result.reshape(1, 1, 2 * PER_COL, width)


def solution(mesh):
    in_specs = (
        P("section", None, "col", "row"),
        P(None, "col", "row"),
        P("section", "row", "col", None, None, None),
        P("section", "row", "col", None, None),
        P("section", "row", "col", None, None, None),
        P("section", "row", "col", None, None),
    )
    out_specs = P("section", None, "col", "row")
    body = functools.partial(local, mesh.shape["row"], mesh.shape["col"], 65536)
    return jax.shard_map(body, mesh=mesh, in_specs=in_specs, out_specs=out_specs, check_vma=False)
```

time: 832 us -> 175 us (0.21)
  waiting for transfers between devices: 505 us -> 22.4 us
  other arithmetic: 89.9 us -> 3.12 us
  blocking collectives: 148 us -> 91.4 us
  matrix products: 25.6 us -> 0 us
  local copies, waits for them, and re-layouts: 26.5 us -> 4.12 us
  starting transfers between devices: 16 us -> 37.2 us
  Pallas kernels: 0 us -> 15.1 us
  between operations: 13.1 us -> 0.15 us
    while x6 -> x0, waiting for transfers between devices: 312 us -> none
    psum x2 -> x0, waiting for transfers between devices: 192 us -> none  [advance(): lax.psum(hidden_part.astype(jnp.bfloat16), 'row').astype(jnp.float32)]
    all_gather x4 -> x0, blocking collectives: 148 us -> none  [the longest x2 77.2 us: advance(): lax.all_gather(stash_now, 'col', axis=0, tiled=True)]
    all_to_all x0 -> x6, blocking collectives: none -> 91.4 us  [exchange(): return lax.all_to_all(v, axis, 0, 0)]
    scatter-add x6 -> x0, other arithmetic: 80.9 us -> none  [tile_product(): summed = jnp.zeros((operand.shape[0], blocks_out, block_size), jnp.float3...]
    dot_general x6 -> x0, matrix products: 25.6 us -> none  [tile_product(): jnp.einsum(pattern, picked, values, preferred_element_type=jnp.float32)]
    all_to_all x0 -> x2, waiting for transfers between devices: none -> 18.1 us  [exchange(): return lax.all_to_all(v, axis, 0, 0)]
    pallas_call x0 -> x5, Pallas kernels: none -> 15.1 us  [the longest x3 9.58 us: forward(): pl.pallas_call(functools.partial(forward_kernel, count), out_shape=jax.Sh...]
  transfers between devices with their start and end apart: 6 -> 6, of which waited for: 4 -> 6; matrix products, arithmetic and copies ran while one was open for 5% -> 0% of each run, Pallas kernels for 0% -> 2%
where the time goes in v1:
time: 175 us; the launch traced here: 174 us
  blocking collectives  91.4 us (52%)
  starting transfers between devices  37.2 us (21%)
  waiting for transfers between devices  22.4 us (13%)
  Pallas kernels  15.1 us (9%)
  local copies, waits for them, and re-layouts  4.12 us (2%)
  other arithmetic  3.12 us (2%)
    all_to_all x6, blocking collectives, exchange(): return lax.all_to_all(v, axis, 0, 0)  91.4 us
    ppermute x4, starting transfers between devices, swap(): return lax.ppermute(v, 'section', SWAP)  25.1 us
    all_to_all x2, waiting for transfers between devices, exchange(): return lax.all_to_all(v, axis, 0, 0)  18.1 us
    all_to_all x2, starting transfers between devices, exchange(): return lax.all_to_all(v, axis, 0, 0)  12.1 us
    pallas_call x3, Pallas kernels, forward(): pl.pallas_call(functools.partial(forward_kernel, count), out_shape=jax.Sh...  9.58 us
    pallas_call x2, Pallas kernels, backward(): pl.pallas_call(backward_kernel, out_shape=jax.ShapeDtypeStruct((n_col, pe...  5.54 us
    ppermute x4, waiting for transfers between devices, swap(): return lax.ppermute(v, 'section', SWAP)  4.27 us
  transfers between devices with their start and end apart: 6, of which 6 were waited for; matrix products, arithmetic and copies ran while one was open for 0% of the time, Pallas kernels for 2%

profile of v1, /device:TPU:1, one launch (start us, length us, event | category | flops | bytes accessed | tf_op | source)
XLA Modules:
  0.0 173.6 jit_solution(758365509465103474)
XLA Ops:
  0.0 0.0 copy-start
  0.0 0.8 constant_dynamic-slice_fusion
  0.8 0.7 bitcast_convert_fusion
  1.6 8.8 %collective-permute-start = (bf16[48,128]{1,0:T(8,128)(2,1)S(1)}, bf16[48,128]{1,0:T(8,128)(2,1)S(1)}, u32[]{:S(2)}, u32[]{:S(2)}) collective-permute-start(bf16[48,128]{1,0:T(8,128)(2,1)S(1)} %pad_maximum_fusion.2), channel_id=1, source_target_pairs={{0,256},{256,0},{1,257},{257,1},{2,258},{258,2},{3,259},{259,3},{4... | collective-permute-start | bytes 36872 | tf_op jit(solution)/shard_map/ppermute | solution.py:167
  10.4 0.0 copy-done
  10.4 0.7 collective-permute-done
  11.2 0.0 copy-start.3
  11.2 0.0 copy-start.4
  11.2 0.0 copy-start.1
  11.2 0.0 copy-start.2
  11.2 1.0 broadcast_in_dim.34
  12.2 7.5 %all-to-all-start.14 = ((bf16[32,3,32,128]{3,2,1,0:T(8,128)(2,1)}), bf16[32,3,32,128]{3,2,1,0:T(8,128)(2,1)S(1)}, u32[]{:S(2)}, u32[]{:S(2)}) async-start(bf16[32,3,32,128]{3,2,1,0:T(8,128)(2,1)} %broadcast_in_dim.34), calls=%async_computation.14 | async-start | bytes 1572864 | tf_op jit(solution)/shard_map/all_to_all | solution.py:150
  19.8 0.0 copy-done.3
  19.8 2.5 %collective-permute-start.1 = (bf16[64,64,128]{2,1,0:T(8,128)(2,1)S(1)}, bf16[64,64,128]{2,1,0:T(8,128)(2,1)}, u32[]{:S(2)}, u32[]{:S(2)}) collective-permute-start(bf16[64,64,128]{2,1,0:T(8,128)(2,1)S(1)} %bitcast.30), channel_id=1, source_target_pairs={{0,256},{256,0},{1,257},{257,1},{2,258},{258,2},{3,259},{259,3},{4... | collective-permute-start | bytes 3145736 | tf_op jit(solution)/shard_map/ppermute | solution.py:167
  22.3 0.0 copy-done.4
  22.3 1.9 %collective-permute-start.2 = (bf16[64,64,128]{2,1,0:T(8,128)(2,1)S(1)}, bf16[64,64,128]{2,1,0:T(8,128)(2,1)}, u32[]{:S(2)}, u32[]{:S(2)}) collective-permute-start(bf16[64,64,128]{2,1,0:T(8,128)(2,1)S(1)} %bitcast.33), channel_id=1, source_target_pairs={{0,256},{256,0},{1,257},{257,1},{2,258},{258,2},{3,259},{259,3},{4... | collective-permute-start | bytes 3145736 | tf_op jit(solution)/shard_map/ppermute | solution.py:167
  24.3 0.4 collective-permute-done.1
  24.7 2.3 %collective-permute-done.2 = bf16[64,64,128]{2,1,0:T(8,128)(2,1)} collective-permute-done((bf16[64,64,128]{2,1,0:T(8,128)(2,1)S(1)}, bf16[64,64,128]{2,1,0:T(8,128)(2,1)}, u32[]{:S(2)}, u32[]{:S(2)}) %collective-permute-start.2) | collective-permute-done | bytes 1048608 | tf_op jit(solution)/shard_map/ppermute | solution.py:167
  27.0 11.6 %all-to-all-done.14 = bf16[32,3,32,128]{3,2,1,0:T(8,128)(2,1)S(1)} async-done(((bf16[32,3,32,128]{3,2,1,0:T(8,128)(2,1)}), bf16[32,3,32,128]{3,2,1,0:T(8,128)(2,1)S(1)}, u32[]{:S(2)}, u32[]{:S(2)}) %all-to-all-start.14) | async-done | bytes 786464 | tf_op jit(solution)/shard_map/all_to_all | solution.py:150
  38.6 0.0 copy-done.1
  38.6 0.0 copy-done.2
  38.6 121.0 %conditional.4 = (bf16[32,128]{1,0:T(8,128)(2,1)}, bf16[32,128]{1,0:T(8,128)(2,1)S(1)}) conditional(s32[]{:T(128)} %convert_element_type.79, (bf16[32,128]{1,0:T(8,128)(2,1)S(1)}, s32[2,128]{1,0:T(2,128)S(1)}, s32[2,128]{1,0:T(2,128)S(1)}, s32[2,128]{1,0:T(2,128)S(1)}, bf16[32,3,32,128]{3,2,1,0:T(8,128)(2,1)S(1)}, ...), branch_computations={%region_0.5_spmd, %region_5.10_spmd} | conditional | flops 6002113536 | bytes 23306288
  38.6 0.1 slice.29.refs_2_
  38.6 3.8 %branch_1_fun.5 = bf16[8,2,64,256]{3,2,1,0:T(8,128)(2,1)S(1)} custom-call(s32[2,128]{1,0:T(2,128)S(1)} %get-tuple-element.64.refs_0_.index, s32[2,128]{1,0:T(2,128)S(1)} %get-tuple-element.65.refs_1_, bf16[32,2,32,128]{3,2,1,0:T(8,128)(2,1)S(1)} %slice.29.refs_2_, bf16[64,64,128]{2,1,0:T(8,128)(2,1)S(1)} %get-tuple-element.67.refs_3_.values, ...), custom_call_target="tpu_custom_call" | custom-call | flops 2000000000 | bytes 4194304 | tf_op jit(solution)/shard_map/cond/branch_1_fun/pallas_call | solution.py:65
  42.5 18.9 %all_to_all.68 = bf16[8,2,64,256]{3,2,1,0:T(8,128)(2,1)S(1)} all-to-all(bf16[8,2,64,256]{3,2,1,0:T(8,128)(2,1)S(1)} %branch_1_fun.5), channel_id=1, replica_groups=mesh['section'=2,'row'=8,'col'=32] {'row'}, dimensions={0} | all-to-all | bytes 1048576 | tf_op jit(solution)/shard_map/cond/branch_1_fun/all_to_all | solution.py:150
  61.3 0.1 convert_reduce_fusion.5
  61.5 13.4 %all_to_all.69.hidden_ref = bf16[8,64,256]{2,1,0:T(8,128)(2,1)S(1)} all-to-all(bf16[8,64,256]{2,1,0:T(8,128)(2,1)S(1)} %broadcast_in_dim.29), channel_id=1, replica_groups=mesh['section'=2,'row'=8,'col'=32] {'row'}, dimensions={0} | all-to-all | bytes 524288 | tf_op jit(solution)/shard_map/cond/branch_1_fun/all_to_all | solution.py:150
  74.8 2.4 %branch_1_fun.6 = bf16[32,32,128]{2,1,0:T(8,128)(2,1)S(1)} custom-call(s32[2,128]{1,0:T(2,128)S(1)} %get-tuple-element.64.refs_0_.index, bf16[8,64,256]{2,1,0:T(8,128)(2,1)S(1)} %all_to_all.69.hidden_ref, bf16[64,64,128]{2,1,0:T(8,128)(2,1)S(1)} %get-tuple-element.67.refs_3_.values), custom_call_target="tpu_custom_call" | custom-call | flops 1000000000 | bytes 2097152 | tf_op jit(solution)/shard_map/cond/branch_1_fun/pallas_call | solution.py:119
  77.3 19.1 %all_to_all.70 = bf16[32,32,128]{2,1,0:T(8,128)(2,1)S(1)} all-to-all(bf16[32,32,128]{2,1,0:T(8,128)(2,1)S(1)} %branch_1_fun.6), channel_id=1, replica_groups=mesh['section'=2,'row'=8,'col'=32] {'col'}, dimensions={0} | all-to-all | bytes 524288 | tf_op jit(solution)/shard_map/cond/branch_1_fun/all_to_all | solution.py:150
  96.4 0.6 add_convert_fusion.3
  97.0 1.5 broadcast_in_dim.30
  98.5 4.6 %all-to-all-start.10 = ((bf16[32,1,32,128]{3,2,1,0:T(8,128)(2,1)}), bf16[32,1,32,128]{3,2,1,0:T(8,128)(2,1)S(1)}, u32[]{:S(2)}, u32[]{:S(2)}) async-start(bf16[32,1,32,128]{3,2,1,0:T(8,128)(2,1)} %broadcast_in_dim.30), calls=%async_computation.10 | async-start | bytes 524288 | tf_op jit(solution)/shard_map/cond/branch_1_fun/all_to_all | solution.py:150
  103.1 2.9 %branch_1_fun.7 = bf16[8,1,64,256]{3,2,1,0:T(8,128)(2,1)S(1)} custom-call(s32[2,128]{1,0:T(2,128)S(1)} %get-tuple-element.69.refs_0_.index, bf16[32,1,32,128]{3,2,1,0:T(8,128)(2,1)S(1)} %slice.32.refs_1_, bf16[64,64,128]{2,1,0:T(8,128)(2,1)} %get-tuple-element.70.refs_2_.values), custom_call_target="tpu_custom_call" | custom-call | flops 1000000000 | bytes 2097152 | tf_op jit(solution)/shard_map/cond/branch_1_fun/pallas_call | solution.py:65
  106.0 6.6 %all-to-all-done.10.refs_1_ = bf16[32,1,32,128]{3,2,1,0:T(8,128)(2,1)S(1)} async-done(((bf16[32,1,32,128]{3,2,1,0:T(8,128)(2,1)}), bf16[32,1,32,128]{3,2,1,0:T(8,128)(2,1)S(1)}, u32[]{:S(2)}, u32[]{:S(2)}) %all-to-all-start.10) | async-done | bytes 262176 | tf_op jit(solution)/shard_map/cond/branch_1_fun/all_to_all | solution.py:150
  112.5 2.9 %branch_1_fun.8 = bf16[8,1,64,256]{3,2,1,0:T(8,128)(2,1)S(1)} custom-call(s32[2,128]{1,0:T(2,128)S(1)} %get-tuple-element.71.refs_0_, bf16[32,1,32,128]{3,2,1,0:T(8,128)(2,1)S(1)} %all-to-all-done.10.refs_1_, bf16[64,64,128]{2,1,0:T(8,128)(2,1)} %get-tuple-element.72.refs_2_), custom_call_target="tpu_custom_call" | custom-call | flops 1000000000 | bytes 2097152 | tf_op jit(solution)/shard_map/cond/branch_1_fun/pallas_call | solution.py:65
  115.4 0.1 pad_maximum_fusion
  115.5 14.5 %all_to_all.71 = bf16[8,2,64,256]{3,2,1,0:T(8,128)(2,1)S(1)} all-to-all(bf16[8,2,64,256]{3,2,1,0:T(8,128)(2,1)S(1)} %pad_maximum_fusion), channel_id=1, replica_groups=mesh['section'=2,'row'=8,'col'=32] {'row'}, dimensions={0} | all-to-all | bytes 1048576 | tf_op jit(solution)/shard_map/cond/branch_1_fun/all_to_all | solution.py:150
  130.0 0.1 convert_reduce_fusion.4
  130.2 11.7 %all_to_all.72.hidden_ref = bf16[8,64,256]{2,1,0:T(8,128)(2,1)S(1)} all-to-all(bf16[8,64,256]{2,1,0:T(8,128)(2,1)S(1)} %broadcast_in_dim.32), channel_id=1, replica_groups=mesh['section'=2,'row'=8,'col'=32] {'row'}, dimensions={0} | all-to-all | bytes 524288 | tf_op jit(solution)/shard_map/cond/branch_1_fun/all_to_all | solution.py:150
  141.9 3.1 %branch_1_fun.9 = bf16[32,32,128]{2,1,0:T(8,128)(2,1)S(1)} custom-call(s32[2,128]{1,0:T(2,128)S(1)} %get-tuple-element.69.refs_0_.index, bf16[8,64,256]{2,1,0:T(8,128)(2,1)S(1)} %all_to_all.72.hidden_ref, bf16[64,64,128]{2,1,0:T(8,128)(2,1)} %get-tuple-element.70.refs_2_.values), custom_call_target="tpu_custom_call" | custom-call | flops 1000000000 | bytes 2097152 | tf_op jit(solution)/shard_map/cond/branch_1_fun/pallas_call | solution.py:119
  145.0 13.8 %all_to_all.73 = bf16[32,32,128]{2,1,0:T(8,128)(2,1)S(1)} all-to-all(bf16[32,32,128]{2,1,0:T(8,128)(2,1)S(1)} %branch_1_fun.9), channel_id=1, replica_groups=mesh['section'=2,'row'=8,'col'=32] {'col'}, dimensions={0} | all-to-all | bytes 524288 | tf_op jit(solution)/shard_map/cond/branch_1_fun/all_to_all | solution.py:150
  158.9 0.7 add_convert_fusion.2
  159.6 0.7 broadcast_select_fusion
  160.3 11.9 %collective-permute-start.3 = (bf16[32,128]{1,0:T(8,128)(2,1)S(1)}, bf16[32,128]{1,0:T(8,128)(2,1)S(1)}, u32[]{:S(2)}, u32[]{:S(2)}) collective-permute-start(bf16[32,128]{1,0:T(8,128)(2,1)S(1)} %get-tuple-element.89), channel_id=1, source_target_pairs={{0,256},{256,0},{1,257},{257,1},{2,258},{258,2},{3,259},{259,3},{4... | collective-permute-start | bytes 24584 | tf_op jit(solution)/shard_map/ppermute | solution.py:167
  172.2 0.8 collective-permute-done.3
  173.0 0.6 select_n.54
  (19 shorter events, 0.3 us)
Async XLA Ops:
  0.0 10.4 %copy-start = (bf16[1,4,2048]{2,1,0:T(4,128)(2,1)S(1)}, bf16[1,4,2048]{2,1,0:T(4,128)(2,1)}, u32[]{:S(2)}) copy-start(bf16[1,4,2048]{2,1,0:T(4,128)(2,1)} %param.9) | copy-start | bytes 49156
  1.6 9.6 %collective-permute-start = (bf16[48,128]{1,0:T(8,128)(2,1)S(1)}, bf16[48,128]{1,0:T(8,128)(2,1)S(1)}, u32[]{:S(2)}, u32[]{:S(2)}) collective-permute-start(bf16[48,128]{1,0:T(8,128)(2,1)S(1)} %pad_maximum_fusion.2), channel_id=1, source_target_pairs={{0,256},{256,0},{1,257},{257,1},{2,258},{258,2},{3,259},{259,3},{4... | collective-permute-start | bytes 36872 | tf_op jit(solution)/shard_map/ppermute | solution.py:167
  11.2 8.6 %copy-start.3 = (bf16[1,1,1,64,64,128]{5,4,3,2,1,0:T(8,128)(2,1)S(1)}, bf16[1,1,1,64,64,128]{5,4,3,2,1,0:T(8,128)(2,1)}, u32[]{:S(2)}) copy-start(bf16[1,1,1,64,64,128]{5,4,3,2,1,0:T(8,128)(2,1)} %param.10) | copy-start | bytes 3145732
  11.2 11.1 %copy-start.4 = (bf16[1,1,1,64,64,128]{5,4,3,2,1,0:T(8,128)(2,1)S(1)}, bf16[1,1,1,64,64,128]{5,4,3,2,1,0:T(8,128)(2,1)}, u32[]{:S(2)}) copy-start(bf16[1,1,1,64,64,128]{5,4,3,2,1,0:T(8,128)(2,1)} %param.12) | copy-start | bytes 3145732
  11.2 27.4 %copy-start.1 = (s32[1,1,1,2,128]{4,3,2,1,0:T(2,128)S(1)}, s32[1,1,1,2,128]{4,3,2,1,0:T(2,128)}, u32[]{:S(2)}) copy-start(s32[1,1,1,2,128]{4,3,2,1,0:T(2,128)} %param.13) | copy-start | bytes 3076
  11.2 27.4 %copy-start.2 = (s32[1,1,1,2,128]{4,3,2,1,0:T(2,128)S(1)}, s32[1,1,1,2,128]{4,3,2,1,0:T(2,128)}, u32[]{:S(2)}) copy-start(s32[1,1,1,2,128]{4,3,2,1,0:T(2,128)} %param.11) | copy-start | bytes 3076
  12.2 26.3 %all-to-all-start.14 = ((bf16[32,3,32,128]{3,2,1,0:T(8,128)(2,1)}), bf16[32,3,32,128]{3,2,1,0:T(8,128)(2,1)S(1)}, u32[]{:S(2)}, u32[]{:S(2)}) async-start(bf16[32,3,32,128]{3,2,1,0:T(8,128)(2,1)} %broadcast_in_dim.34), calls=%async_computation.14 | async-start | bytes 1572864 | tf_op jit(solution)/shard_map/all_to_all | solution.py:150
  19.8 4.9 %collective-permute-start.1 = (bf16[64,64,128]{2,1,0:T(8,128)(2,1)S(1)}, bf16[64,64,128]{2,1,0:T(8,128)(2,1)}, u32[]{:S(2)}, u32[]{:S(2)}) collective-permute-start(bf16[64,64,128]{2,1,0:T(8,128)(2,1)S(1)} %bitcast.30), channel_id=1, source_target_pairs={{0,256},{256,0},{1,257},{257,1},{2,258},{258,2},{3,259},{259,3},{4... | collective-permute-start | bytes 3145736 | tf_op jit(solution)/shard_map/ppermute | solution.py:167
  22.3 4.7 %collective-permute-start.2 = (bf16[64,64,128]{2,1,0:T(8,128)(2,1)S(1)}, bf16[64,64,128]{2,1,0:T(8,128)(2,1)}, u32[]{:S(2)}, u32[]{:S(2)}) collective-permute-start(bf16[64,64,128]{2,1,0:T(8,128)(2,1)S(1)} %bitcast.33), channel_id=1, source_target_pairs={{0,256},{256,0},{1,257},{257,1},{2,258},{258,2},{3,259},{259,3},{4... | collective-permute-start | bytes 3145736 | tf_op jit(solution)/shard_map/ppermute | solution.py:167
  98.5 14.0 %all-to-all-start.10 = ((bf16[32,1,32,128]{3,2,1,0:T(8,128)(2,1)}), bf16[32,1,32,128]{3,2,1,0:T(8,128)(2,1)S(1)}, u32[]{:S(2)}, u32[]{:S(2)}) async-start(bf16[32,1,32,128]{3,2,1,0:T(8,128)(2,1)} %broadcast_in_dim.30), calls=%async_computation.10 | async-start | bytes 524288 | tf_op jit(solution)/shard_map/cond/branch_1_fun/all_to_all | solution.py:150
  160.3 12.7 %collective-permute-start.3 = (bf16[32,128]{1,0:T(8,128)(2,1)S(1)}, bf16[32,128]{1,0:T(8,128)(2,1)S(1)}, u32[]{:S(2)}, u32[]{:S(2)}) collective-permute-start(bf16[32,128]{1,0:T(8,128)(2,1)S(1)} %get-tuple-element.89), channel_id=1, source_target_pairs={{0,256},{256,0},{1,257},{257,1},{2,258},{258,2},{3,259},{259,3},{4... | collective-permute-start | bytes 24584 | tf_op jit(solution)/shard_map/ppermute | solution.py:167

commit v2 on v1

--- a/solution.py
+++ b/solution.py
@@ -158,10 +158,13 @@
     def row_sums(parts):
         return jnp.sum(exchange(parts, "row").astype(jnp.float32), axis=0)
 
-    def finish(hidden, gate_grad, g, w_in):
-        hidden_grad = (gate_grad * gelu_slope(hidden)).astype(jnp.bfloat16)
+    def add(g, part):
+        return (g.astype(jnp.float32) + part).astype(jnp.bfloat16)
+
+    def col_sum(sums, w_in):
+        hidden_grad = (sums[1] * gelu_slope(sums[0])).astype(jnp.bfloat16)
         part = exchange(backward(gather(hidden_grad, "row"), w_in, n_col, width), "col")
-        return (g.astype(jnp.float32) + jnp.sum(part.astype(jnp.float32), axis=0)).astype(jnp.bfloat16)
+        return jnp.sum(part.astype(jnp.float32), axis=0)
 
     def swap(v):
         return lax.ppermute(v, "section", SWAP)
@@ -171,37 +174,33 @@
 
     in_own, out_own = in_values[0, 0, 0], out_values[0, 0, 0]
     in_at, out_at = in_index[0, 0, 0], out_index[0, 0, 0]
-    places = jnp.concatenate([in_at, out_at]).astype(jnp.bfloat16)
-    places = jnp.pad(places, ((0, 12), (0, 0)))
     mine = shard_of(x_stash[0, 0], PER_COL * section)
-    came = swap(jnp.concatenate([shard_of(x_stash[0, 0], PER_COL - PER_COL * section), places]))
-    other = came[:per]
-    at_oth = came[per : per + 4].astype(jnp.int32)
+    other = swap(shard_of(x_stash[0, 0], PER_COL - PER_COL * section))
     g1 = shard_of(out_grad[0], PER_COL * section)
-    shards = jnp.stack([jnp.where(is_last, mine, other), g1, jnp.where(is_last, other, mine)])
-    shards, in_sent, out_sent = lax.optimization_barrier((shards, in_own, out_own))
+    shards = jnp.stack([jnp.where(is_last, mine, other), g1])
+    x0 = jnp.where(is_last, other, mine)
+    shards, in_sent, out_sent, in_at, out_at = lax.optimization_barrier(
+        (shards, in_own, out_own, in_at, out_at)
+    )
     first = gather(shards, "col")
     in_oth, out_oth = swap(in_sent), swap(out_sent)
+    at_oth = swap(jnp.concatenate([in_at, out_at]))
     own = ((in_at, in_own), (out_at, out_own))
     oth = ((at_oth[:2], in_oth), (at_oth[2:], out_oth))
 
-    def later_core(own, oth, first, g1):
-        w1, w0 = own, oth
-        sums = row_sums(products(first[:, :2], w1))
-        g0 = finish(sums[0], sums[1], g1, w1[0])
-        hidden0 = products(first[:, 2:], w0[:1])
-        gate0 = products(gather(g0[None], "col"), w0[1:])
-        sums = row_sums(jnp.concatenate([hidden0, gate0], axis=1))
-        return g0, finish(sums[0], sums[1], g0, w0[0])
-
-    def earlier_core(own, oth, first, g1):
-        w1, w0 = oth, own
-        sums = row_sums(products(first, w1 + w0[:1]))
-        g0 = finish(sums[0], sums[1], g1, w1[0])
-        gate0 = row_sums(products(gather(g0[None], "col"), w0[1:]))[0]
-        return g0, finish(sums[2], gate0, g0, w0[0])
-
-    g0, last = lax.cond(is_last, later_core, earlier_core, own, oth, first, g1)
+    def layers(w1, w0, first, g1, x0):
+        g0 = add(g1, col_sum(row_sums(products(first, w1)), w1[0]))
+        second = gather(jnp.stack([x0, g0]), "col")
+        return g0, col_sum(row_sums(products(second, w0)), w0[0])
+
+    def later_core(own, oth, *rest):
+        return layers(own, oth, *rest)
+
+    def earlier_core(own, oth, *rest):
+        return layers(oth, own, *rest)
+
+    g0, part = lax.cond(is_last, later_core, earlier_core, own, oth, first, g1, x0)
+    last = add(g0, part)
 
     kept = jnp.where(is_last, g0, last)
     came = swap(jnp.where(is_last, last, g0))

time: 175 us -> 177 us (1.011)
  blocking collectives: 91.4 us -> 113 us
  waiting for transfers between devices: 22.4 us -> 13 us
  starting transfers between devices: 37.2 us -> 31.2 us
  other arithmetic: 3.12 us -> 0.36 us
    all_to_all x6 -> x7, blocking collectives: 91.4 us -> 113 us  [exchange(): return lax.all_to_all(v, axis, 0, 0)]
    all_to_all x2 -> x1, waiting for transfers between devices: 18.1 us -> 10.7 us  [exchange(): return lax.all_to_all(v, axis, 0, 0)]
    all_to_all x2 -> x1, starting transfers between devices: 12.1 us -> 7.64 us  [exchange(): return lax.all_to_all(v, axis, 0, 0)]
    ppermute x4 -> x5, waiting for transfers between devices: 4.27 us -> 2.33 us  [swap(): return lax.ppermute(v, 'section', SWAP)]
    unnamed x10 -> x14, local copies, waits for them, and re-layouts: 0.03 us -> 1.96 us
    ppermute x4 -> x5, starting transfers between devices: 25.1 us -> 23.6 us  [swap(): return lax.ppermute(v, 'section', SWAP)]
    pallas_call x3 -> x2, Pallas kernels: 9.58 us -> 9.03 us  [forward(): pl.pallas_call(functools.partial(forward_kernel, count), out_shape=jax.Sh...]
  transfers between devices with their start and end apart: 6 -> 6, of which waited for: 6 -> 4; matrix products, arithmetic and copies ran while one was open for 0% -> 1% of each run, Pallas kernels for 2% -> 0%
where the time goes in v2:
time: 177 us; the launch traced here: 176 us
  blocking collectives  113 us (64%)
  starting transfers between devices  31.2 us (18%)
  Pallas kernels  13.9 us (8%)
  waiting for transfers between devices  13 us (7%)
  local copies, waits for them, and re-layouts  3.76 us (2%)
    all_to_all x7, blocking collectives, exchange(): return lax.all_to_all(v, axis, 0, 0)  113 us
    ppermute x5, starting transfers between devices, swap(): return lax.ppermute(v, 'section', SWAP)  23.6 us
    all_to_all x1, waiting for transfers between devices, exchange(): return lax.all_to_all(v, axis, 0, 0)  10.7 us
    pallas_call x2, Pallas kernels, forward(): pl.pallas_call(functools.partial(forward_kernel, count), out_shape=jax.Sh...  9.03 us
    all_to_all x1, starting transfers between devices, exchange(): return lax.all_to_all(v, axis, 0, 0)  7.64 us
    pallas_call x2, Pallas kernels, backward(): pl.pallas_call(backward_kernel, out_shape=jax.ShapeDtypeStruct((n_col, pe...  4.88 us
  transfers between devices with their start and end apart: 6, of which 4 were waited for; matrix products, arithmetic and copies ran while one was open for 1% of the time, Pallas kernels for 0%

profile of v2, /device:TPU:1, one launch (start us, length us, event | category | flops | bytes accessed | tf_op | source)
XLA Modules:
  0.0 175.9 jit_solution(17268897495453428535)
XLA Ops:
  0.0 0.0 copy-start
  0.0 0.0 copy-start.3
  0.0 0.0 copy-start.6
  0.0 0.7 copy-done.3
  0.8 8.8 %collective-permute-start = (bf16[32,128]{1,0:T(8,128)(2,1)S(1)}, bf16[32,128]{1,0:T(8,128)(2,1)S(1)}, u32[]{:S(2)}, u32[]{:S(2)}) collective-permute-start(bf16[32,128]{1,0:T(8,128)(2,1)S(1)} %reshape.39), channel_id=1, source_target_pairs={{0,256},{256,0},{1,257},{257,1},{2,258},{258,2},{3,259},{259,3},{4... | collective-permute-start | bytes 24584 | tf_op jit(solution)/shard_map/ppermute | solution.py:170
  9.6 0.0 copy-done
  9.6 0.7 collective-permute-done
  10.4 2.3 %collective-permute-start.2 = (bf16[64,64,128]{2,1,0:T(8,128)(2,1)}, bf16[64,64,128]{2,1,0:T(8,128)(2,1)S(1)}, u32[]{:S(2)}, u32[]{:S(2)}) collective-permute-start(bf16[64,64,128]{2,1,0:T(8,128)(2,1)} %bitcast.32), channel_id=1, source_target_pairs={{0,256},{256,0},{1,257},{257,1},{2,258},{258,2},{3,259},{259,3},{4... | collective-permute-start | bytes 3145736 | tf_op jit(solution)/shard_map/ppermute | solution.py:170
  12.7 2.1 %collective-permute-start.3 = (bf16[64,64,128]{2,1,0:T(8,128)(2,1)}, bf16[64,64,128]{2,1,0:T(8,128)(2,1)}, u32[]{:S(2)}, u32[]{:S(2)}) collective-permute-start(bf16[64,64,128]{2,1,0:T(8,128)(2,1)} %bitcast.35), channel_id=1, source_target_pairs={{0,256},{256,0},{1,257},{257,1},{2,258},{258,2},{3,259},{259,3},{4... | collective-permute-start | bytes 3145736 | tf_op jit(solution)/shard_map/ppermute | solution.py:170
  14.7 0.9 broadcast_in_dim.34
  15.7 0.0 copy-start.4
  15.7 0.0 copy-start.5
  15.7 7.6 %all-to-all-start.14 = ((bf16[32,2,32,128]{3,2,1,0:T(8,128)(2,1)}), bf16[32,2,32,128]{3,2,1,0:T(8,128)(2,1)S(1)}, u32[]{:S(2)}, u32[]{:S(2)}) async-start(bf16[32,2,32,128]{3,2,1,0:T(8,128)(2,1)} %broadcast_in_dim.34), calls=%async_computation.14 | async-start | bytes 1048576 | tf_op jit(solution)/shard_map/all_to_all | solution.py:150
  23.3 0.0 copy-done.4
  23.3 0.0 copy-done.5
  23.4 2.5 %collective-permute-start.1 = (s32[4,128]{1,0:T(4,128)S(1)}, s32[4,128]{1,0:T(4,128)S(1)}, u32[]{:S(2)}, u32[]{:S(2)}) collective-permute-start(s32[4,128]{1,0:T(4,128)S(1)} %pad_add_fusion), channel_id=1, source_target_pairs={{0,256},{256,0},{1,257},{257,1},{2,258},{258,2},{3,259},{259,3},{4... | collective-permute-start | bytes 6152 | tf_op jit(solution)/shard_map/ppermute | solution.py:170
  25.9 0.8 collective-permute-done.1
  26.7 10.7 %all-to-all-done.14 = bf16[32,2,32,128]{3,2,1,0:T(8,128)(2,1)S(1)} async-done(((bf16[32,2,32,128]{3,2,1,0:T(8,128)(2,1)}), bf16[32,2,32,128]{3,2,1,0:T(8,128)(2,1)S(1)}, u32[]{:S(2)}, u32[]{:S(2)}) %all-to-all-start.14) | async-done | bytes 524320 | tf_op jit(solution)/shard_map/all_to_all | solution.py:150
  37.4 0.0 collective-permute-done.2
  37.4 0.0 collective-permute-done.3
  37.4 0.0 copy-done.6
  37.4 129.1 %conditional.4 = (f32[32,128]{1,0:T(8,128)S(1)}, bf16[32,128]{1,0:T(8,128)(2,1)S(1)}) conditional(s32[]{:T(128)} %convert_element_type.67, (bf16[32,128]{1,0:T(8,128)(2,1)S(1)}, bf16[32,128]{1,0:T(8,128)(2,1)S(1)}, s32[2,128]{1,0:T(2,128)S(1)}, s32[2,128]{1,0:T(2,128)S(1)}, bf16[32,2,32,128]{3,2,1,0:T(8,128)(2,1)S(1)}, ...), branch_computations={%region_0.5_spmd, %region_5.10_spmd} | conditional | flops 6001847296 | bytes 25411628
  37.4 4.5 %branch_1_fun.4 = bf16[8,2,64,256]{3,2,1,0:T(8,128)(2,1)S(1)} custom-call(s32[2,128]{1,0:T(2,128)S(1)} %get-tuple-element.72.refs_0_.index, s32[2,128]{1,0:T(2,128)S(1)} %get-tuple-element.73.refs_1_, bf16[32,2,32,128]{3,2,1,0:T(8,128)(2,1)S(1)} %get-tuple-element.74.refs_2_, bf16[64,64,128]{2,1,0:T(8,128)(2,1)S(1)} %get-tuple-element.75.refs_3_.values, ...), custom_call_target="tpu_custom_call" | custom-call | flops 2000000000 | bytes 4194304 | tf_op jit(solution)/shard_map/cond/branch_1_fun/pallas_call | solution.py:65
  42.0 19.6 %all_to_all.68 = bf16[8,2,64,256]{3,2,1,0:T(8,128)(2,1)S(1)} all-to-all(bf16[8,2,64,256]{3,2,1,0:T(8,128)(2,1)S(1)} %branch_1_fun.4), channel_id=1, replica_groups=mesh['section'=2,'row'=8,'col'=32] {'row'}, dimensions={0} | all-to-all | bytes 1048576 | tf_op jit(solution)/shard_map/cond/branch_1_fun/all_to_all | solution.py:150
  61.6 0.1 convert_reduce_fusion.5
  61.7 13.0 %all_to_all.69.hidden_ref = bf16[8,64,256]{2,1,0:T(8,128)(2,1)S(1)} all-to-all(bf16[8,64,256]{2,1,0:T(8,128)(2,1)S(1)} %broadcast_in_dim.29), channel_id=1, replica_groups=mesh['section'=2,'row'=8,'col'=32] {'row'}, dimensions={0} | all-to-all | bytes 524288 | tf_op jit(solution)/shard_map/cond/branch_1_fun/all_to_all | solution.py:150
  74.7 2.4 %branch_1_fun.5 = bf16[32,32,128]{2,1,0:T(8,128)(2,1)S(1)} custom-call(s32[2,128]{1,0:T(2,128)S(1)} %get-tuple-element.72.refs_0_.index, bf16[8,64,256]{2,1,0:T(8,128)(2,1)S(1)} %all_to_all.69.hidden_ref, bf16[64,64,128]{2,1,0:T(8,128)(2,1)S(1)} %get-tuple-element.75.refs_3_.values), custom_call_target="tpu_custom_call" | custom-call | flops 1000000000 | bytes 2097152 | tf_op jit(solution)/shard_map/cond/branch_1_fun/pallas_call | solution.py:119
  77.2 19.9 %all_to_all.70 = bf16[32,32,128]{2,1,0:T(8,128)(2,1)S(1)} all-to-all(bf16[32,32,128]{2,1,0:T(8,128)(2,1)S(1)} %branch_1_fun.5), channel_id=1, replica_groups=mesh['section'=2,'row'=8,'col'=32] {'col'}, dimensions={0} | all-to-all | bytes 524288 | tf_op jit(solution)/shard_map/cond/branch_1_fun/all_to_all | solution.py:150
  97.1 0.0 copy-start.1
  97.2 0.6 copy-done.1
  97.7 0.1 broadcast_in_dim.30
  97.8 15.6 %all_to_all.71.refs_2_ = bf16[32,2,32,128]{3,2,1,0:T(8,128)(2,1)S(1)} all-to-all(bf16[32,2,32,128]{3,2,1,0:T(8,128)(2,1)S(1)} %broadcast_in_dim.30), channel_id=1, replica_groups=mesh['section'=2,'row'=8,'col'=32] {'col'}, dimensions={0} | all-to-all | bytes 1048576 | tf_op jit(solution)/shard_map/cond/branch_1_fun/all_to_all | solution.py:150
  113.4 4.5 %branch_1_fun.6 = bf16[8,2,64,256]{3,2,1,0:T(8,128)(2,1)S(1)} custom-call(s32[2,128]{1,0:T(2,128)S(1)} %get-tuple-element.68.refs_0_.index, s32[2,128]{1,0:T(2,128)S(1)} %get-tuple-element.69.refs_1_, bf16[32,2,32,128]{3,2,1,0:T(8,128)(2,1)S(1)} %all_to_all.71.refs_2_, bf16[64,64,128]{2,1,0:T(8,128)(2,1)S(1)} %get-tuple-element.77.refs_3_.values, ...), custom_call_target="tpu_custom_call" | custom-call | flops 2000000000 | bytes 4194304 | tf_op jit(solution)/shard_map/cond/branch_1_fun/pallas_call | solution.py:65
  117.9 14.7 %all_to_all.72 = bf16[8,2,64,256]{3,2,1,0:T(8,128)(2,1)S(1)} all-to-all(bf16[8,2,64,256]{3,2,1,0:T(8,128)(2,1)S(1)} %branch_1_fun.6), channel_id=1, replica_groups=mesh['section'=2,'row'=8,'col'=32] {'row'}, dimensions={0} | all-to-all | bytes 1048576 | tf_op jit(solution)/shard_map/cond/branch_1_fun/all_to_all | solution.py:150
  132.6 0.1 convert_reduce_fusion.4
  132.7 11.7 %all_to_all.73.hidden_ref = bf16[8,64,256]{2,1,0:T(8,128)(2,1)S(1)} all-to-all(bf16[8,64,256]{2,1,0:T(8,128)(2,1)S(1)} %broadcast_in_dim.32), channel_id=1, replica_groups=mesh['section'=2,'row'=8,'col'=32] {'row'}, dimensions={0} | all-to-all | bytes 524288 | tf_op jit(solution)/shard_map/cond/branch_1_fun/all_to_all | solution.py:150
  144.5 2.4 %branch_1_fun.7 = bf16[32,32,128]{2,1,0:T(8,128)(2,1)S(1)} custom-call(s32[2,128]{1,0:T(2,128)S(1)} %get-tuple-element.68.refs_0_.index, bf16[8,64,256]{2,1,0:T(8,128)(2,1)S(1)} %all_to_all.73.hidden_ref, bf16[64,64,128]{2,1,0:T(8,128)(2,1)S(1)} %get-tuple-element.77.refs_3_.values), custom_call_target="tpu_custom_call" | custom-call | flops 1000000000 | bytes 2097152 | tf_op jit(solution)/shard_map/cond/branch_1_fun/pallas_call | solution.py:119
  146.9 18.9 %all_to_all.74 = bf16[32,32,128]{2,1,0:T(8,128)(2,1)S(1)} all-to-all(bf16[32,32,128]{2,1,0:T(8,128)(2,1)S(1)} %branch_1_fun.7), channel_id=1, replica_groups=mesh['section'=2,'row'=8,'col'=32] {'col'}, dimensions={0} | all-to-all | bytes 524288 | tf_op jit(solution)/shard_map/cond/branch_1_fun/all_to_all | solution.py:150
  165.8 0.0 copy-start.2
  165.9 0.6 copy-done.2
  166.5 7.9 %collective-permute-start.4 = (bf16[32,128]{1,0:T(8,128)(2,1)S(1)}, bf16[32,128]{1,0:T(8,128)(2,1)S(1)}, u32[]{:S(2)}, u32[]{:S(2)}) collective-permute-start(bf16[32,128]{1,0:T(8,128)(2,1)S(1)} %get-tuple-element.97), channel_id=1, source_target_pairs={{0,256},{256,0},{1,257},{257,1},{2,258},{258,2},{3,259},{259,3},{4... | collective-permute-start | bytes 24584 | tf_op jit(solution)/shard_map/ppermute | solution.py:170
  174.5 0.8 collective-permute-done.4
  175.3 0.6 select_n.54
  (20 shorter events, 0.4 us)
Async XLA Ops:
  0.0 9.6 %copy-start = (bf16[1,4,2048]{2,1,0:T(4,128)(2,1)S(1)}, bf16[1,4,2048]{2,1,0:T(4,128)(2,1)}, u32[]{:S(2)}) copy-start(bf16[1,4,2048]{2,1,0:T(4,128)(2,1)} %param.9) | copy-start | bytes 49156
  0.0 0.7 copy-start.3
  0.0 37.4 %copy-start.6 = (bf16[1,1,1,64,64,128]{5,4,3,2,1,0:T(8,128)(2,1)S(1)}, bf16[1,1,1,64,64,128]{5,4,3,2,1,0:T(8,128)(2,1)}, u32[]{:S(2)}) copy-start(bf16[1,1,1,64,64,128]{5,4,3,2,1,0:T(8,128)(2,1)} %param.10) | copy-start | bytes 3145732
  0.8 9.6 %collective-permute-start = (bf16[32,128]{1,0:T(8,128)(2,1)S(1)}, bf16[32,128]{1,0:T(8,128)(2,1)S(1)}, u32[]{:S(2)}, u32[]{:S(2)}) collective-permute-start(bf16[32,128]{1,0:T(8,128)(2,1)S(1)} %reshape.39), channel_id=1, source_target_pairs={{0,256},{256,0},{1,257},{257,1},{2,258},{258,2},{3,259},{259,3},{4... | collective-permute-start | bytes 24584 | tf_op jit(solution)/shard_map/ppermute | solution.py:170
  10.4 27.0 %collective-permute-start.2 = (bf16[64,64,128]{2,1,0:T(8,128)(2,1)}, bf16[64,64,128]{2,1,0:T(8,128)(2,1)S(1)}, u32[]{:S(2)}, u32[]{:S(2)}) collective-permute-start(bf16[64,64,128]{2,1,0:T(8,128)(2,1)} %bitcast.32), channel_id=1, source_target_pairs={{0,256},{256,0},{1,257},{257,1},{2,258},{258,2},{3,259},{259,3},{4... | collective-permute-start | bytes 3145736 | tf_op jit(solution)/shard_map/ppermute | solution.py:170
  12.7 24.8 %collective-permute-start.3 = (bf16[64,64,128]{2,1,0:T(8,128)(2,1)}, bf16[64,64,128]{2,1,0:T(8,128)(2,1)}, u32[]{:S(2)}, u32[]{:S(2)}) collective-permute-start(bf16[64,64,128]{2,1,0:T(8,128)(2,1)} %bitcast.35), channel_id=1, source_target_pairs={{0,256},{256,0},{1,257},{257,1},{2,258},{258,2},{3,259},{259,3},{4... | collective-permute-start | bytes 3145736 | tf_op jit(solution)/shard_map/ppermute | solution.py:170
  15.7 7.7 %copy-start.4 = (s32[1,1,1,2,128]{4,3,2,1,0:T(2,128)S(1)}, s32[1,1,1,2,128]{4,3,2,1,0:T(2,128)}, u32[]{:S(2)}) copy-start(s32[1,1,1,2,128]{4,3,2,1,0:T(2,128)} %param.13) | copy-start | bytes 3076
  15.7 7.7 %copy-start.5 = (s32[1,1,1,2,128]{4,3,2,1,0:T(2,128)S(1)}, s32[1,1,1,2,128]{4,3,2,1,0:T(2,128)}, u32[]{:S(2)}) copy-start(s32[1,1,1,2,128]{4,3,2,1,0:T(2,128)} %param.11) | copy-start | bytes 3076
  15.7 21.7 %all-to-all-start.14 = ((bf16[32,2,32,128]{3,2,1,0:T(8,128)(2,1)}), bf16[32,2,32,128]{3,2,1,0:T(8,128)(2,1)S(1)}, u32[]{:S(2)}, u32[]{:S(2)}) async-start(bf16[32,2,32,128]{3,2,1,0:T(8,128)(2,1)} %broadcast_in_dim.34), calls=%async_computation.14 | async-start | bytes 1048576 | tf_op jit(solution)/shard_map/all_to_all | solution.py:150
  23.4 3.3 %collective-permute-start.1 = (s32[4,128]{1,0:T(4,128)S(1)}, s32[4,128]{1,0:T(4,128)S(1)}, u32[]{:S(2)}, u32[]{:S(2)}) collective-permute-start(s32[4,128]{1,0:T(4,128)S(1)} %pad_add_fusion), channel_id=1, source_target_pairs={{0,256},{256,0},{1,257},{257,1},{2,258},{258,2},{3,259},{259,3},{4... | collective-permute-start | bytes 6152 | tf_op jit(solution)/shard_map/ppermute | solution.py:170
  97.1 0.6 copy-start.1
  165.8 0.7 copy-start.2
  166.5 8.7 %collective-permute-start.4 = (bf16[32,128]{1,0:T(8,128)(2,1)S(1)}, bf16[32,128]{1,0:T(8,128)(2,1)S(1)}, u32[]{:S(2)}, u32[]{:S(2)}) collective-permute-start(bf16[32,128]{1,0:T(8,128)(2,1)S(1)} %get-tuple-element.97), channel_id=1, source_target_pairs={{0,256},{256,0},{1,257},{257,1},{2,258},{258,2},{3,259},{259,3},{4... | collective-permute-start | bytes 24584 | tf_op jit(solution)/shard_map/ppermute | solution.py:170

commit v3 on v2

--- a/solution.py
+++ b/solution.py
@@ -20,20 +20,21 @@
     return lax.broadcasted_iota(jnp.int32, (rows, LANES), 1) < BLK
 
 
-def forward_kernel(count, *refs):
+def forward_kernel(count, ahead, *refs):
     index, x_ref, values = refs[:count], refs[count], refs[count + 1 : 2 * count + 1]
-    out_ref, rows, blocks, even, odd = refs[2 * count + 1 :]
+    out_ref, rows, blocks, total = refs[2 * count + 1 + ahead :]
     tokens = blocks.shape[1]
     subs = blocks.shape[0] // 2
     left = left_half(tokens)
+    if ahead:
+        out_ref[:, 0] = refs[2 * count + 1][:, 0]
     for i in range(count):
         rows[...] = x_ref[:, i].reshape(rows.shape).astype(jnp.float32)
         for w in range(subs):
             both = rows[pl.ds(w, tokens, stride=subs), :]
             blocks[2 * w] = both.astype(jnp.bfloat16)
             blocks[2 * w + 1] = pltpu.roll(both, BLK, 1).astype(jnp.bfloat16)
-        even[...] = jnp.zeros_like(even)
-        odd[...] = jnp.zeros_like(odd)
+        total[...] = jnp.zeros_like(total)
 
         def multiply(pair, carry):
             first, second = 2 * pair, 2 * pair + 1
@@ -41,46 +42,46 @@
             product = jnp.dot(
                 jnp.concatenate(picked), values[i][pair], preferred_element_type=jnp.float32
             )
-            even[index[i][1, first]] += product[:tokens]
-            odd[index[i][1, second]] += product[tokens:]
+            total[index[i][1, first]] += jnp.where(left, product[:tokens], 0.0)
+            total[index[i][1, second]] += jnp.where(left, 0.0, product[tokens:])
             return carry
 
         lax.fori_loop(0, values[i].shape[0], multiply, 0, unroll=UNROLL)
         chunk = out_ref.shape[3] // LANES
-        for j in range(even.shape[0] // 2):
-            a, b = 2 * j, 2 * j + 1
-            straight = jnp.where(left, even[a], odd[b])
-            crossed = jnp.where(left, even[b], odd[a])
-            total = straight + pltpu.roll(crossed, BLK, 1)
+        for j in range(total.shape[0] // 2):
+            a, b = total[2 * j], total[2 * j + 1]
+            summed = jnp.where(left, a, b) + pltpu.roll(jnp.where(left, b, a), BLK, 1)
             lanes = slice((j % chunk) * LANES, (j % chunk + 1) * LANES)
-            out_ref[j // chunk, i, :, lanes] = total.astype(jnp.bfloat16)
-
-
-def forward(x, weights, n_row, ff_tile):
+            out_ref[j // chunk, i + ahead, :, lanes] = summed.astype(jnp.bfloat16)
+
+
+def forward(x, weights, n_row, ff_tile, prior=None):
     count = len(weights)
+    ahead = 0 if prior is None else 1
     n_col, _, per, _ = x.shape
     tokens = n_col * PER_COL
     subs = per // PER_COL
-    blocks_out = ff_tile // BLK
     return pl.pallas_call(
-        functools.partial(forward_kernel, count),
-        out_shape=jax.ShapeDtypeStruct((n_row, count, tokens, ff_tile // n_row), jnp.bfloat16),
-        in_specs=[SMEM] * count + [VMEM] * (1 + count),
+        functools.partial(forward_kernel, count, ahead),
+        out_shape=jax.ShapeDtypeStruct(
+            (n_row, count + ahead, tokens, ff_tile // n_row), jnp.bfloat16
+        ),
+        in_specs=[SMEM] * count + [VMEM] * (1 + count + ahead),
         out_specs=VMEM,
         scratch_shapes=[
             pltpu.VMEM((n_col * per, LANES), jnp.float32),
             pltpu.VMEM((2 * subs, tokens, LANES), jnp.bfloat16),
-            pltpu.VMEM((blocks_out, tokens, LANES), jnp.float32),
-            pltpu.VMEM((blocks_out, tokens, LANES), jnp.float32),
+            pltpu.VMEM((ff_tile // BLK, tokens, LANES), jnp.float32),
         ],
         compiler_params=pltpu.CompilerParams(vmem_limit_bytes=16 * 2**20),
         cost_estimate=pl.CostEstimate(
             flops=count * 10**9, bytes_accessed=count * 2 * 2**20, transcendentals=0
         ),
-    )(*[w[0] for w in weights], x, *[w[1] for w in weights])
-
-
-def backward_kernel(index, hidden_ref, values, out_ref, rows, lower, upper, total):
+    )(*[w[0] for w in weights], x, *[w[1] for w in weights], *([prior] if ahead else []))
+
+
+def backward_kernel(ahead, index, hidden_ref, values, *refs):
+    out_ref, rows, lower, upper, total = refs[ahead:]
     tokens = lower.shape[1]
     subs = total.shape[0] // 2
     chunk = hidden_ref.shape[2] // LANES
@@ -109,17 +110,21 @@
     for w in range(subs):
         both = jnp.concatenate([total[2 * w], total[2 * w + 1]], axis=1)
         rows[pl.ds(w, tokens, stride=subs), :] = both
-    out_ref[...] = rows[...].astype(jnp.bfloat16).reshape(out_ref.shape)
-
-
-def backward(hidden_grad, weights, n_col, width):
+    n_col, _, per, _ = out_ref.shape
+    out_ref[:, 0] = rows[...].astype(jnp.bfloat16).reshape(n_col, per, LANES)
+    if ahead:
+        out_ref[:, 1] = jnp.broadcast_to(refs[0][...][None], (n_col, per, LANES))
+
+
+def backward(hidden_grad, weights, n_col, width, shard=None):
     tokens = hidden_grad.shape[1]
     ff_tile = hidden_grad.shape[0] * hidden_grad.shape[2]
     per = PER_COL * width // LANES
+    ahead = 0 if shard is None else 1
     return pl.pallas_call(
-        backward_kernel,
-        out_shape=jax.ShapeDtypeStruct((n_col, per, LANES), jnp.bfloat16),
-        in_specs=[SMEM, VMEM, VMEM],
+        functools.partial(backward_kernel, ahead),
+        out_shape=jax.ShapeDtypeStruct((n_col, 1 + ahead, per, LANES), jnp.bfloat16),
+        in_specs=[SMEM] + [VMEM] * (2 + ahead),
         out_specs=VMEM,
         scratch_shapes=[
             pltpu.VMEM((n_col * per, LANES), jnp.float32),
@@ -129,7 +134,7 @@
         ],
         compiler_params=pltpu.CompilerParams(vmem_limit_bytes=16 * 2**20),
         cost_estimate=pl.CostEstimate(flops=10**9, bytes_accessed=2 * 2**20, transcendentals=0),
-    )(weights[0], hidden_grad, weights[1])
+    )(weights[0], hidden_grad, weights[1], *([shard] if ahead else []))
 
 
 def gelu_slope(hidden):
@@ -152,8 +157,8 @@
     def gather(v, axis):
         return exchange(jnp.broadcast_to(v[None], (lax.axis_size(axis),) + v.shape), axis)
 
-    def products(x, weights):
-        return forward(x, weights, n_row, ff_tile)
+    def products(x, weights, prior=None):
+        return forward(x, weights, n_row, ff_tile, prior)
 
     def row_sums(parts):
         return jnp.sum(exchange(parts, "row").astype(jnp.float32), axis=0)
@@ -161,10 +166,12 @@
     def add(g, part):
         return (g.astype(jnp.float32) + part).astype(jnp.bfloat16)
 
-    def col_sum(sums, w_in):
+    def scatter(sums, w_in, shard=None):
         hidden_grad = (sums[1] * gelu_slope(sums[0])).astype(jnp.bfloat16)
-        part = exchange(backward(gather(hidden_grad, "row"), w_in, n_col, width), "col")
-        return jnp.sum(part.astype(jnp.float32), axis=0)
+        return exchange(backward(gather(hidden_grad, "row"), w_in, n_col, width, shard), "col")
+
+    def total(parts):
+        return jnp.sum(parts[:, 0].astype(jnp.float32), axis=0)
 
     def swap(v):
         return lax.ppermute(v, "section", SWAP)
@@ -179,19 +186,20 @@
     g1 = shard_of(out_grad[0], PER_COL * section)
     shards = jnp.stack([jnp.where(is_last, mine, other), g1])
     x0 = jnp.where(is_last, other, mine)
-    shards, in_sent, out_sent, in_at, out_at = lax.optimization_barrier(
-        (shards, in_own, out_own, in_at, out_at)
-    )
+    shards, in_at, out_at = lax.optimization_barrier((shards, in_at, out_at))
     first = gather(shards, "col")
+    at_oth = swap(jnp.concatenate([in_at, out_at]))
+    at_oth, in_sent, out_sent = lax.optimization_barrier((at_oth, in_own, out_own))
     in_oth, out_oth = swap(in_sent), swap(out_sent)
-    at_oth = swap(jnp.concatenate([in_at, out_at]))
     own = ((in_at, in_own), (out_at, out_own))
     oth = ((at_oth[:2], in_oth), (at_oth[2:], out_oth))
 
     def layers(w1, w0, first, g1, x0):
-        g0 = add(g1, col_sum(row_sums(products(first, w1)), w1[0]))
-        second = gather(jnp.stack([x0, g0]), "col")
-        return g0, col_sum(row_sums(products(second, w0)), w0[0])
+        parts = scatter(row_sums(products(first, w1)), w1[0], x0)
+        g0 = add(g1, total(parts))
+        second = gather(g0[None], "col")
+        hidden0 = products(parts[:, 1:], w0[:1])
+        return g0, total(scatter(row_sums(products(second, w0[1:], hidden0)), w0[0]))
 
     def later_core(own, oth, *rest):
         return layers(own, oth, *rest)

time: 177 us -> 181 us (1.023)
  blocking collectives: 113 us -> 97.2 us
  waiting for transfers between devices: 13 us -> 23.6 us
  starting transfers between devices: 31.2 us -> 38.6 us
    all_to_all x7 -> x6, blocking collectives: 113 us -> 97.2 us  [exchange(): return lax.all_to_all(v, axis, 0, 0)]
    all_to_all x1 -> x2, waiting for transfers between devices: 10.7 us -> 21.3 us  [exchange(): return lax.all_to_all(v, axis, 0, 0)]
    all_to_all x1 -> x2, starting transfers between devices: 7.64 us -> 14.8 us  [exchange(): return lax.all_to_all(v, axis, 0, 0)]
    pallas_call x4 -> x5, Pallas kernels: 13.9 us -> 15.4 us  [the longest x3 10.4 us: forward(): pl.pallas_call(functools.partial(forward_kernel, count, ahead), out_shape...]
  transfers between devices with their start and end apart: 6 -> 7, of which waited for: 4 -> 5; matrix products, arithmetic and copies ran while one was open for 1% -> 1% of each run, Pallas kernels for 0% -> 1%
where the time goes in v3:
time: 181 us; the launch traced here: 180 us
  blocking collectives  97.2 us (54%)
  starting transfers between devices  38.6 us (21%)
  waiting for transfers between devices  23.6 us (13%)
  Pallas kernels  15.4 us (9%)
  local copies, waits for them, and re-layouts  4.5 us (2%)
    all_to_all x6, blocking collectives, exchange(): return lax.all_to_all(v, axis, 0, 0)  97.2 us
    ppermute x5, starting transfers between devices, swap(): return lax.ppermute(v, 'section', SWAP)  23.7 us
    all_to_all x2, waiting for transfers between devices, exchange(): return lax.all_to_all(v, axis, 0, 0)  21.3 us
    all_to_all x2, starting transfers between devices, exchange(): return lax.all_to_all(v, axis, 0, 0)  14.8 us
    pallas_call x3, Pallas kernels, forward(): pl.pallas_call(functools.partial(forward_kernel, count, ahead), out_shape...  10.4 us
    pallas_call x2, Pallas kernels, backward(): pl.pallas_call(functools.partial(backward_kernel, ahead), out_shape=jax.S...  4.93 us
  transfers between devices with their start and end apart: 7, of which 5 were waited for; matrix products, arithmetic and copies ran while one was open for 1% of the time, Pallas kernels for 1%

profile of v3, /device:TPU:1, one launch (start us, length us, event | category | flops | bytes accessed | tf_op | source)
XLA Modules:
  0.0 179.8 jit_solution(11056344450688024398)
XLA Ops:
  0.0 0.0 copy-start
  0.0 0.0 copy-start.3
  0.0 0.7 copy-done.3
  0.8 8.8 %collective-permute-start = (bf16[32,128]{1,0:T(8,128)(2,1)S(1)}, bf16[32,128]{1,0:T(8,128)(2,1)S(1)}, u32[]{:S(2)}, u32[]{:S(2)}) collective-permute-start(bf16[32,128]{1,0:T(8,128)(2,1)S(1)} %reshape.49), channel_id=1, source_target_pairs={{0,256},{256,0},{1,257},{257,1},{2,258},{258,2},{3,259},{259,3},{4... | collective-permute-start | bytes 24584 | tf_op jit(solution)/shard_map/ppermute | solution.py:177
  9.6 0.0 copy-done
  9.6 0.7 collective-permute-done
  10.4 0.0 copy-start.5
  10.4 0.0 copy-start.4
  10.4 0.0 copy-start.6
  10.4 0.6 copy-done.5
  11.1 0.0 copy-done.4
  11.1 2.2 %collective-permute-start.1 = (s32[4,128]{1,0:T(4,128)S(1)}, s32[4,128]{1,0:T(4,128)S(1)}, u32[]{:S(2)}, u32[]{:S(2)}) collective-permute-start(s32[4,128]{1,0:T(4,128)S(1)} %pad_add_fusion), channel_id=1, source_target_pairs={{0,256},{256,0},{1,257},{257,1},{2,258},{258,2},{3,259},{259,3},{4... | collective-permute-start | bytes 6152 | tf_op jit(solution)/shard_map/ppermute | solution.py:177
  13.3 0.8 collective-permute-done.1
  14.1 2.2 %collective-permute-start.2 = (bf16[64,64,128]{2,1,0:T(8,128)(2,1)}, bf16[64,64,128]{2,1,0:T(8,128)(2,1)S(1)}, u32[]{:S(2)}, u32[]{:S(2)}) collective-permute-start(bf16[64,64,128]{2,1,0:T(8,128)(2,1)} %bitcast.24), channel_id=1, source_target_pairs={{0,256},{256,0},{1,257},{257,1},{2,258},{258,2},{3,259},{259,3},{4... | collective-permute-start | bytes 3145736 | tf_op jit(solution)/shard_map/ppermute | solution.py:177
  16.4 2.1 %collective-permute-start.3 = (bf16[64,64,128]{2,1,0:T(8,128)(2,1)}, bf16[64,64,128]{2,1,0:T(8,128)(2,1)}, u32[]{:S(2)}, u32[]{:S(2)}) collective-permute-start(bf16[64,64,128]{2,1,0:T(8,128)(2,1)} %bitcast.27), channel_id=1, source_target_pairs={{0,256},{256,0},{1,257},{257,1},{2,258},{258,2},{3,259},{259,3},{4... | collective-permute-start | bytes 3145736 | tf_op jit(solution)/shard_map/ppermute | solution.py:177
  18.5 0.9 broadcast_in_dim.34
  19.4 7.5 %all-to-all-start.14 = ((bf16[32,2,32,128]{3,2,1,0:T(8,128)(2,1)}), bf16[32,2,32,128]{3,2,1,0:T(8,128)(2,1)S(1)}, u32[]{:S(2)}, u32[]{:S(2)}) async-start(bf16[32,2,32,128]{3,2,1,0:T(8,128)(2,1)} %broadcast_in_dim.34), calls=%async_computation.14 | async-start | bytes 1048576 | tf_op jit(solution)/shard_map/all_to_all | solution.py:155
  26.9 14.1 %all-to-all-done.14 = bf16[32,2,32,128]{3,2,1,0:T(8,128)(2,1)S(1)} async-done(((bf16[32,2,32,128]{3,2,1,0:T(8,128)(2,1)}), bf16[32,2,32,128]{3,2,1,0:T(8,128)(2,1)S(1)}, u32[]{:S(2)}, u32[]{:S(2)}) %all-to-all-start.14) | async-done | bytes 524320 | tf_op jit(solution)/shard_map/all_to_all | solution.py:155
  41.0 0.0 collective-permute-done.2
  41.0 0.0 collective-permute-done.3
  41.0 0.0 copy-done.6
  41.0 129.0 %conditional.4 = (f32[32,128]{1,0:T(8,128)S(1)}, bf16[32,128]{1,0:T(8,128)(2,1)S(1)}) conditional(s32[]{:T(128)} %convert_element_type.71, (bf16[32,128]{1,0:T(8,128)(2,1)S(1)}, s32[2,128]{1,0:T(2,128)S(1)}, s32[2,128]{1,0:T(2,128)S(1)}, bf16[32,2,32,128]{3,2,1,0:T(8,128)(2,1)S(1)}, bf16[64,64,128]{2,1,0:T(8,128)(2,1)S(1)}, ...), branch_computations={%region_0.5_spmd, %region_5.10_spmd} | conditional | flops 6001839104 | bytes 25894988
  41.0 4.9 %branch_1_fun.5 = bf16[8,2,64,256]{3,2,1,0:T(8,128)(2,1)S(1)} custom-call(s32[2,128]{1,0:T(2,128)S(1)} %get-tuple-element.71.refs_0_.index, s32[2,128]{1,0:T(2,128)S(1)} %get-tuple-element.72.refs_1_, bf16[32,2,32,128]{3,2,1,0:T(8,128)(2,1)S(1)} %get-tuple-element.73.refs_2_, bf16[64,64,128]{2,1,0:T(8,128)(2,1)S(1)} %get-tuple-element.74.refs_3_.values, ...), custom_call_target="tpu_custom_call" | custom-call | flops 2000000000 | bytes 4194304 | tf_op jit(solution)/shard_map/cond/branch_1_fun/pallas_call | solution.py:64
  46.0 19.6 %all_to_all.67 = bf16[8,2,64,256]{3,2,1,0:T(8,128)(2,1)S(1)} all-to-all(bf16[8,2,64,256]{3,2,1,0:T(8,128)(2,1)S(1)} %branch_1_fun.5), channel_id=1, replica_groups=mesh['section'=2,'row'=8,'col'=32] {'row'}, dimensions={0} | all-to-all | bytes 1048576 | tf_op jit(solution)/shard_map/cond/branch_1_fun/all_to_all | solution.py:155
  65.6 0.1 convert_reduce_fusion.5
  65.7 13.0 %all_to_all.68.hidden_ref = bf16[8,64,256]{2,1,0:T(8,128)(2,1)S(1)} all-to-all(bf16[8,64,256]{2,1,0:T(8,128)(2,1)S(1)} %broadcast_in_dim.29), channel_id=1, replica_groups=mesh['section'=2,'row'=8,'col'=32] {'row'}, dimensions={0} | all-to-all | bytes 524288 | tf_op jit(solution)/shard_map/cond/branch_1_fun/all_to_all | solution.py:155
  78.7 2.5 %branch_1_fun.6 = bf16[32,2,32,128]{3,2,1,0:T(8,128)(2,1)S(1)} custom-call(s32[2,128]{1,0:T(2,128)S(1)} %get-tuple-element.71.refs_0_.index, bf16[8,64,256]{2,1,0:T(8,128)(2,1)S(1)} %all_to_all.68.hidden_ref, bf16[64,64,128]{2,1,0:T(8,128)(2,1)S(1)} %get-tuple-element.74.refs_3_.values, bf16[32,128]{1,0:T(8,128)(2,1)S(1)} %get-tuple-element.76.refs_0_), custom_call_target="tpu_custom_call" | custom-call | flops 1000000000 | bytes 2097152 | tf_op jit(solution)/shard_map/cond/branch_1_fun/pallas_call | solution.py:124
  81.2 21.7 %all_to_all.69 = bf16[32,2,32,128]{3,2,1,0:T(8,128)(2,1)S(1)} all-to-all(bf16[32,2,32,128]{3,2,1,0:T(8,128)(2,1)S(1)} %branch_1_fun.6), channel_id=1, replica_groups=mesh['section'=2,'row'=8,'col'=32] {'col'}, dimensions={0} | all-to-all | bytes 1048576 | tf_op jit(solution)/shard_map/cond/branch_1_fun/all_to_all | solution.py:155
  103.0 0.0 copy-start.1
  103.0 0.7 broadcast_in_dim.30
  103.7 0.0 copy-done.1
  103.7 7.3 %all-to-all-start.10 = ((bf16[32,1,32,128]{3,2,1,0:T(8,128)(2,1)}), bf16[32,1,32,128]{3,2,1,0:T(8,128)(2,1)S(1)}, u32[]{:S(2)}, u32[]{:S(2)}) async-start(bf16[32,1,32,128]{3,2,1,0:T(8,128)(2,1)} %broadcast_in_dim.30), calls=%async_computation.10 | async-start | bytes 524288 | tf_op jit(solution)/shard_map/cond/branch_1_fun/all_to_all | solution.py:155
  111.1 2.4 %branch_1_fun.7.refs_3_ = bf16[8,1,64,256]{3,2,1,0:T(8,128)(2,1)S(1)} custom-call(s32[2,128]{1,0:T(2,128)S(1)} %get-tuple-element.68.refs_0_.index, bf16[32,1,32,128]{3,2,1,0:T(8,128)(2,1)S(1)} %slice.53.refs_1_, bf16[64,64,128]{2,1,0:T(8,128)(2,1)S(1)} %get-tuple-element.78.refs_2_.values), custom_call_target="tpu_custom_call" | custom-call | flops 1000000000 | bytes 2097152 | tf_op jit(solution)/shard_map/cond/branch_1_fun/pallas_call | solution.py:64
  113.5 7.2 %all-to-all-done.10.refs_1_ = bf16[32,1,32,128]{3,2,1,0:T(8,128)(2,1)S(1)} async-done(((bf16[32,1,32,128]{3,2,1,0:T(8,128)(2,1)}), bf16[32,1,32,128]{3,2,1,0:T(8,128)(2,1)S(1)}, u32[]{:S(2)}, u32[]{:S(2)}) %all-to-all-start.10) | async-done | bytes 262176 | tf_op jit(solution)/shard_map/cond/branch_1_fun/all_to_all | solution.py:155
  120.7 3.1 %branch_1_fun.8 = bf16[8,2,64,256]{3,2,1,0:T(8,128)(2,1)S(1)} custom-call(s32[2,128]{1,0:T(2,128)S(1)} %get-tuple-element.69.refs_0_, bf16[32,1,32,128]{3,2,1,0:T(8,128)(2,1)S(1)} %all-to-all-done.10.refs_1_, bf16[64,64,128]{2,1,0:T(8,128)(2,1)} %get-tuple-element.77.refs_2_, bf16[8,1,64,256]{3,2,1,0:T(8,128)(2,1)S(1)} %branch_1_fun.7.refs_3_), custom_call_target="tpu_custom_call" | custom-call | flops 1000000000 | bytes 2097152 | tf_op jit(solution)/shard_map/cond/branch_1_fun/pallas_call | solution.py:64
  123.8 15.6 %all_to_all.70 = bf16[8,2,64,256]{3,2,1,0:T(8,128)(2,1)S(1)} all-to-all(bf16[8,2,64,256]{3,2,1,0:T(8,128)(2,1)S(1)} %branch_1_fun.8), channel_id=1, replica_groups=mesh['section'=2,'row'=8,'col'=32] {'row'}, dimensions={0} | all-to-all | bytes 1048576 | tf_op jit(solution)/shard_map/cond/branch_1_fun/all_to_all | solution.py:155
  139.4 0.1 convert_reduce_fusion.4
  139.5 12.2 %all_to_all.71.hidden_ref = bf16[8,64,256]{2,1,0:T(8,128)(2,1)S(1)} all-to-all(bf16[8,64,256]{2,1,0:T(8,128)(2,1)S(1)} %broadcast_in_dim.32), channel_id=1, replica_groups=mesh['section'=2,'row'=8,'col'=32] {'row'}, dimensions={0} | all-to-all | bytes 524288 | tf_op jit(solution)/shard_map/cond/branch_1_fun/all_to_all | solution.py:155
  151.7 2.4 %branch_1_fun.9 = bf16[32,1,32,128]{3,2,1,0:T(8,128)(2,1)S(1)} custom-call(s32[2,128]{1,0:T(2,128)S(1)} %get-tuple-element.68.refs_0_.index, bf16[8,64,256]{2,1,0:T(8,128)(2,1)S(1)} %all_to_all.71.hidden_ref, bf16[64,64,128]{2,1,0:T(8,128)(2,1)S(1)} %get-tuple-element.78.refs_2_.values), custom_call_target="tpu_custom_call" | custom-call | flops 1000000000 | bytes 2097152 | tf_op jit(solution)/shard_map/cond/branch_1_fun/pallas_call | solution.py:124
  154.2 15.1 %all_to_all.72 = bf16[32,1,32,128]{3,2,1,0:T(8,128)(2,1)S(1)} all-to-all(bf16[32,1,32,128]{3,2,1,0:T(8,128)(2,1)S(1)} %branch_1_fun.9), channel_id=1, replica_groups=mesh['section'=2,'row'=8,'col'=32] {'col'}, dimensions={0} | all-to-all | bytes 524288 | tf_op jit(solution)/shard_map/cond/branch_1_fun/all_to_all | solution.py:155
  169.3 0.0 copy-start.2
  169.3 0.6 copy-done.2
  170.0 8.4 %collective-permute-start.4 = (bf16[32,128]{1,0:T(8,128)(2,1)S(1)}, bf16[32,128]{1,0:T(8,128)(2,1)S(1)}, u32[]{:S(2)}, u32[]{:S(2)}) collective-permute-start(bf16[32,128]{1,0:T(8,128)(2,1)S(1)} %get-tuple-element.99), channel_id=1, source_target_pairs={{0,256},{256,0},{1,257},{257,1},{2,258},{258,2},{3,259},{259,3},{4... | collective-permute-start | bytes 24584 | tf_op jit(solution)/shard_map/ppermute | solution.py:177
  178.4 0.8 collective-permute-done.4
  179.2 0.6 select_n.54
  (20 shorter events, 0.4 us)
Async XLA Ops:
  0.0 9.6 %copy-start = (bf16[1,4,2048]{2,1,0:T(4,128)(2,1)S(1)}, bf16[1,4,2048]{2,1,0:T(4,128)(2,1)}, u32[]{:S(2)}) copy-start(bf16[1,4,2048]{2,1,0:T(4,128)(2,1)} %param.9) | copy-start | bytes 49156
  0.0 0.7 copy-start.3
  0.8 9.6 %collective-permute-start = (bf16[32,128]{1,0:T(8,128)(2,1)S(1)}, bf16[32,128]{1,0:T(8,128)(2,1)S(1)}, u32[]{:S(2)}, u32[]{:S(2)}) collective-permute-start(bf16[32,128]{1,0:T(8,128)(2,1)S(1)} %reshape.49), channel_id=1, source_target_pairs={{0,256},{256,0},{1,257},{257,1},{2,258},{258,2},{3,259},{259,3},{4... | collective-permute-start | bytes 24584 | tf_op jit(solution)/shard_map/ppermute | solution.py:177
  10.4 0.7 copy-start.5
  10.4 0.7 copy-start.4
  10.4 30.6 %copy-start.6 = (bf16[1,1,1,64,64,128]{5,4,3,2,1,0:T(8,128)(2,1)S(1)}, bf16[1,1,1,64,64,128]{5,4,3,2,1,0:T(8,128)(2,1)}, u32[]{:S(2)}) copy-start(bf16[1,1,1,64,64,128]{5,4,3,2,1,0:T(8,128)(2,1)} %param.10) | copy-start | bytes 3145732
  11.1 3.0 %collective-permute-start.1 = (s32[4,128]{1,0:T(4,128)S(1)}, s32[4,128]{1,0:T(4,128)S(1)}, u32[]{:S(2)}, u32[]{:S(2)}) collective-permute-start(s32[4,128]{1,0:T(4,128)S(1)} %pad_add_fusion), channel_id=1, source_target_pairs={{0,256},{256,0},{1,257},{257,1},{2,258},{258,2},{3,259},{259,3},{4... | collective-permute-start | bytes 6152 | tf_op jit(solution)/shard_map/ppermute | solution.py:177
  14.1 26.9 %collective-permute-start.2 = (bf16[64,64,128]{2,1,0:T(8,128)(2,1)}, bf16[64,64,128]{2,1,0:T(8,128)(2,1)S(1)}, u32[]{:S(2)}, u32[]{:S(2)}) collective-permute-start(bf16[64,64,128]{2,1,0:T(8,128)(2,1)} %bitcast.24), channel_id=1, source_target_pairs={{0,256},{256,0},{1,257},{257,1},{2,258},{258,2},{3,259},{259,3},{4... | collective-permute-start | bytes 3145736 | tf_op jit(solution)/shard_map/ppermute | solution.py:177
  16.4 24.6 %collective-permute-start.3 = (bf16[64,64,128]{2,1,0:T(8,128)(2,1)}, bf16[64,64,128]{2,1,0:T(8,128)(2,1)}, u32[]{:S(2)}, u32[]{:S(2)}) collective-permute-start(bf16[64,64,128]{2,1,0:T(8,128)(2,1)} %bitcast.27), channel_id=1, source_target_pairs={{0,256},{256,0},{1,257},{257,1},{2,258},{258,2},{3,259},{259,3},{4... | collective-permute-start | bytes 3145736 | tf_op jit(solution)/shard_map/ppermute | solution.py:177
  19.4 21.6 %all-to-all-start.14 = ((bf16[32,2,32,128]{3,2,1,0:T(8,128)(2,1)}), bf16[32,2,32,128]{3,2,1,0:T(8,128)(2,1)S(1)}, u32[]{:S(2)}, u32[]{:S(2)}) async-start(bf16[32,2,32,128]{3,2,1,0:T(8,128)(2,1)} %broadcast_in_dim.34), calls=%async_computation.14 | async-start | bytes 1048576 | tf_op jit(solution)/shard_map/all_to_all | solution.py:155
  103.0 0.8 copy-start.1
  103.7 17.0 %all-to-all-start.10 = ((bf16[32,1,32,128]{3,2,1,0:T(8,128)(2,1)}), bf16[32,1,32,128]{3,2,1,0:T(8,128)(2,1)S(1)}, u32[]{:S(2)}, u32[]{:S(2)}) async-start(bf16[32,1,32,128]{3,2,1,0:T(8,128)(2,1)} %broadcast_in_dim.30), calls=%async_computation.10 | async-start | bytes 524288 | tf_op jit(solution)/shard_map/cond/branch_1_fun/all_to_all | solution.py:155
  169.3 0.7 copy-start.2
  170.0 9.2 %collective-permute-start.4 = (bf16[32,128]{1,0:T(8,128)(2,1)S(1)}, bf16[32,128]{1,0:T(8,128)(2,1)S(1)}, u32[]{:S(2)}, u32[]{:S(2)}) collective-permute-start(bf16[32,128]{1,0:T(8,128)(2,1)S(1)} %get-tuple-element.99), channel_id=1, source_target_pairs={{0,256},{256,0},{1,257},{257,1},{2,258},{258,2},{3,259},{259,3},{4... | collective-permute-start | bytes 24584 | tf_op jit(solution)/shard_map/ppermute | solution.py:177

commit v4 on v2

--- a/solution.py
+++ b/solution.py
@@ -20,12 +20,14 @@
     return lax.broadcasted_iota(jnp.int32, (rows, LANES), 1) < BLK
 
 
-def forward_kernel(count, *refs):
+def forward_kernel(count, ahead, *refs):
     index, x_ref, values = refs[:count], refs[count], refs[count + 1 : 2 * count + 1]
-    out_ref, rows, blocks, even, odd = refs[2 * count + 1 :]
+    out_ref, rows, blocks, even, odd = refs[2 * count + 1 + ahead :]
     tokens = blocks.shape[1]
     subs = blocks.shape[0] // 2
     left = left_half(tokens)
+    if ahead:
+        out_ref[:, 0] = refs[2 * count + 1][:, 0]
     for i in range(count):
         rows[...] = x_ref[:, i].reshape(rows.shape).astype(jnp.float32)
         for w in range(subs):
@@ -51,33 +53,35 @@
             a, b = 2 * j, 2 * j + 1
             straight = jnp.where(left, even[a], odd[b])
             crossed = jnp.where(left, even[b], odd[a])
-            total = straight + pltpu.roll(crossed, BLK, 1)
+            summed = straight + pltpu.roll(crossed, BLK, 1)
             lanes = slice((j % chunk) * LANES, (j % chunk + 1) * LANES)
-            out_ref[j // chunk, i, :, lanes] = total.astype(jnp.bfloat16)
-
-
-def forward(x, weights, n_row, ff_tile):
+            out_ref[j // chunk, i + ahead, :, lanes] = summed.astype(jnp.bfloat16)
+
+
+def forward(x, weights, n_row, ff_tile, prior=None):
     count = len(weights)
+    ahead = 0 if prior is None else 1
     n_col, _, per, _ = x.shape
     tokens = n_col * PER_COL
     subs = per // PER_COL
-    blocks_out = ff_tile // BLK
     return pl.pallas_call(
-        functools.partial(forward_kernel, count),
-        out_shape=jax.ShapeDtypeStruct((n_row, count, tokens, ff_tile // n_row), jnp.bfloat16),
-        in_specs=[SMEM] * count + [VMEM] * (1 + count),
+        functools.partial(forward_kernel, count, ahead),
+        out_shape=jax.ShapeDtypeStruct(
+            (n_row, count + ahead, tokens, ff_tile // n_row), jnp.bfloat16
+        ),
+        in_specs=[SMEM] * count + [VMEM] * (1 + count + ahead),
         out_specs=VMEM,
         scratch_shapes=[
             pltpu.VMEM((n_col * per, LANES), jnp.float32),
             pltpu.VMEM((2 * subs, tokens, LANES), jnp.bfloat16),
-            pltpu.VMEM((blocks_out, tokens, LANES), jnp.float32),
-            pltpu.VMEM((blocks_out, tokens, LANES), jnp.float32),
+            pltpu.VMEM((ff_tile // BLK, tokens, LANES), jnp.float32),
+            pltpu.VMEM((ff_tile // BLK, tokens, LANES), jnp.float32),
         ],
         compiler_params=pltpu.CompilerParams(vmem_limit_bytes=16 * 2**20),
         cost_estimate=pl.CostEstimate(
             flops=count * 10**9, bytes_accessed=count * 2 * 2**20, transcendentals=0
         ),
-    )(*[w[0] for w in weights], x, *[w[1] for w in weights])
+    )(*[w[0] for w in weights], x, *[w[1] for w in weights], *([prior] if ahead else []))
 
 
 def backward_kernel(index, hidden_ref, values, out_ref, rows, lower, upper, total):
@@ -152,8 +156,8 @@
     def gather(v, axis):
         return exchange(jnp.broadcast_to(v[None], (lax.axis_size(axis),) + v.shape), axis)
 
-    def products(x, weights):
-        return forward(x, weights, n_row, ff_tile)
+    def products(x, weights, prior=None):
+        return forward(x, weights, n_row, ff_tile, prior)
 
     def row_sums(parts):
         return jnp.sum(exchange(parts, "row").astype(jnp.float32), axis=0)
@@ -174,24 +178,25 @@
 
     in_own, out_own = in_values[0, 0, 0], out_values[0, 0, 0]
     in_at, out_at = in_index[0, 0, 0], out_index[0, 0, 0]
+    places = jnp.concatenate([in_at, out_at]).astype(jnp.bfloat16)
+    places = jnp.pad(places, ((0, 12), (0, 0)))
     mine = shard_of(x_stash[0, 0], PER_COL * section)
-    other = swap(shard_of(x_stash[0, 0], PER_COL - PER_COL * section))
+    came = swap(jnp.concatenate([shard_of(x_stash[0, 0], PER_COL - PER_COL * section), places]))
+    other = came[:per]
+    at_oth = came[per : per + 4].astype(jnp.int32)
     g1 = shard_of(out_grad[0], PER_COL * section)
-    shards = jnp.stack([jnp.where(is_last, mine, other), g1])
-    x0 = jnp.where(is_last, other, mine)
-    shards, in_sent, out_sent, in_at, out_at = lax.optimization_barrier(
-        (shards, in_own, out_own, in_at, out_at)
-    )
+    shards = jnp.stack([jnp.where(is_last, mine, other), g1, jnp.where(is_last, other, mine)])
+    shards, in_sent, out_sent = lax.optimization_barrier((shards, in_own, out_own))
     first = gather(shards, "col")
     in_oth, out_oth = swap(in_sent), swap(out_sent)
-    at_oth = swap(jnp.concatenate([in_at, out_at]))
     own = ((in_at, in_own), (out_at, out_own))
     oth = ((at_oth[:2], in_oth), (at_oth[2:], out_oth))
 
-    def layers(w1, w0, first, g1, x0):
-        g0 = add(g1, col_sum(row_sums(products(first, w1)), w1[0]))
-        second = gather(jnp.stack([x0, g0]), "col")
-        return g0, col_sum(row_sums(products(second, w0)), w0[0])
+    def layers(w1, w0, first, g1):
+        g0 = add(g1, col_sum(row_sums(products(first[:, :2], w1)), w1[0]))
+        second = gather(g0[None], "col")
+        hidden0 = products(first[:, 2:], w0[:1])
+        return g0, col_sum(row_sums(products(second, w0[1:], hidden0)), w0[0])
 
     def later_core(own, oth, *rest):
         return layers(own, oth, *rest)
@@ -199,7 +204,7 @@
     def earlier_core(own, oth, *rest):
         return layers(oth, own, *rest)
 
-    g0, part = lax.cond(is_last, later_core, earlier_core, own, oth, first, g1, x0)
+    g0, part = lax.cond(is_last, later_core, earlier_core, own, oth, first, g1)
     last = add(g0, part)
 
     kept = jnp.where(is_last, g0, last)

time: 177 us -> 173 us (0.977)
  blocking collectives: 113 us -> 92.7 us
  waiting for transfers between devices: 13 us -> 22.6 us
  starting transfers between devices: 31.2 us -> 36.3 us
    all_to_all x7 -> x6, blocking collectives: 113 us -> 92.7 us  [exchange(): return lax.all_to_all(v, axis, 0, 0)]
    all_to_all x1 -> x2, waiting for transfers between devices: 10.7 us -> 18.3 us  [exchange(): return lax.all_to_all(v, axis, 0, 0)]
    all_to_all x1 -> x2, starting transfers between devices: 7.64 us -> 12 us  [exchange(): return lax.all_to_all(v, axis, 0, 0)]
    ppermute x5 -> x4, waiting for transfers between devices: 2.33 us -> 4.27 us  [swap(): return lax.ppermute(v, 'section', SWAP)]
    ppermute x5 -> x4, starting transfers between devices: 23.6 us -> 24.3 us  [swap(): return lax.ppermute(v, 'section', SWAP)]
    pallas_call x2 -> x3, Pallas kernels: 9.03 us -> 9.61 us  [forward(): pl.pallas_call(functools.partial(forward_kernel, count, ahead), out_shape...]
  transfers between devices with their start and end apart: 6 -> 6, of which waited for: 4 -> 6; matrix products, arithmetic and copies ran while one was open for 1% -> 0% of each run, Pallas kernels for 0% -> 2%
where the time goes in v4:
time: 173 us; the launch traced here: 172 us
  blocking collectives  92.7 us (54%)
  starting transfers between devices  36.3 us (21%)
  waiting for transfers between devices  22.6 us (13%)
  Pallas kernels  15.1 us (9%)
  local copies, waits for them, and re-layouts  4.66 us (3%)
    all_to_all x6, blocking collectives, exchange(): return lax.all_to_all(v, axis, 0, 0)  92.7 us
    ppermute x4, starting transfers between devices, swap(): return lax.ppermute(v, 'section', SWAP)  24.3 us
    all_to_all x2, waiting for transfers between devices, exchange(): return lax.all_to_all(v, axis, 0, 0)  18.3 us
    all_to_all x2, starting transfers between devices, exchange(): return lax.all_to_all(v, axis, 0, 0)  12 us
    pallas_call x3, Pallas kernels, forward(): pl.pallas_call(functools.partial(forward_kernel, count, ahead), out_shape...  9.61 us
    pallas_call x2, Pallas kernels, backward(): pl.pallas_call(backward_kernel, out_shape=jax.ShapeDtypeStruct((n_col, pe...  5.54 us
    ppermute x4, waiting for transfers between devices, swap(): return lax.ppermute(v, 'section', SWAP)  4.27 us
  transfers between devices with their start and end apart: 6, of which 6 were waited for; matrix products, arithmetic and copies ran while one was open for 0% of the time, Pallas kernels for 2%

profile of v4, /device:TPU:1, one launch (start us, length us, event | category | flops | bytes accessed | tf_op | source)
XLA Modules:
  0.0 172.0 jit_solution(5129703102994690462)
XLA Ops:
  0.0 0.0 copy-start
  0.0 0.0 copy-start.3
  0.0 0.7 copy-done.3
  0.8 0.0 copy-start.4
  0.8 0.0 copy-start.5
  0.8 0.6 copy-done.4
  1.4 0.0 copy-done.5
  1.5 8.8 %collective-permute-start = (bf16[48,128]{1,0:T(8,128)(2,1)S(1)}, bf16[48,128]{1,0:T(8,128)(2,1)S(1)}, u32[]{:S(2)}, u32[]{:S(2)}) collective-permute-start(bf16[48,128]{1,0:T(8,128)(2,1)S(1)} %pad_maximum_fusion.1), channel_id=1, source_target_pairs={{0,256},{256,0},{1,257},{257,1},{2,258},{258,2},{3,259},{259,3},{4... | collective-permute-start | bytes 36872 | tf_op jit(solution)/shard_map/ppermute | solution.py:174
  10.3 0.0 copy-done
  10.3 0.7 collective-permute-done
  11.1 0.0 copy-start.6
  11.1 0.0 copy-start.7
  11.1 1.0 broadcast_in_dim.34
  12.1 7.5 %all-to-all-start.14 = ((bf16[32,3,32,128]{3,2,1,0:T(8,128)(2,1)}), bf16[32,3,32,128]{3,2,1,0:T(8,128)(2,1)S(1)}, u32[]{:S(2)}, u32[]{:S(2)}) async-start(bf16[32,3,32,128]{3,2,1,0:T(8,128)(2,1)} %broadcast_in_dim.34), calls=%async_computation.14 | async-start | bytes 1572864 | tf_op jit(solution)/shard_map/all_to_all | solution.py:154
  19.7 0.0 copy-done.6
  19.7 2.5 %collective-permute-start.1 = (bf16[64,64,128]{2,1,0:T(8,128)(2,1)S(1)}, bf16[64,64,128]{2,1,0:T(8,128)(2,1)}, u32[]{:S(2)}, u32[]{:S(2)}) collective-permute-start(bf16[64,64,128]{2,1,0:T(8,128)(2,1)S(1)} %bitcast.26), channel_id=1, source_target_pairs={{0,256},{256,0},{1,257},{257,1},{2,258},{258,2},{3,259},{259,3},{4... | collective-permute-start | bytes 3145736 | tf_op jit(solution)/shard_map/ppermute | solution.py:174
  22.2 0.0 copy-done.7
  22.2 1.9 %collective-permute-start.2 = (bf16[64,64,128]{2,1,0:T(8,128)(2,1)S(1)}, bf16[64,64,128]{2,1,0:T(8,128)(2,1)}, u32[]{:S(2)}, u32[]{:S(2)}) collective-permute-start(bf16[64,64,128]{2,1,0:T(8,128)(2,1)S(1)} %bitcast.29), channel_id=1, source_target_pairs={{0,256},{256,0},{1,257},{257,1},{2,258},{258,2},{3,259},{259,3},{4... | collective-permute-start | bytes 3145736 | tf_op jit(solution)/shard_map/ppermute | solution.py:174
  24.2 0.4 collective-permute-done.1
  24.6 2.3 %collective-permute-done.2 = bf16[64,64,128]{2,1,0:T(8,128)(2,1)} collective-permute-done((bf16[64,64,128]{2,1,0:T(8,128)(2,1)S(1)}, bf16[64,64,128]{2,1,0:T(8,128)(2,1)}, u32[]{:S(2)}, u32[]{:S(2)}) %collective-permute-start.2) | collective-permute-done | bytes 1048608 | tf_op jit(solution)/shard_map/ppermute | solution.py:174
  26.9 11.6 %all-to-all-done.14 = bf16[32,3,32,128]{3,2,1,0:T(8,128)(2,1)S(1)} async-done(((bf16[32,3,32,128]{3,2,1,0:T(8,128)(2,1)}), bf16[32,3,32,128]{3,2,1,0:T(8,128)(2,1)S(1)}, u32[]{:S(2)}, u32[]{:S(2)}) %all-to-all-start.14) | async-done | bytes 786464 | tf_op jit(solution)/shard_map/all_to_all | solution.py:154
  38.5 121.0 %conditional.4 = (f32[32,128]{1,0:T(8,128)S(1)}, bf16[32,128]{1,0:T(8,128)(2,1)S(1)}) conditional(s32[]{:T(128)} %convert_element_type.73, (bf16[32,128]{1,0:T(8,128)(2,1)S(1)}, bf16[32,3,32,128]{3,2,1,0:T(8,128)(2,1)S(1)}, s32[2,128]{1,0:T(2,128)S(1)}, s32[2,128]{1,0:T(2,128)S(1)}, bf16[64,64,128]{2,1,0:T(8,128)(2,1)}, ...), branch_computations={%region_0.5_spmd, %region_5.10_spmd} | conditional | flops 6001839104 | bytes 22290536
  38.5 0.1 slice.38.refs_2_
  38.5 3.8 %branch_1_fun.5 = bf16[8,2,64,256]{3,2,1,0:T(8,128)(2,1)S(1)} custom-call(s32[2,128]{1,0:T(2,128)S(1)} %get-tuple-element.66.refs_0_.index, s32[2,128]{1,0:T(2,128)S(1)} %get-tuple-element.67.refs_1_, bf16[32,2,32,128]{3,2,1,0:T(8,128)(2,1)S(1)} %slice.38.refs_2_, bf16[64,64,128]{2,1,0:T(8,128)(2,1)S(1)} %get-tuple-element.69.refs_3_.values, ...), custom_call_target="tpu_custom_call" | custom-call | flops 2000000000 | bytes 4194304 | tf_op jit(solution)/shard_map/cond/branch_1_fun/pallas_call | solution.py:67
  42.3 18.9 %all_to_all.67 = bf16[8,2,64,256]{3,2,1,0:T(8,128)(2,1)S(1)} all-to-all(bf16[8,2,64,256]{3,2,1,0:T(8,128)(2,1)S(1)} %branch_1_fun.5), channel_id=1, replica_groups=mesh['section'=2,'row'=8,'col'=32] {'row'}, dimensions={0} | all-to-all | bytes 1048576 | tf_op jit(solution)/shard_map/cond/branch_1_fun/all_to_all | solution.py:154
  61.2 0.1 convert_reduce_fusion.5
  61.4 11.7 %all_to_all.68.hidden_ref = bf16[8,64,256]{2,1,0:T(8,128)(2,1)S(1)} all-to-all(bf16[8,64,256]{2,1,0:T(8,128)(2,1)S(1)} %broadcast_in_dim.29), channel_id=1, replica_groups=mesh['section'=2,'row'=8,'col'=32] {'row'}, dimensions={0} | all-to-all | bytes 524288 | tf_op jit(solution)/shard_map/cond/branch_1_fun/all_to_all | solution.py:154
  73.1 2.4 %branch_1_fun.6 = bf16[32,32,128]{2,1,0:T(8,128)(2,1)S(1)} custom-call(s32[2,128]{1,0:T(2,128)S(1)} %get-tuple-element.66.refs_0_.index, bf16[8,64,256]{2,1,0:T(8,128)(2,1)S(1)} %all_to_all.68.hidden_ref, bf16[64,64,128]{2,1,0:T(8,128)(2,1)S(1)} %get-tuple-element.69.refs_3_.values), custom_call_target="tpu_custom_call" | custom-call | flops 1000000000 | bytes 2097152 | tf_op jit(solution)/shard_map/cond/branch_1_fun/pallas_call | solution.py:123
  75.5 21.9 %all_to_all.69 = bf16[32,32,128]{2,1,0:T(8,128)(2,1)S(1)} all-to-all(bf16[32,32,128]{2,1,0:T(8,128)(2,1)S(1)} %branch_1_fun.6), channel_id=1, replica_groups=mesh['section'=2,'row'=8,'col'=32] {'col'}, dimensions={0} | all-to-all | bytes 524288 | tf_op jit(solution)/shard_map/cond/branch_1_fun/all_to_all | solution.py:154
  97.5 0.0 copy-start.1
  97.5 0.8 broadcast_in_dim.30
  98.2 0.0 copy-done.1
  98.2 4.5 %all-to-all-start.10 = ((bf16[32,1,32,128]{3,2,1,0:T(8,128)(2,1)}), bf16[32,1,32,128]{3,2,1,0:T(8,128)(2,1)S(1)}, u32[]{:S(2)}, u32[]{:S(2)}) async-start(bf16[32,1,32,128]{3,2,1,0:T(8,128)(2,1)} %broadcast_in_dim.30), calls=%async_computation.10 | async-start | bytes 524288 | tf_op jit(solution)/shard_map/cond/branch_1_fun/all_to_all | solution.py:154
  102.7 2.9 %branch_1_fun.7.refs_3_ = bf16[8,1,64,256]{3,2,1,0:T(8,128)(2,1)S(1)} custom-call(s32[2,128]{1,0:T(2,128)S(1)} %get-tuple-element.63.refs_0_.index, bf16[32,1,32,128]{3,2,1,0:T(8,128)(2,1)S(1)} %slice.41.refs_1_, bf16[64,64,128]{2,1,0:T(8,128)(2,1)} %get-tuple-element.72.refs_2_.values), custom_call_target="tpu_custom_call" | custom-call | flops 1000000000 | bytes 2097152 | tf_op jit(solution)/shard_map/cond/branch_1_fun/pallas_call | solution.py:67
  105.6 6.7 %all-to-all-done.10.refs_1_ = bf16[32,1,32,128]{3,2,1,0:T(8,128)(2,1)S(1)} async-done(((bf16[32,1,32,128]{3,2,1,0:T(8,128)(2,1)}), bf16[32,1,32,128]{3,2,1,0:T(8,128)(2,1)S(1)}, u32[]{:S(2)}, u32[]{:S(2)}) %all-to-all-start.10) | async-done | bytes 262176 | tf_op jit(solution)/shard_map/cond/branch_1_fun/all_to_all | solution.py:154
  112.4 2.9 %branch_1_fun.8 = bf16[8,2,64,256]{3,2,1,0:T(8,128)(2,1)S(1)} custom-call(s32[2,128]{1,0:T(2,128)S(1)} %get-tuple-element.64.refs_0_, bf16[32,1,32,128]{3,2,1,0:T(8,128)(2,1)S(1)} %all-to-all-done.10.refs_1_, bf16[64,64,128]{2,1,0:T(8,128)(2,1)} %get-tuple-element.71.refs_2_, bf16[8,1,64,256]{3,2,1,0:T(8,128)(2,1)S(1)} %branch_1_fun.7.refs_3_), custom_call_target="tpu_custom_call" | custom-call | flops 1000000000 | bytes 2097152 | tf_op jit(solution)/shard_map/cond/branch_1_fun/pallas_call | solution.py:67
  115.3 14.7 %all_to_all.70 = bf16[8,2,64,256]{3,2,1,0:T(8,128)(2,1)S(1)} all-to-all(bf16[8,2,64,256]{3,2,1,0:T(8,128)(2,1)S(1)} %branch_1_fun.8), channel_id=1, replica_groups=mesh['section'=2,'row'=8,'col'=32] {'row'}, dimensions={0} | all-to-all | bytes 1048576 | tf_op jit(solution)/shard_map/cond/branch_1_fun/all_to_all | solution.py:154
  130.0 0.1 convert_reduce_fusion.4
  130.1 11.7 %all_to_all.71.hidden_ref = bf16[8,64,256]{2,1,0:T(8,128)(2,1)S(1)} all-to-all(bf16[8,64,256]{2,1,0:T(8,128)(2,1)S(1)} %broadcast_in_dim.32), channel_id=1, replica_groups=mesh['section'=2,'row'=8,'col'=32] {'row'}, dimensions={0} | all-to-all | bytes 524288 | tf_op jit(solution)/shard_map/cond/branch_1_fun/all_to_all | solution.py:154
  141.8 3.1 %branch_1_fun.9 = bf16[32,32,128]{2,1,0:T(8,128)(2,1)S(1)} custom-call(s32[2,128]{1,0:T(2,128)S(1)} %get-tuple-element.63.refs_0_.index, bf16[8,64,256]{2,1,0:T(8,128)(2,1)S(1)} %all_to_all.71.hidden_ref, bf16[64,64,128]{2,1,0:T(8,128)(2,1)} %get-tuple-element.72.refs_2_.values), custom_call_target="tpu_custom_call" | custom-call | flops 1000000000 | bytes 2097152 | tf_op jit(solution)/shard_map/cond/branch_1_fun/pallas_call | solution.py:123
  145.0 13.8 %all_to_all.72 = bf16[32,32,128]{2,1,0:T(8,128)(2,1)S(1)} all-to-all(bf16[32,32,128]{2,1,0:T(8,128)(2,1)S(1)} %branch_1_fun.9), channel_id=1, replica_groups=mesh['section'=2,'row'=8,'col'=32] {'col'}, dimensions={0} | all-to-all | bytes 524288 | tf_op jit(solution)/shard_map/cond/branch_1_fun/all_to_all | solution.py:154
  158.8 0.0 copy-start.2
  158.8 0.6 copy-done.2
  159.5 11.1 %collective-permute-start.3 = (bf16[32,128]{1,0:T(8,128)(2,1)S(1)}, bf16[32,128]{1,0:T(8,128)(2,1)S(1)}, u32[]{:S(2)}, u32[]{:S(2)}) collective-permute-start(bf16[32,128]{1,0:T(8,128)(2,1)S(1)} %get-tuple-element.87), channel_id=1, source_target_pairs={{0,256},{256,0},{1,257},{257,1},{2,258},{258,2},{3,259},{259,3},{4... | collective-permute-start | bytes 24584 | tf_op jit(solution)/shard_map/ppermute | solution.py:174
  170.6 0.8 collective-permute-done.3
  171.4 0.6 select_n.54
  (23 shorter events, 0.4 us)
Async XLA Ops:
  0.0 10.3 %copy-start = (bf16[1,4,2048]{2,1,0:T(4,128)(2,1)S(1)}, bf16[1,4,2048]{2,1,0:T(4,128)(2,1)}, u32[]{:S(2)}) copy-start(bf16[1,4,2048]{2,1,0:T(4,128)(2,1)} %param.9) | copy-start | bytes 49156
  0.0 0.7 copy-start.3
  0.8 0.7 copy-start.4
  0.8 0.7 copy-start.5
  1.5 9.6 %collective-permute-start = (bf16[48,128]{1,0:T(8,128)(2,1)S(1)}, bf16[48,128]{1,0:T(8,128)(2,1)S(1)}, u32[]{:S(2)}, u32[]{:S(2)}) collective-permute-start(bf16[48,128]{1,0:T(8,128)(2,1)S(1)} %pad_maximum_fusion.1), channel_id=1, source_target_pairs={{0,256},{256,0},{1,257},{257,1},{2,258},{258,2},{3,259},{259,3},{4... | collective-permute-start | bytes 36872 | tf_op jit(solution)/shard_map/ppermute | solution.py:174
  11.1 8.6 %copy-start.6 = (bf16[1,1,1,64,64,128]{5,4,3,2,1,0:T(8,128)(2,1)S(1)}, bf16[1,1,1,64,64,128]{5,4,3,2,1,0:T(8,128)(2,1)}, u32[]{:S(2)}) copy-start(bf16[1,1,1,64,64,128]{5,4,3,2,1,0:T(8,128)(2,1)} %param.10) | copy-start | bytes 3145732
  11.1 11.1 %copy-start.7 = (bf16[1,1,1,64,64,128]{5,4,3,2,1,0:T(8,128)(2,1)S(1)}, bf16[1,1,1,64,64,128]{5,4,3,2,1,0:T(8,128)(2,1)}, u32[]{:S(2)}) copy-start(bf16[1,1,1,64,64,128]{5,4,3,2,1,0:T(8,128)(2,1)} %param.12) | copy-start | bytes 3145732
  12.1 26.3 %all-to-all-start.14 = ((bf16[32,3,32,128]{3,2,1,0:T(8,128)(2,1)}), bf16[32,3,32,128]{3,2,1,0:T(8,128)(2,1)S(1)}, u32[]{:S(2)}, u32[]{:S(2)}) async-start(bf16[32,3,32,128]{3,2,1,0:T(8,128)(2,1)} %broadcast_in_dim.34), calls=%async_computation.14 | async-start | bytes 1572864 | tf_op jit(solution)/shard_map/all_to_all | solution.py:154
  19.7 4.9 %collective-permute-start.1 = (bf16[64,64,128]{2,1,0:T(8,128)(2,1)S(1)}, bf16[64,64,128]{2,1,0:T(8,128)(2,1)}, u32[]{:S(2)}, u32[]{:S(2)}) collective-permute-start(bf16[64,64,128]{2,1,0:T(8,128)(2,1)S(1)} %bitcast.26), channel_id=1, source_target_pairs={{0,256},{256,0},{1,257},{257,1},{2,258},{258,2},{3,259},{259,3},{4... | collective-permute-start | bytes 3145736 | tf_op jit(solution)/shard_map/ppermute | solution.py:174
  22.2 4.7 %collective-permute-start.2 = (bf16[64,64,128]{2,1,0:T(8,128)(2,1)S(1)}, bf16[64,64,128]{2,1,0:T(8,128)(2,1)}, u32[]{:S(2)}, u32[]{:S(2)}) collective-permute-start(bf16[64,64,128]{2,1,0:T(8,128)(2,1)S(1)} %bitcast.29), channel_id=1, source_target_pairs={{0,256},{256,0},{1,257},{257,1},{2,258},{258,2},{3,259},{259,3},{4... | collective-permute-start | bytes 3145736 | tf_op jit(solution)/shard_map/ppermute | solution.py:174
  97.5 0.8 copy-start.1
  98.2 14.1 %all-to-all-start.10 = ((bf16[32,1,32,128]{3,2,1,0:T(8,128)(2,1)}), bf16[32,1,32,128]{3,2,1,0:T(8,128)(2,1)S(1)}, u32[]{:S(2)}, u32[]{:S(2)}) async-start(bf16[32,1,32,128]{3,2,1,0:T(8,128)(2,1)} %broadcast_in_dim.30), calls=%async_computation.10 | async-start | bytes 524288 | tf_op jit(solution)/shard_map/cond/branch_1_fun/all_to_all | solution.py:154
  158.8 0.7 copy-start.2
  159.5 11.9 %collective-permute-start.3 = (bf16[32,128]{1,0:T(8,128)(2,1)S(1)}, bf16[32,128]{1,0:T(8,128)(2,1)S(1)}, u32[]{:S(2)}, u32[]{:S(2)}) collective-permute-start(bf16[32,128]{1,0:T(8,128)(2,1)S(1)} %get-tuple-element.87), channel_id=1, source_target_pairs={{0,256},{256,0},{1,257},{257,1},{2,258},{258,2},{3,259},{259,3},{4... | collective-permute-start | bytes 24584 | tf_op jit(solution)/shard_map/ppermute | solution.py:174

commit v5 on v4

--- a/solution.py
+++ b/solution.py
@@ -11,18 +11,38 @@
 BLK = 64
 PER_COL = 2
 SWAP = [(0, 1), (1, 0)]
-UNROLL = 16
-SMEM = pl.BlockSpec(memory_space=pltpu.SMEM)
+UNROLL = 32
 VMEM = pl.BlockSpec(memory_space=pltpu.VMEM)
+ANY = pl.BlockSpec(memory_space=pl.ANY)
 
 
 def left_half(rows):
     return lax.broadcasted_iota(jnp.int32, (rows, LANES), 1) < BLK
 
 
+def fetches(count, index_in, values_in, index, values, sems):
+    copies = [
+        pltpu.make_async_copy(source, target.at[i], sems.at[k, i])
+        for i in range(count)
+        for k, (source, target) in enumerate([(index_in[i], index), (values_in[i], values)])
+    ]
+    for copy in copies:
+        copy.start()
+    return copies
+
+
+def fetch_scratch(count, weights):
+    return [
+        pltpu.SMEM((count,) + weights[0][0].shape, jnp.int32),
+        pltpu.VMEM((count,) + weights[0][1].shape, jnp.bfloat16),
+        pltpu.SemaphoreType.DMA((2, count)),
+    ]
+
+
 def forward_kernel(count, ahead, *refs):
-    index, x_ref, values = refs[:count], refs[count], refs[count + 1 : 2 * count + 1]
-    out_ref, rows, blocks, even, odd = refs[2 * count + 1 + ahead :]
+    index_in, x_ref, values_in = refs[:count], refs[count], refs[count + 1 : 2 * count + 1]
+    out_ref, index, values, sems, rows, blocks, even, odd = refs[2 * count + 1 + ahead :]
+    copies = fetches(count, index_in, values_in, index, values, sems)
     tokens = blocks.shape[1]
     subs = blocks.shape[0] // 2
     left = left_half(tokens)
@@ -37,17 +57,20 @@
         even[...] = jnp.zeros_like(even)
         odd[...] = jnp.zeros_like(odd)
 
+        copies[2 * i].wait()
+        copies[2 * i + 1].wait()
+
         def multiply(pair, carry):
             first, second = 2 * pair, 2 * pair + 1
-            picked = [blocks[index[i][0, n]][:, :BLK] for n in (first, second)]
+            picked = [blocks[index[i, 0, n]][:, :BLK] for n in (first, second)]
             product = jnp.dot(
-                jnp.concatenate(picked), values[i][pair], preferred_element_type=jnp.float32
+                jnp.concatenate(picked), values[i, pair], preferred_element_type=jnp.float32
             )
-            even[index[i][1, first]] += product[:tokens]
-            odd[index[i][1, second]] += product[tokens:]
+            even[index[i, 1, first]] += product[:tokens]
+            odd[index[i, 1, second]] += product[tokens:]
             return carry
 
-        lax.fori_loop(0, values[i].shape[0], multiply, 0, unroll=UNROLL)
+        lax.fori_loop(0, values.shape[1], multiply, 0, unroll=UNROLL)
         chunk = out_ref.shape[3] // LANES
         for j in range(even.shape[0] // 2):
             a, b = 2 * j, 2 * j + 1
@@ -69,9 +92,10 @@
         out_shape=jax.ShapeDtypeStruct(
             (n_row, count + ahead, tokens, ff_tile // n_row), jnp.bfloat16
         ),
-        in_specs=[SMEM] * count + [VMEM] * (1 + count + ahead),
+        in_specs=[ANY] * count + [VMEM] + [ANY] * count + [VMEM] * ahead,
         out_specs=VMEM,
-        scratch_shapes=[
+        scratch_shapes=fetch_scratch(count, weights)
+        + [
             pltpu.VMEM((n_col * per, LANES), jnp.float32),
             pltpu.VMEM((2 * subs, tokens, LANES), jnp.bfloat16),
             pltpu.VMEM((ff_tile // BLK, tokens, LANES), jnp.float32),
@@ -84,7 +108,10 @@
     )(*[w[0] for w in weights], x, *[w[1] for w in weights], *([prior] if ahead else []))
 
 
-def backward_kernel(index, hidden_ref, values, out_ref, rows, lower, upper, total):
+def backward_kernel(
+    index_in, hidden_ref, values_in, out_ref, index, values, sems, rows, lower, upper, total
+):
+    copies = fetches(1, [index_in], [values_in], index, values, sems)
     tokens = lower.shape[1]
     subs = total.shape[0] // 2
     chunk = hidden_ref.shape[2] // LANES
@@ -98,18 +125,20 @@
         lower[2 * j + 1] = jnp.where(left, turned, 0.0).astype(jnp.bfloat16)
         upper[2 * j] = jnp.where(left, 0.0, turned).astype(jnp.bfloat16)
     total[...] = jnp.zeros_like(total)
+    for copy in copies:
+        copy.wait()
 
     def multiply(pair, carry):
         first, second = 2 * pair, 2 * pair + 1
-        picked = jnp.concatenate([lower[index[1, first]], upper[index[1, second]]])
+        picked = jnp.concatenate([lower[index[0, 1, first]], upper[index[0, 1, second]]])
         product = lax.dot_general(
-            picked, values[pair], (((1,), (1,)), ((), ())), preferred_element_type=jnp.float32
+            picked, values[0, pair], (((1,), (1,)), ((), ())), preferred_element_type=jnp.float32
         )
-        total[index[0, first]] += product[:tokens]
-        total[index[0, second]] += product[tokens:]
+        total[index[0, 0, first]] += product[:tokens]
+        total[index[0, 0, second]] += product[tokens:]
         return carry
 
-    lax.fori_loop(0, values.shape[0], multiply, 0, unroll=UNROLL)
+    lax.fori_loop(0, values.shape[1], multiply, 0, unroll=UNROLL)
     for w in range(subs):
         both = jnp.concatenate([total[2 * w], total[2 * w + 1]], axis=1)
         rows[pl.ds(w, tokens, stride=subs), :] = both
@@ -123,9 +152,10 @@
     return pl.pallas_call(
         backward_kernel,
         out_shape=jax.ShapeDtypeStruct((n_col, per, LANES), jnp.bfloat16),
-        in_specs=[SMEM, VMEM, VMEM],
+        in_specs=[ANY, VMEM, ANY],
         out_specs=VMEM,
-        scratch_shapes=[
+        scratch_shapes=fetch_scratch(1, [weights])
+        + [
             pltpu.VMEM((n_col * per, LANES), jnp.float32),
             pltpu.VMEM((ff_tile // BLK, tokens, LANES), jnp.bfloat16),
             pltpu.VMEM((ff_tile // BLK, tokens, LANES), jnp.bfloat16),

time: 173 us -> 171 us (0.988)
  Pallas kernels: 15.1 us -> 12.3 us
    pallas_call x3, Pallas kernels: 9.61 us -> 7.61 us  [forward(): pl.pallas_call(functools.partial(forward_kernel, count, ahead), out_shape...]
  transfers between devices with their start and end apart: 6 -> 6, of which waited for: 6 -> 6; matrix products, arithmetic and copies ran while one was open for 0% -> 0% of each run, Pallas kernels for 2% -> 1%
where the time goes in v5:
time: 171 us; the launch traced here: 170 us
  blocking collectives  92.9 us (54%)
  starting transfers between devices  36.1 us (21%)
  waiting for transfers between devices  23.1 us (14%)
  Pallas kernels  12.3 us (7%)
  local copies, waits for them, and re-layouts  4.66 us (3%)
    all_to_all x6, blocking collectives, exchange(): return lax.all_to_all(v, axis, 0, 0)  92.9 us
    ppermute x4, starting transfers between devices, swap(): return lax.ppermute(v, 'section', SWAP)  24.1 us
    all_to_all x2, waiting for transfers between devices, exchange(): return lax.all_to_all(v, axis, 0, 0)  18.9 us
    all_to_all x2, starting transfers between devices, exchange(): return lax.all_to_all(v, axis, 0, 0)  12 us
    pallas_call x3, Pallas kernels, forward(): pl.pallas_call(functools.partial(forward_kernel, count, ahead), out_shape...  7.61 us
    pallas_call x2, Pallas kernels, backward(): pl.pallas_call(backward_kernel, out_shape=jax.ShapeDtypeStruct((n_col, pe...  4.69 us
    ppermute x4, waiting for transfers between devices, swap(): return lax.ppermute(v, 'section', SWAP)  4.27 us
  transfers between devices with their start and end apart: 6, of which 6 were waited for; matrix products, arithmetic and copies ran while one was open for 0% of the time, Pallas kernels for 1%

profile of v5, /device:TPU:1, one launch (start us, length us, event | category | flops | bytes accessed | tf_op | source)
XLA Modules:
  0.0 169.8 jit_solution(4244302182852329151)
XLA Ops:
  0.0 0.0 copy-start
  0.0 0.0 copy-start.3
  0.0 0.7 copy-done.3
  0.8 0.0 copy-start.4
  0.8 0.0 copy-start.5
  0.8 0.6 copy-done.4
  1.4 0.0 copy-done.5
  1.5 8.8 %collective-permute-start = (bf16[48,128]{1,0:T(8,128)(2,1)S(1)}, bf16[48,128]{1,0:T(8,128)(2,1)S(1)}, u32[]{:S(2)}, u32[]{:S(2)}) collective-permute-start(bf16[48,128]{1,0:T(8,128)(2,1)S(1)} %pad_maximum_fusion.1), channel_id=1, source_target_pairs={{0,256},{256,0},{1,257},{257,1},{2,258},{258,2},{3,259},{259,3},{4... | collective-permute-start | bytes 36872 | tf_op jit(solution)/shard_map/ppermute | solution.py:204
  10.3 0.0 copy-done
  10.3 0.7 collective-permute-done
  11.1 0.0 copy-start.6
  11.1 0.0 copy-start.7
  11.1 1.0 broadcast_in_dim.34
  12.1 7.5 %all-to-all-start.14 = ((bf16[32,3,32,128]{3,2,1,0:T(8,128)(2,1)}), bf16[32,3,32,128]{3,2,1,0:T(8,128)(2,1)S(1)}, u32[]{:S(2)}, u32[]{:S(2)}) async-start(bf16[32,3,32,128]{3,2,1,0:T(8,128)(2,1)} %broadcast_in_dim.34), calls=%async_computation.14 | async-start | bytes 1572864 | tf_op jit(solution)/shard_map/all_to_all | solution.py:184
  19.7 0.0 copy-done.6
  19.7 2.5 %collective-permute-start.1 = (bf16[64,64,128]{2,1,0:T(8,128)(2,1)S(1)}, bf16[64,64,128]{2,1,0:T(8,128)(2,1)}, u32[]{:S(2)}, u32[]{:S(2)}) collective-permute-start(bf16[64,64,128]{2,1,0:T(8,128)(2,1)S(1)} %bitcast.26), channel_id=1, source_target_pairs={{0,256},{256,0},{1,257},{257,1},{2,258},{258,2},{3,259},{259,3},{4... | collective-permute-start | bytes 3145736 | tf_op jit(solution)/shard_map/ppermute | solution.py:204
  22.2 0.0 copy-done.7
  22.2 1.9 %collective-permute-start.2 = (bf16[64,64,128]{2,1,0:T(8,128)(2,1)S(1)}, bf16[64,64,128]{2,1,0:T(8,128)(2,1)}, u32[]{:S(2)}, u32[]{:S(2)}) collective-permute-start(bf16[64,64,128]{2,1,0:T(8,128)(2,1)S(1)} %bitcast.29), channel_id=1, source_target_pairs={{0,256},{256,0},{1,257},{257,1},{2,258},{258,2},{3,259},{259,3},{4... | collective-permute-start | bytes 3145736 | tf_op jit(solution)/shard_map/ppermute | solution.py:204
  24.2 0.4 collective-permute-done.1
  24.6 2.3 %collective-permute-done.2 = bf16[64,64,128]{2,1,0:T(8,128)(2,1)} collective-permute-done((bf16[64,64,128]{2,1,0:T(8,128)(2,1)S(1)}, bf16[64,64,128]{2,1,0:T(8,128)(2,1)}, u32[]{:S(2)}, u32[]{:S(2)}) %collective-permute-start.2) | collective-permute-done | bytes 1048608 | tf_op jit(solution)/shard_map/ppermute | solution.py:204
  26.9 11.6 %all-to-all-done.14 = bf16[32,3,32,128]{3,2,1,0:T(8,128)(2,1)S(1)} async-done(((bf16[32,3,32,128]{3,2,1,0:T(8,128)(2,1)}), bf16[32,3,32,128]{3,2,1,0:T(8,128)(2,1)S(1)}, u32[]{:S(2)}, u32[]{:S(2)}) %all-to-all-start.14) | async-done | bytes 786464 | tf_op jit(solution)/shard_map/all_to_all | solution.py:184
  38.5 119.0 %conditional.4 = (f32[32,128]{1,0:T(8,128)S(1)}, bf16[32,128]{1,0:T(8,128)(2,1)S(1)}) conditional(s32[]{:T(128)} %convert_element_type.73, (bf16[32,128]{1,0:T(8,128)(2,1)S(1)}, bf16[32,3,32,128]{3,2,1,0:T(8,128)(2,1)S(1)}, s32[2,128]{1,0:T(2,128)S(1)}, s32[2,128]{1,0:T(2,128)S(1)}, bf16[64,64,128]{2,1,0:T(8,128)(2,1)}, ...), branch_computations={%region_0.5_spmd, %region_5.10_spmd} | conditional | flops 6001839104 | bytes 22290536
  38.5 0.1 slice.38.refs_2_
  38.5 3.0 %branch_1_fun.5 = bf16[8,2,64,256]{3,2,1,0:T(8,128)(2,1)S(1)} custom-call(s32[2,128]{1,0:T(2,128)S(1)} %get-tuple-element.66.refs_0_.index_in, s32[2,128]{1,0:T(2,128)S(1)} %get-tuple-element.67.refs_1_, bf16[32,2,32,128]{3,2,1,0:T(8,128)(2,1)S(1)} %slice.38.refs_2_, bf16[64,64,128]{2,1,0:T(8,128)(2,1)S(1)} %get-tuple-element.69.refs_3_.values_in, ...), custom_call_target="tpu_custom_call" | custom-call | flops 2000000000 | bytes 4194304 | tf_op jit(solution)/shard_map/cond/branch_1_fun/pallas_call | solution.py:90
  41.5 18.8 %all_to_all.67 = bf16[8,2,64,256]{3,2,1,0:T(8,128)(2,1)S(1)} all-to-all(bf16[8,2,64,256]{3,2,1,0:T(8,128)(2,1)S(1)} %branch_1_fun.5), channel_id=1, replica_groups=mesh['section'=2,'row'=8,'col'=32] {'row'}, dimensions={0} | all-to-all | bytes 1048576 | tf_op jit(solution)/shard_map/cond/branch_1_fun/all_to_all | solution.py:184
  60.4 0.1 convert_reduce_fusion.5
  60.5 11.4 %all_to_all.68.hidden_ref = bf16[8,64,256]{2,1,0:T(8,128)(2,1)S(1)} all-to-all(bf16[8,64,256]{2,1,0:T(8,128)(2,1)S(1)} %broadcast_in_dim.29), channel_id=1, replica_groups=mesh['section'=2,'row'=8,'col'=32] {'row'}, dimensions={0} | all-to-all | bytes 524288 | tf_op jit(solution)/shard_map/cond/branch_1_fun/all_to_all | solution.py:184
  71.9 2.0 %branch_1_fun.6 = bf16[32,32,128]{2,1,0:T(8,128)(2,1)S(1)} custom-call(s32[2,128]{1,0:T(2,128)S(1)} %get-tuple-element.66.refs_0_.index_in, bf16[8,64,256]{2,1,0:T(8,128)(2,1)S(1)} %all_to_all.68.hidden_ref, bf16[64,64,128]{2,1,0:T(8,128)(2,1)S(1)} %get-tuple-element.69.refs_3_.values_in), custom_call_target="tpu_custom_call" | custom-call | flops 1000000000 | bytes 2097152 | tf_op jit(solution)/shard_map/cond/branch_1_fun/pallas_call | solution.py:152
  74.0 22.4 %all_to_all.69 = bf16[32,32,128]{2,1,0:T(8,128)(2,1)S(1)} all-to-all(bf16[32,32,128]{2,1,0:T(8,128)(2,1)S(1)} %branch_1_fun.6), channel_id=1, replica_groups=mesh['section'=2,'row'=8,'col'=32] {'col'}, dimensions={0} | all-to-all | bytes 524288 | tf_op jit(solution)/shard_map/cond/branch_1_fun/all_to_all | solution.py:184
  96.4 0.0 copy-start.1
  96.4 0.8 broadcast_in_dim.30
  97.2 0.0 copy-done.1
  97.2 4.5 %all-to-all-start.10 = ((bf16[32,1,32,128]{3,2,1,0:T(8,128)(2,1)}), bf16[32,1,32,128]{3,2,1,0:T(8,128)(2,1)S(1)}, u32[]{:S(2)}, u32[]{:S(2)}) async-start(bf16[32,1,32,128]{3,2,1,0:T(8,128)(2,1)} %broadcast_in_dim.30), calls=%async_computation.10 | async-start | bytes 524288 | tf_op jit(solution)/shard_map/cond/branch_1_fun/all_to_all | solution.py:184
  101.7 2.3 %branch_1_fun.7.refs_3_ = bf16[8,1,64,256]{3,2,1,0:T(8,128)(2,1)S(1)} custom-call(s32[2,128]{1,0:T(2,128)S(1)} %get-tuple-element.63.refs_0_.index_in, bf16[32,1,32,128]{3,2,1,0:T(8,128)(2,1)S(1)} %slice.41.refs_1_, bf16[64,64,128]{2,1,0:T(8,128)(2,1)} %get-tuple-element.72.refs_2_.values_in), custom_call_target="tpu_custom_call" | custom-call | flops 1000000000 | bytes 2097152 | tf_op jit(solution)/shard_map/cond/branch_1_fun/pallas_call | solution.py:90
  104.0 7.3 %all-to-all-done.10.refs_1_ = bf16[32,1,32,128]{3,2,1,0:T(8,128)(2,1)S(1)} async-done(((bf16[32,1,32,128]{3,2,1,0:T(8,128)(2,1)}), bf16[32,1,32,128]{3,2,1,0:T(8,128)(2,1)S(1)}, u32[]{:S(2)}, u32[]{:S(2)}) %all-to-all-start.10) | async-done | bytes 262176 | tf_op jit(solution)/shard_map/cond/branch_1_fun/all_to_all | solution.py:184
  111.3 2.3 %branch_1_fun.8 = bf16[8,2,64,256]{3,2,1,0:T(8,128)(2,1)S(1)} custom-call(s32[2,128]{1,0:T(2,128)S(1)} %get-tuple-element.64.refs_0_, bf16[32,1,32,128]{3,2,1,0:T(8,128)(2,1)S(1)} %all-to-all-done.10.refs_1_, bf16[64,64,128]{2,1,0:T(8,128)(2,1)} %get-tuple-element.71.refs_2_, bf16[8,1,64,256]{3,2,1,0:T(8,128)(2,1)S(1)} %branch_1_fun.7.refs_3_), custom_call_target="tpu_custom_call" | custom-call | flops 1000000000 | bytes 2097152 | tf_op jit(solution)/shard_map/cond/branch_1_fun/pallas_call | solution.py:90
  113.6 14.7 %all_to_all.70 = bf16[8,2,64,256]{3,2,1,0:T(8,128)(2,1)S(1)} all-to-all(bf16[8,2,64,256]{3,2,1,0:T(8,128)(2,1)S(1)} %branch_1_fun.8), channel_id=1, replica_groups=mesh['section'=2,'row'=8,'col'=32] {'row'}, dimensions={0} | all-to-all | bytes 1048576 | tf_op jit(solution)/shard_map/cond/branch_1_fun/all_to_all | solution.py:184
  128.3 0.1 convert_reduce_fusion.4
  128.5 11.7 %all_to_all.71.hidden_ref = bf16[8,64,256]{2,1,0:T(8,128)(2,1)S(1)} all-to-all(bf16[8,64,256]{2,1,0:T(8,128)(2,1)S(1)} %broadcast_in_dim.32), channel_id=1, replica_groups=mesh['section'=2,'row'=8,'col'=32] {'row'}, dimensions={0} | all-to-all | bytes 524288 | tf_op jit(solution)/shard_map/cond/branch_1_fun/all_to_all | solution.py:184
  140.2 2.7 %branch_1_fun.9 = bf16[32,32,128]{2,1,0:T(8,128)(2,1)S(1)} custom-call(s32[2,128]{1,0:T(2,128)S(1)} %get-tuple-element.63.refs_0_.index_in, bf16[8,64,256]{2,1,0:T(8,128)(2,1)S(1)} %all_to_all.71.hidden_ref, bf16[64,64,128]{2,1,0:T(8,128)(2,1)} %get-tuple-element.72.refs_2_.values_in), custom_call_target="tpu_custom_call" | custom-call | flops 1000000000 | bytes 2097152 | tf_op jit(solution)/shard_map/cond/branch_1_fun/pallas_call | solution.py:152
  142.9 13.8 %all_to_all.72 = bf16[32,32,128]{2,1,0:T(8,128)(2,1)S(1)} all-to-all(bf16[32,32,128]{2,1,0:T(8,128)(2,1)S(1)} %branch_1_fun.9), channel_id=1, replica_groups=mesh['section'=2,'row'=8,'col'=32] {'col'}, dimensions={0} | all-to-all | bytes 524288 | tf_op jit(solution)/shard_map/cond/branch_1_fun/all_to_all | solution.py:184
  156.7 0.0 copy-start.2
  156.8 0.6 copy-done.2
  157.4 10.9 %collective-permute-start.3 = (bf16[32,128]{1,0:T(8,128)(2,1)S(1)}, bf16[32,128]{1,0:T(8,128)(2,1)S(1)}, u32[]{:S(2)}, u32[]{:S(2)}) collective-permute-start(bf16[32,128]{1,0:T(8,128)(2,1)S(1)} %get-tuple-element.87), channel_id=1, source_target_pairs={{0,256},{256,0},{1,257},{257,1},{2,258},{258,2},{3,259},{259,3},{4... | collective-permute-start | bytes 24584 | tf_op jit(solution)/shard_map/ppermute | solution.py:204
  168.3 0.8 collective-permute-done.3
  169.1 0.6 select_n.54
  (23 shorter events, 0.4 us)
Async XLA Ops:
  0.0 10.3 %copy-start = (bf16[1,4,2048]{2,1,0:T(4,128)(2,1)S(1)}, bf16[1,4,2048]{2,1,0:T(4,128)(2,1)}, u32[]{:S(2)}) copy-start(bf16[1,4,2048]{2,1,0:T(4,128)(2,1)} %param.9) | copy-start | bytes 49156
  0.0 0.7 copy-start.3
  0.8 0.7 copy-start.4
  0.8 0.7 copy-start.5
  1.5 9.6 %collective-permute-start = (bf16[48,128]{1,0:T(8,128)(2,1)S(1)}, bf16[48,128]{1,0:T(8,128)(2,1)S(1)}, u32[]{:S(2)}, u32[]{:S(2)}) collective-permute-start(bf16[48,128]{1,0:T(8,128)(2,1)S(1)} %pad_maximum_fusion.1), channel_id=1, source_target_pairs={{0,256},{256,0},{1,257},{257,1},{2,258},{258,2},{3,259},{259,3},{4... | collective-permute-start | bytes 36872 | tf_op jit(solution)/shard_map/ppermute | solution.py:204
  11.1 8.6 %copy-start.6 = (bf16[1,1,1,64,64,128]{5,4,3,2,1,0:T(8,128)(2,1)S(1)}, bf16[1,1,1,64,64,128]{5,4,3,2,1,0:T(8,128)(2,1)}, u32[]{:S(2)}) copy-start(bf16[1,1,1,64,64,128]{5,4,3,2,1,0:T(8,128)(2,1)} %param.10) | copy-start | bytes 3145732
  11.1 11.1 %copy-start.7 = (bf16[1,1,1,64,64,128]{5,4,3,2,1,0:T(8,128)(2,1)S(1)}, bf16[1,1,1,64,64,128]{5,4,3,2,1,0:T(8,128)(2,1)}, u32[]{:S(2)}) copy-start(bf16[1,1,1,64,64,128]{5,4,3,2,1,0:T(8,128)(2,1)} %param.12) | copy-start | bytes 3145732
  12.1 26.3 %all-to-all-start.14 = ((bf16[32,3,32,128]{3,2,1,0:T(8,128)(2,1)}), bf16[32,3,32,128]{3,2,1,0:T(8,128)(2,1)S(1)}, u32[]{:S(2)}, u32[]{:S(2)}) async-start(bf16[32,3,32,128]{3,2,1,0:T(8,128)(2,1)} %broadcast_in_dim.34), calls=%async_computation.14 | async-start | bytes 1572864 | tf_op jit(solution)/shard_map/all_to_all | solution.py:184
  19.7 4.9 %collective-permute-start.1 = (bf16[64,64,128]{2,1,0:T(8,128)(2,1)S(1)}, bf16[64,64,128]{2,1,0:T(8,128)(2,1)}, u32[]{:S(2)}, u32[]{:S(2)}) collective-permute-start(bf16[64,64,128]{2,1,0:T(8,128)(2,1)S(1)} %bitcast.26), channel_id=1, source_target_pairs={{0,256},{256,0},{1,257},{257,1},{2,258},{258,2},{3,259},{259,3},{4... | collective-permute-start | bytes 3145736 | tf_op jit(solution)/shard_map/ppermute | solution.py:204
  22.2 4.7 %collective-permute-start.2 = (bf16[64,64,128]{2,1,0:T(8,128)(2,1)S(1)}, bf16[64,64,128]{2,1,0:T(8,128)(2,1)}, u32[]{:S(2)}, u32[]{:S(2)}) collective-permute-start(bf16[64,64,128]{2,1,0:T(8,128)(2,1)S(1)} %bitcast.29), channel_id=1, source_target_pairs={{0,256},{256,0},{1,257},{257,1},{2,258},{258,2},{3,259},{259,3},{4... | collective-permute-start | bytes 3145736 | tf_op jit(solution)/shard_map/ppermute | solution.py:204
  96.4 0.8 copy-start.1
  97.2 14.1 %all-to-all-start.10 = ((bf16[32,1,32,128]{3,2,1,0:T(8,128)(2,1)}), bf16[32,1,32,128]{3,2,1,0:T(8,128)(2,1)S(1)}, u32[]{:S(2)}, u32[]{:S(2)}) async-start(bf16[32,1,32,128]{3,2,1,0:T(8,128)(2,1)} %broadcast_in_dim.30), calls=%async_computation.10 | async-start | bytes 524288 | tf_op jit(solution)/shard_map/cond/branch_1_fun/all_to_all | solution.py:184
  156.7 0.7 copy-start.2
  157.4 11.7 %collective-permute-start.3 = (bf16[32,128]{1,0:T(8,128)(2,1)S(1)}, bf16[32,128]{1,0:T(8,128)(2,1)S(1)}, u32[]{:S(2)}, u32[]{:S(2)}) collective-permute-start(bf16[32,128]{1,0:T(8,128)(2,1)S(1)} %get-tuple-element.87), channel_id=1, source_target_pairs={{0,256},{256,0},{1,257},{257,1},{2,258},{258,2},{3,259},{259,3},{4... | collective-permute-start | bytes 24584 | tf_op jit(solution)/shard_map/ppermute | solution.py:204

commit v6 on v5

--- a/solution.py
+++ b/solution.py
@@ -43,8 +43,8 @@
     index_in, x_ref, values_in = refs[:count], refs[count], refs[count + 1 : 2 * count + 1]
     out_ref, index, values, sems, rows, blocks, even, odd = refs[2 * count + 1 + ahead :]
     copies = fetches(count, index_in, values_in, index, values, sems)
-    tokens = blocks.shape[1]
-    subs = blocks.shape[0] // 2
+    tokens = blocks.shape[2]
+    subs = blocks.shape[1] // 2
     left = left_half(tokens)
     if ahead:
         out_ref[:, 0] = refs[2 * count + 1][:, 0]
@@ -52,8 +52,9 @@
         rows[...] = x_ref[:, i].reshape(rows.shape).astype(jnp.float32)
         for w in range(subs):
             both = rows[pl.ds(w, tokens, stride=subs), :]
-            blocks[2 * w] = both.astype(jnp.bfloat16)
-            blocks[2 * w + 1] = pltpu.roll(both, BLK, 1).astype(jnp.bfloat16)
+            blocks[i, 2 * w] = both.astype(jnp.bfloat16)
+            blocks[i, 2 * w + 1] = pltpu.roll(both, BLK, 1).astype(jnp.bfloat16)
+    for i in range(count):
         even[...] = jnp.zeros_like(even)
         odd[...] = jnp.zeros_like(odd)
 
@@ -62,7 +63,7 @@
 
         def multiply(pair, carry):
             first, second = 2 * pair, 2 * pair + 1
-            picked = [blocks[index[i, 0, n]][:, :BLK] for n in (first, second)]
+            picked = [blocks[i, index[i, 0, n]][:, :BLK] for n in (first, second)]
             product = jnp.dot(
                 jnp.concatenate(picked), values[i, pair], preferred_element_type=jnp.float32
             )
@@ -97,7 +98,7 @@
         scratch_shapes=fetch_scratch(count, weights)
         + [
             pltpu.VMEM((n_col * per, LANES), jnp.float32),
-            pltpu.VMEM((2 * subs, tokens, LANES), jnp.bfloat16),
+            pltpu.VMEM((count, 2 * subs, tokens, LANES), jnp.bfloat16),
             pltpu.VMEM((ff_tile // BLK, tokens, LANES), jnp.float32),
             pltpu.VMEM((ff_tile // BLK, tokens, LANES), jnp.float32),
         ],
@@ -108,9 +109,8 @@
     )(*[w[0] for w in weights], x, *[w[1] for w in weights], *([prior] if ahead else []))
 
 
-def backward_kernel(
-    index_in, hidden_ref, values_in, out_ref, index, values, sems, rows, lower, upper, total
-):
+def backward_kernel(index_in, hidden_ref, values_in, *refs):
+    out_ref, index, values, sems, rows, lower, upper, total = refs[-8:]
     copies = fetches(1, [index_in], [values_in], index, values, sems)
     tokens = lower.shape[1]
     subs = total.shape[0] // 2
@@ -142,17 +142,23 @@
     for w in range(subs):
         both = jnp.concatenate([total[2 * w], total[2 * w + 1]], axis=1)
         rows[pl.ds(w, tokens, stride=subs), :] = both
-    out_ref[...] = rows[...].astype(jnp.bfloat16).reshape(out_ref.shape)
-
-
-def backward(hidden_grad, weights, n_col, width):
+    n_col = out_ref.shape[0]
+    per = rows.shape[0] // n_col
+    out_ref[:, :per] = rows[...].astype(jnp.bfloat16).reshape(n_col, per, LANES)
+    if len(refs) > 8:
+        out_ref[:, per:] = jnp.broadcast_to(refs[0][...][None], (n_col,) + refs[0].shape)
+
+
+def backward(hidden_grad, weights, n_col, width, more):
     tokens = hidden_grad.shape[1]
     ff_tile = hidden_grad.shape[0] * hidden_grad.shape[2]
     per = PER_COL * width // LANES
     return pl.pallas_call(
         backward_kernel,
-        out_shape=jax.ShapeDtypeStruct((n_col, per, LANES), jnp.bfloat16),
-        in_specs=[ANY, VMEM, ANY],
+        out_shape=jax.ShapeDtypeStruct(
+            (n_col, per + sum(m.shape[0] for m in more), LANES), jnp.bfloat16
+        ),
+        in_specs=[ANY, VMEM, ANY] + [VMEM] * len(more),
         out_specs=VMEM,
         scratch_shapes=fetch_scratch(1, [weights])
         + [
@@ -163,7 +169,7 @@
         ],
         compiler_params=pltpu.CompilerParams(vmem_limit_bytes=16 * 2**20),
         cost_estimate=pl.CostEstimate(flops=10**9, bytes_accessed=2 * 2**20, transcendentals=0),
-    )(weights[0], hidden_grad, weights[1])
+    )(weights[0], hidden_grad, weights[1], *more)
 
 
 def gelu_slope(hidden):
@@ -195,10 +201,12 @@
     def add(g, part):
         return (g.astype(jnp.float32) + part).astype(jnp.bfloat16)
 
-    def col_sum(sums, w_in):
+    def scatter(sums, w_in, *more):
         hidden_grad = (sums[1] * gelu_slope(sums[0])).astype(jnp.bfloat16)
-        part = exchange(backward(gather(hidden_grad, "row"), w_in, n_col, width), "col")
-        return jnp.sum(part.astype(jnp.float32), axis=0)
+        return exchange(backward(gather(hidden_grad, "row"), w_in, n_col, width, more), "col")
+
+    def total(parts):
+        return jnp.sum(parts[:, :per].astype(jnp.float32), axis=0)
 
     def swap(v):
         return lax.ppermute(v, "section", SWAP)
@@ -215,18 +223,22 @@
     other = came[:per]
     at_oth = came[per : per + 4].astype(jnp.int32)
     g1 = shard_of(out_grad[0], PER_COL * section)
-    shards = jnp.stack([jnp.where(is_last, mine, other), g1, jnp.where(is_last, other, mine)])
+    x0 = jnp.where(is_last, other, mine)
+    shards = jnp.concatenate([jnp.where(is_last, mine, other), g1, x0[: per // 2]])
     shards, in_sent, out_sent = lax.optimization_barrier((shards, in_own, out_own))
     first = gather(shards, "col")
     in_oth, out_oth = swap(in_sent), swap(out_sent)
     own = ((in_at, in_own), (out_at, out_own))
     oth = ((at_oth[:2], in_oth), (at_oth[2:], out_oth))
 
-    def layers(w1, w0, first, g1):
-        g0 = add(g1, col_sum(row_sums(products(first[:, :2], w1)), w1[0]))
+    def layers(w1, w0, first, g1, more):
+        x1_g1 = first[:, : 2 * per].reshape(n_col, 2, per, LANES)
+        parts = scatter(row_sums(products(x1_g1, w1)), w1[0], more)
+        g0 = add(g1, total(parts))
         second = gather(g0[None], "col")
-        hidden0 = products(first[:, 2:], w0[:1])
-        return g0, col_sum(row_sums(products(second, w0[1:], hidden0)), w0[0])
+        x0_all = jnp.concatenate([first[:, 2 * per :], parts[:, per:]], axis=1)
+        hidden0 = products(x0_all[:, None], w0[:1])
+        return g0, total(scatter(row_sums(products(second, w0[1:], hidden0)), w0[0]))
 
     def later_core(own, oth, *rest):
         return layers(own, oth, *rest)
@@ -234,7 +246,7 @@
     def earlier_core(own, oth, *rest):
         return layers(oth, own, *rest)
 
-    g0, part = lax.cond(is_last, later_core, earlier_core, own, oth, first, g1)
+    g0, part = lax.cond(is_last, later_core, earlier_core, own, oth, first, g1, x0[per // 2 :])
     last = add(g0, part)
 
     kept = jnp.where(is_last, g0, last)

time: 171 us -> 169 us (0.988)
  waiting for transfers between devices: 23.1 us -> 21.1 us
    all_to_all x2, waiting for transfers between devices: 18.9 us -> 16.9 us  [exchange(): return lax.all_to_all(v, axis, 0, 0)]
where the time goes in v6:
time: 169 us; the launch traced here: 168 us
  blocking collectives  92.9 us (55%)
  starting transfers between devices  36.8 us (22%)
  waiting for transfers between devices  21.1 us (12%)
  Pallas kernels  12.3 us (7%)
  local copies, waits for them, and re-layouts  4.58 us (3%)
    all_to_all x6, blocking collectives, exchange(): return lax.all_to_all(v, axis, 0, 0)  92.9 us
    ppermute x4, starting transfers between devices, swap(): return lax.ppermute(v, 'section', SWAP)  23.8 us
    all_to_all x2, waiting for transfers between devices, exchange(): return lax.all_to_all(v, axis, 0, 0)  16.9 us
    all_to_all x2, starting transfers between devices, exchange(): return lax.all_to_all(v, axis, 0, 0)  13 us
    pallas_call x3, Pallas kernels, forward(): pl.pallas_call(functools.partial(forward_kernel, count, ahead), out_shape...  7.54 us
    pallas_call x2, Pallas kernels, backward(): pl.pallas_call(backward_kernel, out_shape=jax.ShapeDtypeStruct((n_col, pe...  4.72 us
    ppermute x4, waiting for transfers between devices, swap(): return lax.ppermute(v, 'section', SWAP)  4.26 us
  transfers between devices with their start and end apart: 6, of which 6 were waited for; matrix products, arithmetic and copies ran while one was open for 0% of the time, Pallas kernels for 1%

profile of v6, /device:TPU:1, one launch (start us, length us, event | category | flops | bytes accessed | tf_op | source)
XLA Modules:
  0.0 168.3 jit_solution(16080186366975732456)
XLA Ops:
  0.0 0.0 copy-start
  0.0 0.0 copy-start.3
  0.0 0.7 copy-done.3
  0.8 0.0 copy-start.4
  0.8 0.0 copy-start.5
  0.8 0.6 copy-done.4
  1.4 0.0 copy-done.5
  1.5 8.8 %collective-permute-start = (bf16[48,128]{1,0:T(8,128)(2,1)S(1)}, bf16[48,128]{1,0:T(8,128)(2,1)S(1)}, u32[]{:S(2)}, u32[]{:S(2)}) collective-permute-start(bf16[48,128]{1,0:T(8,128)(2,1)S(1)} %pad_maximum_fusion.1), channel_id=1, source_target_pairs={{0,256},{256,0},{1,257},{257,1},{2,258},{258,2},{3,259},{259,3},{4... | collective-permute-start | bytes 36872 | tf_op jit(solution)/shard_map/ppermute | solution.py:212
  10.3 0.0 copy-done
  10.3 0.0 copy-start.6
  10.3 0.0 copy-start.7
  10.4 0.7 collective-permute-done
  11.1 0.9 broadcast_in_dim.39
  12.0 7.5 %all-to-all-start.14 = ((bf16[32,80,128]{2,1,0:T(8,128)(2,1)}), bf16[32,80,128]{2,1,0:T(8,128)(2,1)S(1)}, u32[]{:S(2)}, u32[]{:S(2)}) async-start(bf16[32,80,128]{2,1,0:T(8,128)(2,1)} %broadcast_in_dim.39), calls=%async_computation.14 | async-start | bytes 1310720 | tf_op jit(solution)/shard_map/all_to_all | solution.py:190
  19.6 0.0 copy-done.6
  19.6 2.5 %collective-permute-start.1 = (bf16[64,64,128]{2,1,0:T(8,128)(2,1)S(1)}, bf16[64,64,128]{2,1,0:T(8,128)(2,1)}, u32[]{:S(2)}, u32[]{:S(2)}) collective-permute-start(bf16[64,64,128]{2,1,0:T(8,128)(2,1)S(1)} %bitcast.30), channel_id=1, source_target_pairs={{0,256},{256,0},{1,257},{257,1},{2,258},{258,2},{3,259},{259,3},{4... | collective-permute-start | bytes 3145736 | tf_op jit(solution)/shard_map/ppermute | solution.py:212
  22.1 0.0 copy-done.7
  22.1 1.9 %collective-permute-start.2 = (bf16[64,64,128]{2,1,0:T(8,128)(2,1)S(1)}, bf16[64,64,128]{2,1,0:T(8,128)(2,1)}, u32[]{:S(2)}, u32[]{:S(2)}) collective-permute-start(bf16[64,64,128]{2,1,0:T(8,128)(2,1)S(1)} %bitcast.33), channel_id=1, source_target_pairs={{0,256},{256,0},{1,257},{257,1},{2,258},{258,2},{3,259},{259,3},{4... | collective-permute-start | bytes 3145736 | tf_op jit(solution)/shard_map/ppermute | solution.py:212
  24.1 0.4 collective-permute-done.1
  24.5 2.3 %collective-permute-done.2 = bf16[64,64,128]{2,1,0:T(8,128)(2,1)} collective-permute-done((bf16[64,64,128]{2,1,0:T(8,128)(2,1)S(1)}, bf16[64,64,128]{2,1,0:T(8,128)(2,1)}, u32[]{:S(2)}, u32[]{:S(2)}) %collective-permute-start.2) | collective-permute-done | bytes 1048608 | tf_op jit(solution)/shard_map/ppermute | solution.py:212
  26.8 9.6 %all-to-all-done.14 = bf16[32,80,128]{2,1,0:T(8,128)(2,1)S(1)} async-done(((bf16[32,80,128]{2,1,0:T(8,128)(2,1)}), bf16[32,80,128]{2,1,0:T(8,128)(2,1)S(1)}, u32[]{:S(2)}, u32[]{:S(2)}) %all-to-all-start.14) | async-done | bytes 655392 | tf_op jit(solution)/shard_map/all_to_all | solution.py:190
  36.4 119.9 %conditional.4 = (f32[32,128]{1,0:T(8,128)S(1)}, bf16[32,128]{1,0:T(8,128)(2,1)S(1)}) conditional(s32[]{:T(128)} %convert_element_type.73, (bf16[32,128]{1,0:T(8,128)(2,1)S(1)}, bf16[32,80,128]{2,1,0:T(8,128)(2,1)S(1)}, s32[2,128]{1,0:T(2,128)S(1)}, s32[2,128]{1,0:T(2,128)S(1)}, bf16[64,64,128]{2,1,0:T(8,128)(2,1)}, ...), branch_computations={%region_0.5_spmd, %region_5.10_spmd} | conditional | flops 6002363392 | bytes 23076968
  36.4 0.1 slice.52
  36.5 2.9 %branch_1_fun.5 = bf16[8,2,64,256]{3,2,1,0:T(8,128)(2,1)S(1)} custom-call(s32[2,128]{1,0:T(2,128)S(1)} %get-tuple-element.71.refs_0_.index_in, s32[2,128]{1,0:T(2,128)S(1)} %get-tuple-element.72.refs_1_, bf16[32,2,32,128]{3,2,1,0:T(8,128)(2,1)S(1)} %bitcast.24, bf16[64,64,128]{2,1,0:T(8,128)(2,1)S(1)} %get-tuple-element.74.refs_3_.values_in, ...), custom_call_target="tpu_custom_call" | custom-call | flops 2000000000 | bytes 4194304 | tf_op jit(solution)/shard_map/cond/branch_1_fun/pallas_call | solution.py:91
  39.4 19.0 %all_to_all.67 = bf16[8,2,64,256]{3,2,1,0:T(8,128)(2,1)S(1)} all-to-all(bf16[8,2,64,256]{3,2,1,0:T(8,128)(2,1)S(1)} %branch_1_fun.5), channel_id=1, replica_groups=mesh['section'=2,'row'=8,'col'=32] {'row'}, dimensions={0} | all-to-all | bytes 1048576 | tf_op jit(solution)/shard_map/cond/branch_1_fun/all_to_all | solution.py:190
  58.4 0.1 convert_reduce_fusion.5
  58.5 11.7 %all_to_all.68.hidden_ref = bf16[8,64,256]{2,1,0:T(8,128)(2,1)S(1)} all-to-all(bf16[8,64,256]{2,1,0:T(8,128)(2,1)S(1)} %broadcast_in_dim.33), channel_id=1, replica_groups=mesh['section'=2,'row'=8,'col'=32] {'row'}, dimensions={0} | all-to-all | bytes 524288 | tf_op jit(solution)/shard_map/cond/branch_1_fun/all_to_all | solution.py:190
  70.3 2.0 %branch_1_fun.6 = bf16[32,48,128]{2,1,0:T(8,128)(2,1)S(1)} custom-call(s32[2,128]{1,0:T(2,128)S(1)} %get-tuple-element.71.refs_0_.index_in, bf16[8,64,256]{2,1,0:T(8,128)(2,1)S(1)} %all_to_all.68.hidden_ref, bf16[64,64,128]{2,1,0:T(8,128)(2,1)S(1)} %get-tuple-element.74.refs_3_.values_in, bf16[16,128]{1,0:T(8,128)(2,1)S(1)} %get-tuple-element.76.refs_0_), custom_call_target="tpu_custom_call" | custom-call | flops 1000000000 | bytes 2097152 | tf_op jit(solution)/shard_map/cond/branch_1_fun/pallas_call | solution.py:156
  72.3 21.9 %all_to_all.69 = bf16[32,48,128]{2,1,0:T(8,128)(2,1)S(1)} all-to-all(bf16[32,48,128]{2,1,0:T(8,128)(2,1)S(1)} %branch_1_fun.6), channel_id=1, replica_groups=mesh['section'=2,'row'=8,'col'=32] {'col'}, dimensions={0} | all-to-all | bytes 786432 | tf_op jit(solution)/shard_map/cond/branch_1_fun/all_to_all | solution.py:190
  94.3 0.0 copy-start.1
  94.3 0.8 broadcast_in_dim.34
  95.1 0.0 copy-done.1
  95.1 5.5 %all-to-all-start.10 = ((bf16[32,1,32,128]{3,2,1,0:T(8,128)(2,1)}), bf16[32,1,32,128]{3,2,1,0:T(8,128)(2,1)S(1)}, u32[]{:S(2)}, u32[]{:S(2)}) async-start(bf16[32,1,32,128]{3,2,1,0:T(8,128)(2,1)} %broadcast_in_dim.34), calls=%async_computation.10 | async-start | bytes 524288 | tf_op jit(solution)/shard_map/cond/branch_1_fun/all_to_all | solution.py:190
  100.6 2.3 %branch_1_fun.7.refs_3_ = bf16[8,1,64,256]{3,2,1,0:T(8,128)(2,1)S(1)} custom-call(s32[2,128]{1,0:T(2,128)S(1)} %get-tuple-element.68.refs_0_.index_in, bf16[32,1,32,128]{3,2,1,0:T(8,128)(2,1)S(1)} %maximum_bitcast_fusion.1.refs_1_, bf16[64,64,128]{2,1,0:T(8,128)(2,1)} %get-tuple-element.78.refs_2_.values_in), custom_call_target="tpu_custom_call" | custom-call | flops 1000000000 | bytes 2097152 | tf_op jit(solution)/shard_map/cond/branch_1_fun/pallas_call | solution.py:91
  102.9 7.3 %all-to-all-done.10.refs_1_ = bf16[32,1,32,128]{3,2,1,0:T(8,128)(2,1)S(1)} async-done(((bf16[32,1,32,128]{3,2,1,0:T(8,128)(2,1)}), bf16[32,1,32,128]{3,2,1,0:T(8,128)(2,1)S(1)}, u32[]{:S(2)}, u32[]{:S(2)}) %all-to-all-start.10) | async-done | bytes 262176 | tf_op jit(solution)/shard_map/cond/branch_1_fun/all_to_all | solution.py:190
  110.2 2.3 %branch_1_fun.8 = bf16[8,2,64,256]{3,2,1,0:T(8,128)(2,1)S(1)} custom-call(s32[2,128]{1,0:T(2,128)S(1)} %get-tuple-element.69.refs_0_, bf16[32,1,32,128]{3,2,1,0:T(8,128)(2,1)S(1)} %all-to-all-done.10.refs_1_, bf16[64,64,128]{2,1,0:T(8,128)(2,1)} %get-tuple-element.77.refs_2_, bf16[8,1,64,256]{3,2,1,0:T(8,128)(2,1)S(1)} %branch_1_fun.7.refs_3_), custom_call_target="tpu_custom_call" | custom-call | flops 1000000000 | bytes 2097152 | tf_op jit(solution)/shard_map/cond/branch_1_fun/pallas_call | solution.py:91
  112.5 14.7 %all_to_all.70 = bf16[8,2,64,256]{3,2,1,0:T(8,128)(2,1)S(1)} all-to-all(bf16[8,2,64,256]{3,2,1,0:T(8,128)(2,1)S(1)} %branch_1_fun.8), channel_id=1, replica_groups=mesh['section'=2,'row'=8,'col'=32] {'row'}, dimensions={0} | all-to-all | bytes 1048576 | tf_op jit(solution)/shard_map/cond/branch_1_fun/all_to_all | solution.py:190
  127.2 0.1 convert_reduce_fusion.4
  127.3 11.7 %all_to_all.71.hidden_ref = bf16[8,64,256]{2,1,0:T(8,128)(2,1)S(1)} all-to-all(bf16[8,64,256]{2,1,0:T(8,128)(2,1)S(1)} %broadcast_in_dim.37), channel_id=1, replica_groups=mesh['section'=2,'row'=8,'col'=32] {'row'}, dimensions={0} | all-to-all | bytes 524288 | tf_op jit(solution)/shard_map/cond/branch_1_fun/all_to_all | solution.py:190
  139.1 2.7 %branch_1_fun.9 = bf16[32,32,128]{2,1,0:T(8,128)(2,1)S(1)} custom-call(s32[2,128]{1,0:T(2,128)S(1)} %get-tuple-element.68.refs_0_.index_in, bf16[8,64,256]{2,1,0:T(8,128)(2,1)S(1)} %all_to_all.71.hidden_ref, bf16[64,64,128]{2,1,0:T(8,128)(2,1)} %get-tuple-element.78.refs_2_.values_in), custom_call_target="tpu_custom_call" | custom-call | flops 1000000000 | bytes 2097152 | tf_op jit(solution)/shard_map/cond/branch_1_fun/pallas_call | solution.py:156
  141.8 13.9 %all_to_all.72 = bf16[32,32,128]{2,1,0:T(8,128)(2,1)S(1)} all-to-all(bf16[32,32,128]{2,1,0:T(8,128)(2,1)S(1)} %branch_1_fun.9), channel_id=1, replica_groups=mesh['section'=2,'row'=8,'col'=32] {'col'}, dimensions={0} | all-to-all | bytes 524288 | tf_op jit(solution)/shard_map/cond/branch_1_fun/all_to_all | solution.py:190
  155.6 0.0 copy-start.2
  155.7 0.6 copy-done.2
  156.3 10.5 %collective-permute-start.3 = (bf16[32,128]{1,0:T(8,128)(2,1)S(1)}, bf16[32,128]{1,0:T(8,128)(2,1)S(1)}, u32[]{:S(2)}, u32[]{:S(2)}) collective-permute-start(bf16[32,128]{1,0:T(8,128)(2,1)S(1)} %get-tuple-element.93), channel_id=1, source_target_pairs={{0,256},{256,0},{1,257},{257,1},{2,258},{258,2},{3,259},{259,3},{4... | collective-permute-start | bytes 24584 | tf_op jit(solution)/shard_map/ppermute | solution.py:212
  166.9 0.8 collective-permute-done.3
  167.7 0.6 select_n.54
  (25 shorter events, 0.4 us)
Async XLA Ops:
  0.0 10.3 %copy-start = (bf16[1,4,2048]{2,1,0:T(4,128)(2,1)S(1)}, bf16[1,4,2048]{2,1,0:T(4,128)(2,1)}, u32[]{:S(2)}) copy-start(bf16[1,4,2048]{2,1,0:T(4,128)(2,1)} %param.9) | copy-start | bytes 49156
  0.0 0.7 copy-start.3
  0.8 0.7 copy-start.4
  0.8 0.7 copy-start.5
  1.5 9.6 %collective-permute-start = (bf16[48,128]{1,0:T(8,128)(2,1)S(1)}, bf16[48,128]{1,0:T(8,128)(2,1)S(1)}, u32[]{:S(2)}, u32[]{:S(2)}) collective-permute-start(bf16[48,128]{1,0:T(8,128)(2,1)S(1)} %pad_maximum_fusion.1), channel_id=1, source_target_pairs={{0,256},{256,0},{1,257},{257,1},{2,258},{258,2},{3,259},{259,3},{4... | collective-permute-start | bytes 36872 | tf_op jit(solution)/shard_map/ppermute | solution.py:212
  10.3 9.2 %copy-start.6 = (bf16[1,1,1,64,64,128]{5,4,3,2,1,0:T(8,128)(2,1)S(1)}, bf16[1,1,1,64,64,128]{5,4,3,2,1,0:T(8,128)(2,1)}, u32[]{:S(2)}) copy-start(bf16[1,1,1,64,64,128]{5,4,3,2,1,0:T(8,128)(2,1)} %param.10) | copy-start | bytes 3145732
  10.3 11.8 %copy-start.7 = (bf16[1,1,1,64,64,128]{5,4,3,2,1,0:T(8,128)(2,1)S(1)}, bf16[1,1,1,64,64,128]{5,4,3,2,1,0:T(8,128)(2,1)}, u32[]{:S(2)}) copy-start(bf16[1,1,1,64,64,128]{5,4,3,2,1,0:T(8,128)(2,1)} %param.12) | copy-start | bytes 3145732
  12.0 24.3 %all-to-all-start.14 = ((bf16[32,80,128]{2,1,0:T(8,128)(2,1)}), bf16[32,80,128]{2,1,0:T(8,128)(2,1)S(1)}, u32[]{:S(2)}, u32[]{:S(2)}) async-start(bf16[32,80,128]{2,1,0:T(8,128)(2,1)} %broadcast_in_dim.39), calls=%async_computation.14 | async-start | bytes 1310720 | tf_op jit(solution)/shard_map/all_to_all | solution.py:190
  19.6 4.9 %collective-permute-start.1 = (bf16[64,64,128]{2,1,0:T(8,128)(2,1)S(1)}, bf16[64,64,128]{2,1,0:T(8,128)(2,1)}, u32[]{:S(2)}, u32[]{:S(2)}) collective-permute-start(bf16[64,64,128]{2,1,0:T(8,128)(2,1)S(1)} %bitcast.30), channel_id=1, source_target_pairs={{0,256},{256,0},{1,257},{257,1},{2,258},{258,2},{3,259},{259,3},{4... | collective-permute-start | bytes 3145736 | tf_op jit(solution)/shard_map/ppermute | solution.py:212
  22.1 4.7 %collective-permute-start.2 = (bf16[64,64,128]{2,1,0:T(8,128)(2,1)S(1)}, bf16[64,64,128]{2,1,0:T(8,128)(2,1)}, u32[]{:S(2)}, u32[]{:S(2)}) collective-permute-start(bf16[64,64,128]{2,1,0:T(8,128)(2,1)S(1)} %bitcast.33), channel_id=1, source_target_pairs={{0,256},{256,0},{1,257},{257,1},{2,258},{258,2},{3,259},{259,3},{4... | collective-permute-start | bytes 3145736 | tf_op jit(solution)/shard_map/ppermute | solution.py:212
  94.3 0.8 copy-start.1
  95.1 15.1 %all-to-all-start.10 = ((bf16[32,1,32,128]{3,2,1,0:T(8,128)(2,1)}), bf16[32,1,32,128]{3,2,1,0:T(8,128)(2,1)S(1)}, u32[]{:S(2)}, u32[]{:S(2)}) async-start(bf16[32,1,32,128]{3,2,1,0:T(8,128)(2,1)} %broadcast_in_dim.34), calls=%async_computation.10 | async-start | bytes 524288 | tf_op jit(solution)/shard_map/cond/branch_1_fun/all_to_all | solution.py:190
  155.6 0.7 copy-start.2
  156.3 11.4 %collective-permute-start.3 = (bf16[32,128]{1,0:T(8,128)(2,1)S(1)}, bf16[32,128]{1,0:T(8,128)(2,1)S(1)}, u32[]{:S(2)}, u32[]{:S(2)}) collective-permute-start(bf16[32,128]{1,0:T(8,128)(2,1)S(1)} %get-tuple-element.93), channel_id=1, source_target_pairs={{0,256},{256,0},{1,257},{257,1},{2,258},{258,2},{3,259},{259,3},{4... | collective-permute-start | bytes 24584 | tf_op jit(solution)/shard_map/ppermute | solution.py:212

commit v7 on v6

--- a/solution.py
+++ b/solution.py
@@ -224,29 +224,28 @@
     at_oth = came[per : per + 4].astype(jnp.int32)
     g1 = shard_of(out_grad[0], PER_COL * section)
     x0 = jnp.where(is_last, other, mine)
-    shards = jnp.concatenate([jnp.where(is_last, mine, other), g1, x0[: per // 2]])
+    shards = jnp.stack([jnp.where(is_last, mine, other), g1])
     shards, in_sent, out_sent = lax.optimization_barrier((shards, in_own, out_own))
     first = gather(shards, "col")
     in_oth, out_oth = swap(in_sent), swap(out_sent)
     own = ((in_at, in_own), (out_at, out_own))
     oth = ((at_oth[:2], in_oth), (at_oth[2:], out_oth))
 
-    def layers(w1, w0, first, g1, more):
-        x1_g1 = first[:, : 2 * per].reshape(n_col, 2, per, LANES)
-        parts = scatter(row_sums(products(x1_g1, w1)), w1[0], more)
+    def later_core(own, oth, first, g1, x0):
+        w1, w0 = own, oth
+        g0 = add(g1, total(scatter(row_sums(products(first, w1)), w1[0])))
+        second = gather(jnp.stack([x0, g0]), "col")
+        return g0, total(scatter(row_sums(products(second, w0)), w0[0]))
+
+    def earlier_core(own, oth, first, g1, x0):
+        w1, w0 = oth, own
+        parts = scatter(row_sums(products(first, w1)), w1[0], x0)
         g0 = add(g1, total(parts))
         second = gather(g0[None], "col")
-        x0_all = jnp.concatenate([first[:, 2 * per :], parts[:, per:]], axis=1)
-        hidden0 = products(x0_all[:, None], w0[:1])
+        hidden0 = products(parts[:, None, per:], w0[:1])
         return g0, total(scatter(row_sums(products(second, w0[1:], hidden0)), w0[0]))
 
-    def later_core(own, oth, *rest):
-        return layers(own, oth, *rest)
-
-    def earlier_core(own, oth, *rest):
-        return layers(oth, own, *rest)
-
-    g0, part = lax.cond(is_last, later_core, earlier_core, own, oth, first, g1, x0[per // 2 :])
+    g0, part = lax.cond(is_last, later_core, earlier_core, own, oth, first, g1, x0)
     last = add(g0, part)
 
     kept = jnp.where(is_last, g0, last)

time: 169 us -> 172 us (1.018)
  blocking collectives: 92.9 us -> 110 us
  starting transfers between devices: 36.8 us -> 30.7 us
  waiting for transfers between devices: 21.1 us -> 15.6 us
  Pallas kernels: 12.3 us -> 9.71 us
    all_to_all x6 -> x7, blocking collectives: 92.9 us -> 110 us  [exchange(): return lax.all_to_all(v, axis, 0, 0)]
    all_to_all x2 -> x1, starting transfers between devices: 13 us -> 7.51 us  [exchange(): return lax.all_to_all(v, axis, 0, 0)]
    all_to_all x2 -> x1, waiting for transfers between devices: 16.9 us -> 14 us  [exchange(): return lax.all_to_all(v, axis, 0, 0)]
    ppermute x4, waiting for transfers between devices: 4.26 us -> 1.55 us  [swap(): return lax.ppermute(v, 'section', SWAP)]
    pallas_call x3 -> x2, Pallas kernels: 7.54 us -> 5.68 us  [forward(): pl.pallas_call(functools.partial(forward_kernel, count, ahead), out_shape...]
  transfers between devices with their start and end apart: 6 -> 5, of which waited for: 6 -> 3; matrix products, arithmetic and copies ran while one was open for 0% -> 1% of each run, Pallas kernels for 1% -> 0%
where the time goes in v7:
time: 172 us; the launch traced here: 171 us
  blocking collectives  110 us (64%)
  starting transfers between devices  30.7 us (18%)
  waiting for transfers between devices  15.6 us (9%)
  Pallas kernels  9.71 us (6%)
  local copies, waits for them, and re-layouts  4.42 us (3%)
    all_to_all x7, blocking collectives, exchange(): return lax.all_to_all(v, axis, 0, 0)  110 us
    ppermute x4, starting transfers between devices, swap(): return lax.ppermute(v, 'section', SWAP)  23.2 us
    all_to_all x1, waiting for transfers between devices, exchange(): return lax.all_to_all(v, axis, 0, 0)  14 us
    all_to_all x1, starting transfers between devices, exchange(): return lax.all_to_all(v, axis, 0, 0)  7.51 us
    pallas_call x2, Pallas kernels, forward(): pl.pallas_call(functools.partial(forward_kernel, count, ahead), out_shape...  5.68 us
    pallas_call x2, Pallas kernels, backward(): pl.pallas_call(backward_kernel, out_shape=jax.ShapeDtypeStruct((n_col, pe...  4.02 us
  transfers between devices with their start and end apart: 5, of which 3 were waited for; matrix products, arithmetic and copies ran while one was open for 1% of the time, Pallas kernels for 0%

profile of v7, /device:TPU:1, one launch (start us, length us, event | category | flops | bytes accessed | tf_op | source)
XLA Modules:
  0.0 170.9 jit_solution(6705567791086289398)
XLA Ops:
  0.0 0.0 copy-start
  0.0 0.0 copy-start.3
  0.0 0.7 copy-done.3
  0.8 0.0 copy-start.4
  0.8 0.0 copy-start.5
  0.8 0.0 copy-start.6
  0.8 0.6 copy-done.4
  1.4 0.0 copy-done.5
  1.5 8.8 %collective-permute-start = (bf16[48,128]{1,0:T(8,128)(2,1)S(1)}, bf16[48,128]{1,0:T(8,128)(2,1)S(1)}, u32[]{:S(2)}, u32[]{:S(2)}) collective-permute-start(bf16[48,128]{1,0:T(8,128)(2,1)S(1)} %pad_maximum_fusion.2), channel_id=1, source_target_pairs={{0,256},{256,0},{1,257},{257,1},{2,258},{258,2},{3,259},{259,3},{4... | collective-permute-start | bytes 36872 | tf_op jit(solution)/shard_map/ppermute | solution.py:212
  10.3 0.0 copy-done
  10.3 0.7 collective-permute-done
  11.1 2.3 %collective-permute-start.1 = (bf16[64,64,128]{2,1,0:T(8,128)(2,1)}, bf16[64,64,128]{2,1,0:T(8,128)(2,1)S(1)}, u32[]{:S(2)}, u32[]{:S(2)}) collective-permute-start(bf16[64,64,128]{2,1,0:T(8,128)(2,1)} %bitcast.30), channel_id=1, source_target_pairs={{0,256},{256,0},{1,257},{257,1},{2,258},{258,2},{3,259},{259,3},{4... | collective-permute-start | bytes 3145736 | tf_op jit(solution)/shard_map/ppermute | solution.py:212
  13.4 2.1 %collective-permute-start.2 = (bf16[64,64,128]{2,1,0:T(8,128)(2,1)}, bf16[64,64,128]{2,1,0:T(8,128)(2,1)}, u32[]{:S(2)}, u32[]{:S(2)}) collective-permute-start(bf16[64,64,128]{2,1,0:T(8,128)(2,1)} %bitcast.33), channel_id=1, source_target_pairs={{0,256},{256,0},{1,257},{257,1},{2,258},{258,2},{3,259},{259,3},{4... | collective-permute-start | bytes 3145736 | tf_op jit(solution)/shard_map/ppermute | solution.py:212
  15.5 0.9 broadcast_in_dim.37
  16.4 7.5 %all-to-all-start.14 = ((bf16[32,2,32,128]{3,2,1,0:T(8,128)(2,1)}), bf16[32,2,32,128]{3,2,1,0:T(8,128)(2,1)S(1)}, u32[]{:S(2)}, u32[]{:S(2)}) async-start(bf16[32,2,32,128]{3,2,1,0:T(8,128)(2,1)} %broadcast_in_dim.37), calls=%async_computation.14 | async-start | bytes 1048576 | tf_op jit(solution)/shard_map/all_to_all | solution.py:190
  23.9 14.0 %all-to-all-done.14 = bf16[32,2,32,128]{3,2,1,0:T(8,128)(2,1)S(1)} async-done(((bf16[32,2,32,128]{3,2,1,0:T(8,128)(2,1)}), bf16[32,2,32,128]{3,2,1,0:T(8,128)(2,1)S(1)}, u32[]{:S(2)}, u32[]{:S(2)}) %all-to-all-start.14) | async-done | bytes 524320 | tf_op jit(solution)/shard_map/all_to_all | solution.py:190
  38.0 0.0 collective-permute-done.1
  38.0 0.0 collective-permute-done.2
  38.0 0.0 copy-done.6
  38.0 121.3 %conditional.4 = (f32[32,128]{1,0:T(8,128)S(1)}, bf16[32,128]{1,0:T(8,128)(2,1)S(1)}) conditional(s32[]{:T(128)} %convert_element_type.73, (bf16[32,128]{1,0:T(8,128)(2,1)S(1)}, s32[2,128]{1,0:T(2,128)S(1)}, s32[2,128]{1,0:T(2,128)S(1)}, bf16[32,2,32,128]{3,2,1,0:T(8,128)(2,1)S(1)}, bf16[64,64,128]{2,1,0:T(8,128)(2,1)S(1)}, ...), branch_computations={%region_0.5_spmd, %region_5.10_spmd} | conditional | flops 6001847296 | bytes 25894988
  38.0 2.8 %branch_1_fun.4 = bf16[8,2,64,256]{3,2,1,0:T(8,128)(2,1)S(1)} custom-call(s32[2,128]{1,0:T(2,128)S(1)} %get-tuple-element.72.refs_0_.index_in, s32[2,128]{1,0:T(2,128)S(1)} %get-tuple-element.73.refs_1_, bf16[32,2,32,128]{3,2,1,0:T(8,128)(2,1)S(1)} %get-tuple-element.74.refs_2_, bf16[64,64,128]{2,1,0:T(8,128)(2,1)S(1)} %get-tuple-element.75.refs_3_.values_in, ...), custom_call_target="tpu_custom_call" | custom-call | flops 2000000000 | bytes 4194304 | tf_op jit(solution)/shard_map/cond/branch_1_fun/pallas_call | solution.py:91
  40.9 19.6 %all_to_all.67 = bf16[8,2,64,256]{3,2,1,0:T(8,128)(2,1)S(1)} all-to-all(bf16[8,2,64,256]{3,2,1,0:T(8,128)(2,1)S(1)} %branch_1_fun.4), channel_id=1, replica_groups=mesh['section'=2,'row'=8,'col'=32] {'row'}, dimensions={0} | all-to-all | bytes 1048576 | tf_op jit(solution)/shard_map/cond/branch_1_fun/all_to_all | solution.py:190
  60.5 0.1 convert_reduce_fusion.5
  60.6 13.0 %all_to_all.68.hidden_ref = bf16[8,64,256]{2,1,0:T(8,128)(2,1)S(1)} all-to-all(bf16[8,64,256]{2,1,0:T(8,128)(2,1)S(1)} %broadcast_in_dim.32), channel_id=1, replica_groups=mesh['section'=2,'row'=8,'col'=32] {'row'}, dimensions={0} | all-to-all | bytes 524288 | tf_op jit(solution)/shard_map/cond/branch_1_fun/all_to_all | solution.py:190
  73.6 2.0 %branch_1_fun.5 = bf16[32,32,128]{2,1,0:T(8,128)(2,1)S(1)} custom-call(s32[2,128]{1,0:T(2,128)S(1)} %get-tuple-element.72.refs_0_.index_in, bf16[8,64,256]{2,1,0:T(8,128)(2,1)S(1)} %all_to_all.68.hidden_ref, bf16[64,64,128]{2,1,0:T(8,128)(2,1)S(1)} %get-tuple-element.75.refs_3_.values_in), custom_call_target="tpu_custom_call" | custom-call | flops 1000000000 | bytes 2097152 | tf_op jit(solution)/shard_map/cond/branch_1_fun/pallas_call | solution.py:156
  75.7 19.7 %all_to_all.69 = bf16[32,32,128]{2,1,0:T(8,128)(2,1)S(1)} all-to-all(bf16[32,32,128]{2,1,0:T(8,128)(2,1)S(1)} %branch_1_fun.5), channel_id=1, replica_groups=mesh['section'=2,'row'=8,'col'=32] {'col'}, dimensions={0} | all-to-all | bytes 524288 | tf_op jit(solution)/shard_map/cond/branch_1_fun/all_to_all | solution.py:190
  95.4 0.0 copy-start.1
  95.4 0.6 copy-done.1
  96.0 0.1 broadcast_in_dim.33
  96.1 15.9 %all_to_all.70.refs_2_ = bf16[32,2,32,128]{3,2,1,0:T(8,128)(2,1)S(1)} all-to-all(bf16[32,2,32,128]{3,2,1,0:T(8,128)(2,1)S(1)} %broadcast_in_dim.33), channel_id=1, replica_groups=mesh['section'=2,'row'=8,'col'=32] {'col'}, dimensions={0} | all-to-all | bytes 1048576 | tf_op jit(solution)/shard_map/cond/branch_1_fun/all_to_all | solution.py:190
  111.9 2.8 %branch_1_fun.6 = bf16[8,2,64,256]{3,2,1,0:T(8,128)(2,1)S(1)} custom-call(s32[2,128]{1,0:T(2,128)S(1)} %get-tuple-element.68.refs_0_.index_in, s32[2,128]{1,0:T(2,128)S(1)} %get-tuple-element.69.refs_1_, bf16[32,2,32,128]{3,2,1,0:T(8,128)(2,1)S(1)} %all_to_all.70.refs_2_, bf16[64,64,128]{2,1,0:T(8,128)(2,1)S(1)} %get-tuple-element.77.refs_3_.values_in, ...), custom_call_target="tpu_custom_call" | custom-call | flops 2000000000 | bytes 4194304 | tf_op jit(solution)/shard_map/cond/branch_1_fun/pallas_call | solution.py:91
  114.8 14.7 %all_to_all.71 = bf16[8,2,64,256]{3,2,1,0:T(8,128)(2,1)S(1)} all-to-all(bf16[8,2,64,256]{3,2,1,0:T(8,128)(2,1)S(1)} %branch_1_fun.6), channel_id=1, replica_groups=mesh['section'=2,'row'=8,'col'=32] {'row'}, dimensions={0} | all-to-all | bytes 1048576 | tf_op jit(solution)/shard_map/cond/branch_1_fun/all_to_all | solution.py:190
  129.4 0.1 convert_reduce_fusion.4
  129.6 11.7 %all_to_all.72.hidden_ref = bf16[8,64,256]{2,1,0:T(8,128)(2,1)S(1)} all-to-all(bf16[8,64,256]{2,1,0:T(8,128)(2,1)S(1)} %broadcast_in_dim.35), channel_id=1, replica_groups=mesh['section'=2,'row'=8,'col'=32] {'row'}, dimensions={0} | all-to-all | bytes 524288 | tf_op jit(solution)/shard_map/cond/branch_1_fun/all_to_all | solution.py:190
  141.3 2.0 %branch_1_fun.7 = bf16[32,32,128]{2,1,0:T(8,128)(2,1)S(1)} custom-call(s32[2,128]{1,0:T(2,128)S(1)} %get-tuple-element.68.refs_0_.index_in, bf16[8,64,256]{2,1,0:T(8,128)(2,1)S(1)} %all_to_all.72.hidden_ref, bf16[64,64,128]{2,1,0:T(8,128)(2,1)S(1)} %get-tuple-element.77.refs_3_.values_in), custom_call_target="tpu_custom_call" | custom-call | flops 1000000000 | bytes 2097152 | tf_op jit(solution)/shard_map/cond/branch_1_fun/pallas_call | solution.py:156
  143.3 15.3 %all_to_all.73 = bf16[32,32,128]{2,1,0:T(8,128)(2,1)S(1)} all-to-all(bf16[32,32,128]{2,1,0:T(8,128)(2,1)S(1)} %branch_1_fun.7), channel_id=1, replica_groups=mesh['section'=2,'row'=8,'col'=32] {'col'}, dimensions={0} | all-to-all | bytes 524288 | tf_op jit(solution)/shard_map/cond/branch_1_fun/all_to_all | solution.py:190
  158.6 0.0 copy-start.2
  158.7 0.6 copy-done.2
  159.3 10.1 %collective-permute-start.3 = (bf16[32,128]{1,0:T(8,128)(2,1)S(1)}, bf16[32,128]{1,0:T(8,128)(2,1)S(1)}, u32[]{:S(2)}, u32[]{:S(2)}) collective-permute-start(bf16[32,128]{1,0:T(8,128)(2,1)S(1)} %get-tuple-element.93), channel_id=1, source_target_pairs={{0,256},{256,0},{1,257},{257,1},{2,258},{258,2},{3,259},{259,3},{4... | collective-permute-start | bytes 24584 | tf_op jit(solution)/shard_map/ppermute | solution.py:212
  169.4 0.8 collective-permute-done.3
  170.2 0.6 select_n.54
  (23 shorter events, 0.4 us)
Async XLA Ops:
  0.0 10.3 %copy-start = (bf16[1,4,2048]{2,1,0:T(4,128)(2,1)S(1)}, bf16[1,4,2048]{2,1,0:T(4,128)(2,1)}, u32[]{:S(2)}) copy-start(bf16[1,4,2048]{2,1,0:T(4,128)(2,1)} %param.9) | copy-start | bytes 49156
  0.0 0.7 copy-start.3
  0.8 0.7 copy-start.4
  0.8 0.7 copy-start.5
  0.8 37.2 %copy-start.6 = (bf16[1,1,1,64,64,128]{5,4,3,2,1,0:T(8,128)(2,1)S(1)}, bf16[1,1,1,64,64,128]{5,4,3,2,1,0:T(8,128)(2,1)}, u32[]{:S(2)}) copy-start(bf16[1,1,1,64,64,128]{5,4,3,2,1,0:T(8,128)(2,1)} %param.10) | copy-start | bytes 3145732
  1.5 9.6 %collective-permute-start = (bf16[48,128]{1,0:T(8,128)(2,1)S(1)}, bf16[48,128]{1,0:T(8,128)(2,1)S(1)}, u32[]{:S(2)}, u32[]{:S(2)}) collective-permute-start(bf16[48,128]{1,0:T(8,128)(2,1)S(1)} %pad_maximum_fusion.2), channel_id=1, source_target_pairs={{0,256},{256,0},{1,257},{257,1},{2,258},{258,2},{3,259},{259,3},{4... | collective-permute-start | bytes 36872 | tf_op jit(solution)/shard_map/ppermute | solution.py:212
  11.1 26.9 %collective-permute-start.1 = (bf16[64,64,128]{2,1,0:T(8,128)(2,1)}, bf16[64,64,128]{2,1,0:T(8,128)(2,1)S(1)}, u32[]{:S(2)}, u32[]{:S(2)}) collective-permute-start(bf16[64,64,128]{2,1,0:T(8,128)(2,1)} %bitcast.30), channel_id=1, source_target_pairs={{0,256},{256,0},{1,257},{257,1},{2,258},{258,2},{3,259},{259,3},{4... | collective-permute-start | bytes 3145736 | tf_op jit(solution)/shard_map/ppermute | solution.py:212
  13.4 24.6 %collective-permute-start.2 = (bf16[64,64,128]{2,1,0:T(8,128)(2,1)}, bf16[64,64,128]{2,1,0:T(8,128)(2,1)}, u32[]{:S(2)}, u32[]{:S(2)}) collective-permute-start(bf16[64,64,128]{2,1,0:T(8,128)(2,1)} %bitcast.33), channel_id=1, source_target_pairs={{0,256},{256,0},{1,257},{257,1},{2,258},{258,2},{3,259},{259,3},{4... | collective-permute-start | bytes 3145736 | tf_op jit(solution)/shard_map/ppermute | solution.py:212
  16.4 21.6 %all-to-all-start.14 = ((bf16[32,2,32,128]{3,2,1,0:T(8,128)(2,1)}), bf16[32,2,32,128]{3,2,1,0:T(8,128)(2,1)S(1)}, u32[]{:S(2)}, u32[]{:S(2)}) async-start(bf16[32,2,32,128]{3,2,1,0:T(8,128)(2,1)} %broadcast_in_dim.37), calls=%async_computation.14 | async-start | bytes 1048576 | tf_op jit(solution)/shard_map/all_to_all | solution.py:190
  95.4 0.6 copy-start.1
  158.6 0.7 copy-start.2
  159.3 10.9 %collective-permute-start.3 = (bf16[32,128]{1,0:T(8,128)(2,1)S(1)}, bf16[32,128]{1,0:T(8,128)(2,1)S(1)}, u32[]{:S(2)}, u32[]{:S(2)}) collective-permute-start(bf16[32,128]{1,0:T(8,128)(2,1)S(1)} %get-tuple-element.93), channel_id=1, source_target_pairs={{0,256},{256,0},{1,257},{257,1},{2,258},{258,2},{3,259},{259,3},{4... | collective-permute-start | bytes 24584 | tf_op jit(solution)/shard_map/ppermute | solution.py:212

commit v8 on v6

--- a/solution.py
+++ b/solution.py
@@ -231,20 +231,25 @@
     own = ((in_at, in_own), (out_at, out_own))
     oth = ((at_oth[:2], in_oth), (at_oth[2:], out_oth))
 
-    def layers(w1, w0, first, g1, more):
-        x1_g1 = first[:, : 2 * per].reshape(n_col, 2, per, LANES)
-        parts = scatter(row_sums(products(x1_g1, w1)), w1[0], more)
+    def both_of(first):
+        return first[:, : 2 * per].reshape(n_col, 2, per, LANES)
+
+    def later_core(own, oth, first, g1, more):
+        w1, w0 = own, oth
+        g0 = add(g1, total(scatter(row_sums(products(both_of(first), w1)), w1[0])))
+        second = gather(jnp.concatenate([g0, more]), "col")
+        x0_all = jnp.concatenate([first[:, 2 * per :], second[:, per:]], axis=1)
+        x0_g0 = jnp.stack([x0_all, second[:, :per]], axis=1)
+        return g0, total(scatter(row_sums(products(x0_g0, w0)), w0[0]))
+
+    def earlier_core(own, oth, first, g1, more):
+        w1, w0 = oth, own
+        parts = scatter(row_sums(products(both_of(first), w1)), w1[0], more)
         g0 = add(g1, total(parts))
         second = gather(g0[None], "col")
         x0_all = jnp.concatenate([first[:, 2 * per :], parts[:, per:]], axis=1)
         hidden0 = products(x0_all[:, None], w0[:1])
         return g0, total(scatter(row_sums(products(second, w0[1:], hidden0)), w0[0]))
-
-    def later_core(own, oth, *rest):
-        return layers(own, oth, *rest)
-
-    def earlier_core(own, oth, *rest):
-        return layers(oth, own, *rest)
 
     g0, part = lax.cond(is_last, later_core, earlier_core, own, oth, first, g1, x0[per // 2 :])
     last = add(g0, part)

time: 169 us -> 170 us (level)
  starting transfers between devices: 36.8 us -> 33.2 us
  waiting for transfers between devices: 21.1 us -> 24.1 us
  blocking collectives: 92.9 us -> 94.7 us
    all_to_all x2, waiting for transfers between devices: 16.9 us -> 19.8 us  [exchange(): return lax.all_to_all(v, axis, 0, 0)]
    ppermute x4, starting transfers between devices: 23.8 us -> 21.3 us  [swap(): return lax.ppermute(v, 'section', SWAP)]
    all_to_all x6, blocking collectives: 92.9 us -> 94.7 us  [exchange(): return lax.all_to_all(v, axis, 0, 0)]
    pallas_call x3 -> x2, Pallas kernels: 7.54 us -> 6.4 us  [forward(): pl.pallas_call(functools.partial(forward_kernel, count, ahead), out_shape...]
  transfers between devices with their start and end apart: 6 -> 6, of which waited for: 6 -> 6; matrix products, arithmetic and copies ran while one was open for 0% -> 0% of each run, Pallas kernels for 1% -> 0%
where the time goes in v8:
time: 170 us; the launch traced here: 169 us
  blocking collectives  94.7 us (56%)
  starting transfers between devices  33.2 us (20%)
  waiting for transfers between devices  24.1 us (14%)
  Pallas kernels  11.1 us (7%)
  local copies, waits for them, and re-layouts  5.2 us (3%)
    all_to_all x6, blocking collectives, exchange(): return lax.all_to_all(v, axis, 0, 0)  94.7 us
    ppermute x4, starting transfers between devices, swap(): return lax.ppermute(v, 'section', SWAP)  21.3 us
    all_to_all x2, waiting for transfers between devices, exchange(): return lax.all_to_all(v, axis, 0, 0)  19.8 us
    all_to_all x2, starting transfers between devices, exchange(): return lax.all_to_all(v, axis, 0, 0)  12 us
    pallas_call x2, Pallas kernels, forward(): pl.pallas_call(functools.partial(forward_kernel, count, ahead), out_shape...  6.4 us
    pallas_call x2, Pallas kernels, backward(): pl.pallas_call(backward_kernel, out_shape=jax.ShapeDtypeStruct((n_col, pe...  4.7 us
    ppermute x4, waiting for transfers between devices, swap(): return lax.ppermute(v, 'section', SWAP)  4.26 us
  transfers between devices with their start and end apart: 6, of which 6 were waited for; matrix products, arithmetic and copies ran while one was open for 0% of the time, Pallas kernels for 0%

profile of v8, /device:TPU:1, one launch (start us, length us, event | category | flops | bytes accessed | tf_op | source)
XLA Modules:
  0.0 169.1 jit_solution(14984830961222275108)
XLA Ops:
  0.0 0.0 copy-start
  0.0 0.0 copy-start.3
  0.0 0.7 copy-done.3
  0.8 0.0 copy-start.4
  0.8 0.0 copy-start.5
  0.8 0.6 copy-done.4
  1.4 0.0 copy-done.5
  1.5 8.8 %collective-permute-start = (bf16[48,128]{1,0:T(8,128)(2,1)S(1)}, bf16[48,128]{1,0:T(8,128)(2,1)S(1)}, u32[]{:S(2)}, u32[]{:S(2)}) collective-permute-start(bf16[48,128]{1,0:T(8,128)(2,1)S(1)} %pad_maximum_fusion.3), channel_id=1, source_target_pairs={{0,256},{256,0},{1,257},{257,1},{2,258},{258,2},{3,259},{259,3},{4... | collective-permute-start | bytes 36872 | tf_op jit(solution)/shard_map/ppermute | solution.py:212
  10.3 0.0 copy-done
  10.3 0.0 copy-start.6
  10.3 0.0 copy-start.7
  10.4 0.7 collective-permute-done
  11.1 0.9 broadcast_in_dim.37
  12.1 7.5 %all-to-all-start.14 = ((bf16[32,80,128]{2,1,0:T(8,128)(2,1)}), bf16[32,80,128]{2,1,0:T(8,128)(2,1)S(1)}, u32[]{:S(2)}, u32[]{:S(2)}) async-start(bf16[32,80,128]{2,1,0:T(8,128)(2,1)} %broadcast_in_dim.37), calls=%async_computation.14 | async-start | bytes 1310720 | tf_op jit(solution)/shard_map/all_to_all | solution.py:190
  19.6 0.0 copy-done.6
  19.6 2.5 %collective-permute-start.1 = (bf16[64,64,128]{2,1,0:T(8,128)(2,1)S(1)}, bf16[64,64,128]{2,1,0:T(8,128)(2,1)}, u32[]{:S(2)}, u32[]{:S(2)}) collective-permute-start(bf16[64,64,128]{2,1,0:T(8,128)(2,1)S(1)} %bitcast.34), channel_id=1, source_target_pairs={{0,256},{256,0},{1,257},{257,1},{2,258},{258,2},{3,259},{259,3},{4... | collective-permute-start | bytes 3145736 | tf_op jit(solution)/shard_map/ppermute | solution.py:212
  22.1 0.0 copy-done.7
  22.1 1.9 %collective-permute-start.2 = (bf16[64,64,128]{2,1,0:T(8,128)(2,1)S(1)}, bf16[64,64,128]{2,1,0:T(8,128)(2,1)}, u32[]{:S(2)}, u32[]{:S(2)}) collective-permute-start(bf16[64,64,128]{2,1,0:T(8,128)(2,1)S(1)} %bitcast.37), channel_id=1, source_target_pairs={{0,256},{256,0},{1,257},{257,1},{2,258},{258,2},{3,259},{259,3},{4... | collective-permute-start | bytes 3145736 | tf_op jit(solution)/shard_map/ppermute | solution.py:212
  24.1 0.4 collective-permute-done.1
  24.5 2.3 %collective-permute-done.2 = bf16[64,64,128]{2,1,0:T(8,128)(2,1)} collective-permute-done((bf16[64,64,128]{2,1,0:T(8,128)(2,1)S(1)}, bf16[64,64,128]{2,1,0:T(8,128)(2,1)}, u32[]{:S(2)}, u32[]{:S(2)}) %collective-permute-start.2) | collective-permute-done | bytes 1048608 | tf_op jit(solution)/shard_map/ppermute | solution.py:212
  26.8 9.6 %all-to-all-done.14 = bf16[32,80,128]{2,1,0:T(8,128)(2,1)S(1)} async-done(((bf16[32,80,128]{2,1,0:T(8,128)(2,1)}), bf16[32,80,128]{2,1,0:T(8,128)(2,1)S(1)}, u32[]{:S(2)}, u32[]{:S(2)}) %all-to-all-start.14) | async-done | bytes 655392 | tf_op jit(solution)/shard_map/all_to_all | solution.py:190
  36.4 123.2 %conditional.4 = (f32[32,128]{1,0:T(8,128)S(1)}, bf16[32,128]{1,0:T(8,128)(2,1)S(1)}) conditional(s32[]{:T(128)} %convert_element_type.73, (bf16[32,128]{1,0:T(8,128)(2,1)S(1)}, bf16[32,80,128]{2,1,0:T(8,128)(2,1)S(1)}, s32[2,128]{1,0:T(2,128)S(1)}, s32[2,128]{1,0:T(2,128)S(1)}, bf16[64,64,128]{2,1,0:T(8,128)(2,1)}, ...), branch_computations={%region_0.5_spmd, %region_5.10_spmd} | conditional | flops 6002650112 | bytes 24940648
  36.4 0.1 slice.53
  36.5 2.9 %branch_1_fun.4 = bf16[8,2,64,256]{3,2,1,0:T(8,128)(2,1)S(1)} custom-call(s32[2,128]{1,0:T(2,128)S(1)} %get-tuple-element.72.refs_0_.index_in, s32[2,128]{1,0:T(2,128)S(1)} %get-tuple-element.73.refs_1_, bf16[32,2,32,128]{3,2,1,0:T(8,128)(2,1)S(1)} %bitcast.28, bf16[64,64,128]{2,1,0:T(8,128)(2,1)S(1)} %get-tuple-element.74.refs_3_.values_in, ...), custom_call_target="tpu_custom_call" | custom-call | flops 2000000000 | bytes 4194304 | tf_op jit(solution)/shard_map/cond/branch_1_fun/pallas_call | solution.py:91
  39.4 19.0 %all_to_all.67 = bf16[8,2,64,256]{3,2,1,0:T(8,128)(2,1)S(1)} all-to-all(bf16[8,2,64,256]{3,2,1,0:T(8,128)(2,1)S(1)} %branch_1_fun.4), channel_id=1, replica_groups=mesh['section'=2,'row'=8,'col'=32] {'row'}, dimensions={0} | all-to-all | bytes 1048576 | tf_op jit(solution)/shard_map/cond/branch_1_fun/all_to_all | solution.py:190
  58.4 0.1 convert_reduce_fusion.5
  58.6 11.7 %all_to_all.68.hidden_ref = bf16[8,64,256]{2,1,0:T(8,128)(2,1)S(1)} all-to-all(bf16[8,64,256]{2,1,0:T(8,128)(2,1)S(1)} %broadcast_in_dim.32), channel_id=1, replica_groups=mesh['section'=2,'row'=8,'col'=32] {'row'}, dimensions={0} | all-to-all | bytes 524288 | tf_op jit(solution)/shard_map/cond/branch_1_fun/all_to_all | solution.py:190
  70.3 2.0 %branch_1_fun.5 = bf16[32,32,128]{2,1,0:T(8,128)(2,1)S(1)} custom-call(s32[2,128]{1,0:T(2,128)S(1)} %get-tuple-element.72.refs_0_.index_in, bf16[8,64,256]{2,1,0:T(8,128)(2,1)S(1)} %all_to_all.68.hidden_ref, bf16[64,64,128]{2,1,0:T(8,128)(2,1)S(1)} %get-tuple-element.74.refs_3_.values_in), custom_call_target="tpu_custom_call" | custom-call | flops 1000000000 | bytes 2097152 | tf_op jit(solution)/shard_map/cond/branch_1_fun/pallas_call | solution.py:156
  72.3 21.3 %all_to_all.69 = bf16[32,32,128]{2,1,0:T(8,128)(2,1)S(1)} all-to-all(bf16[32,32,128]{2,1,0:T(8,128)(2,1)S(1)} %branch_1_fun.5), channel_id=1, replica_groups=mesh['section'=2,'row'=8,'col'=32] {'col'}, dimensions={0} | all-to-all | bytes 524288 | tf_op jit(solution)/shard_map/cond/branch_1_fun/all_to_all | solution.py:190
  93.7 0.0 copy-start.1
  93.7 0.6 copy-done.1
  94.3 0.8 broadcast_in_dim.33
  95.1 4.5 %all-to-all-start.10 = ((bf16[32,48,128]{2,1,0:T(8,128)(2,1)}), bf16[32,48,128]{2,1,0:T(8,128)(2,1)S(1)}, u32[]{:S(2)}, u32[]{:S(2)}) async-start(bf16[32,48,128]{2,1,0:T(8,128)(2,1)} %broadcast_in_dim.33), calls=%async_computation.10 | async-start | bytes 786432 | tf_op jit(solution)/shard_map/cond/branch_1_fun/all_to_all | solution.py:190
  99.6 10.2 %all-to-all-done.10 = bf16[32,48,128]{2,1,0:T(8,128)(2,1)S(1)} async-done(((bf16[32,48,128]{2,1,0:T(8,128)(2,1)}), bf16[32,48,128]{2,1,0:T(8,128)(2,1)S(1)}, u32[]{:S(2)}, u32[]{:S(2)}) %all-to-all-start.10) | async-done | bytes 393248 | tf_op jit(solution)/shard_map/cond/branch_1_fun/all_to_all | solution.py:190
  109.9 3.5 %branch_1_fun.6 = bf16[8,2,64,256]{3,2,1,0:T(8,128)(2,1)S(1)} custom-call(s32[2,128]{1,0:T(2,128)S(1)} %get-tuple-element.68.refs_0_.index_in, s32[2,128]{1,0:T(2,128)S(1)} %get-tuple-element.69.refs_1_, bf16[32,2,32,128]{3,2,1,0:T(8,128)(2,1)S(1)} %pad_maximum_fusion.refs_2_, bf16[64,64,128]{2,1,0:T(8,128)(2,1)} %get-tuple-element.77.refs_3_.values_in, ...), custom_call_target="tpu_custom_call" | custom-call | flops 2000000000 | bytes 4194304 | tf_op jit(solution)/shard_map/cond/branch_1_fun/pallas_call | solution.py:91
  113.4 14.6 %all_to_all.70 = bf16[8,2,64,256]{3,2,1,0:T(8,128)(2,1)S(1)} all-to-all(bf16[8,2,64,256]{3,2,1,0:T(8,128)(2,1)S(1)} %branch_1_fun.6), channel_id=1, replica_groups=mesh['section'=2,'row'=8,'col'=32] {'row'}, dimensions={0} | all-to-all | bytes 1048576 | tf_op jit(solution)/shard_map/cond/branch_1_fun/all_to_all | solution.py:190
  128.0 0.1 convert_reduce_fusion.4
  128.1 11.7 %all_to_all.71.hidden_ref = bf16[8,64,256]{2,1,0:T(8,128)(2,1)S(1)} all-to-all(bf16[8,64,256]{2,1,0:T(8,128)(2,1)S(1)} %broadcast_in_dim.35), channel_id=1, replica_groups=mesh['section'=2,'row'=8,'col'=32] {'row'}, dimensions={0} | all-to-all | bytes 524288 | tf_op jit(solution)/shard_map/cond/branch_1_fun/all_to_all | solution.py:190
  139.9 2.7 %branch_1_fun.7 = bf16[32,32,128]{2,1,0:T(8,128)(2,1)S(1)} custom-call(s32[2,128]{1,0:T(2,128)S(1)} %get-tuple-element.68.refs_0_.index_in, bf16[8,64,256]{2,1,0:T(8,128)(2,1)S(1)} %all_to_all.71.hidden_ref, bf16[64,64,128]{2,1,0:T(8,128)(2,1)} %get-tuple-element.77.refs_3_.values_in), custom_call_target="tpu_custom_call" | custom-call | flops 1000000000 | bytes 2097152 | tf_op jit(solution)/shard_map/cond/branch_1_fun/pallas_call | solution.py:156
  142.5 16.3 %all_to_all.72 = bf16[32,32,128]{2,1,0:T(8,128)(2,1)S(1)} all-to-all(bf16[32,32,128]{2,1,0:T(8,128)(2,1)S(1)} %branch_1_fun.7), channel_id=1, replica_groups=mesh['section'=2,'row'=8,'col'=32] {'col'}, dimensions={0} | all-to-all | bytes 524288 | tf_op jit(solution)/shard_map/cond/branch_1_fun/all_to_all | solution.py:190
  158.9 0.0 copy-start.2
  158.9 0.6 copy-done.2
  159.6 8.0 %collective-permute-start.3 = (bf16[32,128]{1,0:T(8,128)(2,1)S(1)}, bf16[32,128]{1,0:T(8,128)(2,1)S(1)}, u32[]{:S(2)}, u32[]{:S(2)}) collective-permute-start(bf16[32,128]{1,0:T(8,128)(2,1)S(1)} %get-tuple-element.95), channel_id=1, source_target_pairs={{0,256},{256,0},{1,257},{257,1},{2,258},{258,2},{3,259},{259,3},{4... | collective-permute-start | bytes 24584 | tf_op jit(solution)/shard_map/ppermute | solution.py:212
  167.6 0.8 collective-permute-done.3
  168.4 0.6 select_n.54
  (27 shorter events, 0.5 us)
Async XLA Ops:
  0.0 10.3 %copy-start = (bf16[1,4,2048]{2,1,0:T(4,128)(2,1)S(1)}, bf16[1,4,2048]{2,1,0:T(4,128)(2,1)}, u32[]{:S(2)}) copy-start(bf16[1,4,2048]{2,1,0:T(4,128)(2,1)} %param.9) | copy-start | bytes 49156
  0.0 0.7 copy-start.3
  0.8 0.7 copy-start.4
  0.8 0.7 copy-start.5
  1.5 9.6 %collective-permute-start = (bf16[48,128]{1,0:T(8,128)(2,1)S(1)}, bf16[48,128]{1,0:T(8,128)(2,1)S(1)}, u32[]{:S(2)}, u32[]{:S(2)}) collective-permute-start(bf16[48,128]{1,0:T(8,128)(2,1)S(1)} %pad_maximum_fusion.3), channel_id=1, source_target_pairs={{0,256},{256,0},{1,257},{257,1},{2,258},{258,2},{3,259},{259,3},{4... | collective-permute-start | bytes 36872 | tf_op jit(solution)/shard_map/ppermute | solution.py:212
  10.3 9.2 %copy-start.6 = (bf16[1,1,1,64,64,128]{5,4,3,2,1,0:T(8,128)(2,1)S(1)}, bf16[1,1,1,64,64,128]{5,4,3,2,1,0:T(8,128)(2,1)}, u32[]{:S(2)}) copy-start(bf16[1,1,1,64,64,128]{5,4,3,2,1,0:T(8,128)(2,1)} %param.10) | copy-start | bytes 3145732
  10.3 11.8 %copy-start.7 = (bf16[1,1,1,64,64,128]{5,4,3,2,1,0:T(8,128)(2,1)S(1)}, bf16[1,1,1,64,64,128]{5,4,3,2,1,0:T(8,128)(2,1)}, u32[]{:S(2)}) copy-start(bf16[1,1,1,64,64,128]{5,4,3,2,1,0:T(8,128)(2,1)} %param.12) | copy-start | bytes 3145732
  12.1 24.3 %all-to-all-start.14 = ((bf16[32,80,128]{2,1,0:T(8,128)(2,1)}), bf16[32,80,128]{2,1,0:T(8,128)(2,1)S(1)}, u32[]{:S(2)}, u32[]{:S(2)}) async-start(bf16[32,80,128]{2,1,0:T(8,128)(2,1)} %broadcast_in_dim.37), calls=%async_computation.14 | async-start | bytes 1310720 | tf_op jit(solution)/shard_map/all_to_all | solution.py:190
  19.6 4.9 %collective-permute-start.1 = (bf16[64,64,128]{2,1,0:T(8,128)(2,1)S(1)}, bf16[64,64,128]{2,1,0:T(8,128)(2,1)}, u32[]{:S(2)}, u32[]{:S(2)}) collective-permute-start(bf16[64,64,128]{2,1,0:T(8,128)(2,1)S(1)} %bitcast.34), channel_id=1, source_target_pairs={{0,256},{256,0},{1,257},{257,1},{2,258},{258,2},{3,259},{259,3},{4... | collective-permute-start | bytes 3145736 | tf_op jit(solution)/shard_map/ppermute | solution.py:212
  22.1 4.7 %collective-permute-start.2 = (bf16[64,64,128]{2,1,0:T(8,128)(2,1)S(1)}, bf16[64,64,128]{2,1,0:T(8,128)(2,1)}, u32[]{:S(2)}, u32[]{:S(2)}) collective-permute-start(bf16[64,64,128]{2,1,0:T(8,128)(2,1)S(1)} %bitcast.37), channel_id=1, source_target_pairs={{0,256},{256,0},{1,257},{257,1},{2,258},{258,2},{3,259},{259,3},{4... | collective-permute-start | bytes 3145736 | tf_op jit(solution)/shard_map/ppermute | solution.py:212
  93.7 0.6 copy-start.1
  95.1 14.7 %all-to-all-start.10 = ((bf16[32,48,128]{2,1,0:T(8,128)(2,1)}), bf16[32,48,128]{2,1,0:T(8,128)(2,1)S(1)}, u32[]{:S(2)}, u32[]{:S(2)}) async-start(bf16[32,48,128]{2,1,0:T(8,128)(2,1)} %broadcast_in_dim.33), calls=%async_computation.10 | async-start | bytes 786432 | tf_op jit(solution)/shard_map/cond/branch_1_fun/all_to_all | solution.py:190
  158.9 0.7 copy-start.2
  159.6 8.8 %collective-permute-start.3 = (bf16[32,128]{1,0:T(8,128)(2,1)S(1)}, bf16[32,128]{1,0:T(8,128)(2,1)S(1)}, u32[]{:S(2)}, u32[]{:S(2)}) collective-permute-start(bf16[32,128]{1,0:T(8,128)(2,1)S(1)} %get-tuple-element.95), channel_id=1, source_target_pairs={{0,256},{256,0},{1,257},{257,1},{2,258},{258,2},{3,259},{259,3},{4... | collective-permute-start | bytes 24584 | tf_op jit(solution)/shard_map/ppermute | solution.py:212

commit v9 on v6

--- a/solution.py
+++ b/solution.py
@@ -11,7 +11,7 @@
 BLK = 64
 PER_COL = 2
 SWAP = [(0, 1), (1, 0)]
-UNROLL = 32
+UNROLL = 64
 VMEM = pl.BlockSpec(memory_space=pltpu.VMEM)
 ANY = pl.BlockSpec(memory_space=pl.ANY)
 

time: 169 us -> 169 us (level)
  no operation moved by 1% of the time
where the time goes in v9:
time: 169 us; the launch traced here: 168 us
  blocking collectives  92.9 us (55%)
  starting transfers between devices  36.8 us (22%)
  waiting for transfers between devices  21.3 us (13%)
  Pallas kernels  11.5 us (7%)
  local copies, waits for them, and re-layouts  4.58 us (3%)
    all_to_all x6, blocking collectives, exchange(): return lax.all_to_all(v, axis, 0, 0)  92.9 us
    ppermute x4, starting transfers between devices, swap(): return lax.ppermute(v, 'section', SWAP)  23.8 us
    all_to_all x2, waiting for transfers between devices, exchange(): return lax.all_to_all(v, axis, 0, 0)  17 us
    all_to_all x2, starting transfers between devices, exchange(): return lax.all_to_all(v, axis, 0, 0)  13 us
    pallas_call x3, Pallas kernels, forward(): pl.pallas_call(functools.partial(forward_kernel, count, ahead), out_shape...  6.99 us
    pallas_call x2, Pallas kernels, backward(): pl.pallas_call(backward_kernel, out_shape=jax.ShapeDtypeStruct((n_col, pe...  4.54 us
    ppermute x4, waiting for transfers between devices, swap(): return lax.ppermute(v, 'section', SWAP)  4.26 us
  transfers between devices with their start and end apart: 6, of which 6 were waited for; matrix products, arithmetic and copies ran while one was open for 0% of the time, Pallas kernels for 1%

profile of v9, /device:TPU:1, one launch (start us, length us, event | category | flops | bytes accessed | tf_op | source)
XLA Modules:
  0.0 167.7 jit_solution(6281332741345127347)
XLA Ops:
  0.0 0.0 copy-start
  0.0 0.0 copy-start.3
  0.0 0.7 copy-done.3
  0.8 0.0 copy-start.4
  0.8 0.0 copy-start.5
  0.8 0.6 copy-done.4
  1.4 0.0 copy-done.5
  1.5 8.8 %collective-permute-start = (bf16[48,128]{1,0:T(8,128)(2,1)S(1)}, bf16[48,128]{1,0:T(8,128)(2,1)S(1)}, u32[]{:S(2)}, u32[]{:S(2)}) collective-permute-start(bf16[48,128]{1,0:T(8,128)(2,1)S(1)} %pad_maximum_fusion.1), channel_id=1, source_target_pairs={{0,256},{256,0},{1,257},{257,1},{2,258},{258,2},{3,259},{259,3},{4... | collective-permute-start | bytes 36872 | tf_op jit(solution)/shard_map/ppermute | solution.py:212
  10.3 0.0 copy-done
  10.3 0.0 copy-start.6
  10.3 0.0 copy-start.7
  10.4 0.7 collective-permute-done
  11.1 0.9 broadcast_in_dim.39
  12.0 7.5 %all-to-all-start.14 = ((bf16[32,80,128]{2,1,0:T(8,128)(2,1)}), bf16[32,80,128]{2,1,0:T(8,128)(2,1)S(1)}, u32[]{:S(2)}, u32[]{:S(2)}) async-start(bf16[32,80,128]{2,1,0:T(8,128)(2,1)} %broadcast_in_dim.39), calls=%async_computation.14 | async-start | bytes 1310720 | tf_op jit(solution)/shard_map/all_to_all | solution.py:190
  19.6 0.0 copy-done.6
  19.6 2.5 %collective-permute-start.1 = (bf16[64,64,128]{2,1,0:T(8,128)(2,1)S(1)}, bf16[64,64,128]{2,1,0:T(8,128)(2,1)}, u32[]{:S(2)}, u32[]{:S(2)}) collective-permute-start(bf16[64,64,128]{2,1,0:T(8,128)(2,1)S(1)} %bitcast.30), channel_id=1, source_target_pairs={{0,256},{256,0},{1,257},{257,1},{2,258},{258,2},{3,259},{259,3},{4... | collective-permute-start | bytes 3145736 | tf_op jit(solution)/shard_map/ppermute | solution.py:212
  22.1 0.0 copy-done.7
  22.1 1.9 %collective-permute-start.2 = (bf16[64,64,128]{2,1,0:T(8,128)(2,1)S(1)}, bf16[64,64,128]{2,1,0:T(8,128)(2,1)}, u32[]{:S(2)}, u32[]{:S(2)}) collective-permute-start(bf16[64,64,128]{2,1,0:T(8,128)(2,1)S(1)} %bitcast.33), channel_id=1, source_target_pairs={{0,256},{256,0},{1,257},{257,1},{2,258},{258,2},{3,259},{259,3},{4... | collective-permute-start | bytes 3145736 | tf_op jit(solution)/shard_map/ppermute | solution.py:212
  24.1 0.4 collective-permute-done.1
  24.5 2.3 %collective-permute-done.2 = bf16[64,64,128]{2,1,0:T(8,128)(2,1)} collective-permute-done((bf16[64,64,128]{2,1,0:T(8,128)(2,1)S(1)}, bf16[64,64,128]{2,1,0:T(8,128)(2,1)}, u32[]{:S(2)}, u32[]{:S(2)}) %collective-permute-start.2) | collective-permute-done | bytes 1048608 | tf_op jit(solution)/shard_map/ppermute | solution.py:212
  26.8 9.6 %all-to-all-done.14 = bf16[32,80,128]{2,1,0:T(8,128)(2,1)S(1)} async-done(((bf16[32,80,128]{2,1,0:T(8,128)(2,1)}), bf16[32,80,128]{2,1,0:T(8,128)(2,1)S(1)}, u32[]{:S(2)}, u32[]{:S(2)}) %all-to-all-start.14) | async-done | bytes 655392 | tf_op jit(solution)/shard_map/all_to_all | solution.py:190
  36.4 119.3 %conditional.4 = (f32[32,128]{1,0:T(8,128)S(1)}, bf16[32,128]{1,0:T(8,128)(2,1)S(1)}) conditional(s32[]{:T(128)} %convert_element_type.73, (bf16[32,128]{1,0:T(8,128)(2,1)S(1)}, bf16[32,80,128]{2,1,0:T(8,128)(2,1)S(1)}, s32[2,128]{1,0:T(2,128)S(1)}, s32[2,128]{1,0:T(2,128)S(1)}, bf16[64,64,128]{2,1,0:T(8,128)(2,1)}, ...), branch_computations={%region_0.5_spmd, %region_5.10_spmd} | conditional | flops 6002363392 | bytes 23076968
  36.4 0.1 slice.52
  36.5 2.7 %branch_1_fun.5 = bf16[8,2,64,256]{3,2,1,0:T(8,128)(2,1)S(1)} custom-call(s32[2,128]{1,0:T(2,128)S(1)} %get-tuple-element.71.refs_0_.index_in, s32[2,128]{1,0:T(2,128)S(1)} %get-tuple-element.72.refs_1_, bf16[32,2,32,128]{3,2,1,0:T(8,128)(2,1)S(1)} %bitcast.24, bf16[64,64,128]{2,1,0:T(8,128)(2,1)S(1)} %get-tuple-element.74.refs_3_.values_in, ...), custom_call_target="tpu_custom_call" | custom-call | flops 2000000000 | bytes 4194304 | tf_op jit(solution)/shard_map/cond/branch_1_fun/pallas_call | solution.py:91
  39.1 19.0 %all_to_all.67 = bf16[8,2,64,256]{3,2,1,0:T(8,128)(2,1)S(1)} all-to-all(bf16[8,2,64,256]{3,2,1,0:T(8,128)(2,1)S(1)} %branch_1_fun.5), channel_id=1, replica_groups=mesh['section'=2,'row'=8,'col'=32] {'row'}, dimensions={0} | all-to-all | bytes 1048576 | tf_op jit(solution)/shard_map/cond/branch_1_fun/all_to_all | solution.py:190
  58.1 0.1 convert_reduce_fusion.5
  58.3 11.7 %all_to_all.68.hidden_ref = bf16[8,64,256]{2,1,0:T(8,128)(2,1)S(1)} all-to-all(bf16[8,64,256]{2,1,0:T(8,128)(2,1)S(1)} %broadcast_in_dim.33), channel_id=1, replica_groups=mesh['section'=2,'row'=8,'col'=32] {'row'}, dimensions={0} | all-to-all | bytes 524288 | tf_op jit(solution)/shard_map/cond/branch_1_fun/all_to_all | solution.py:190
  70.0 1.9 %branch_1_fun.6 = bf16[32,48,128]{2,1,0:T(8,128)(2,1)S(1)} custom-call(s32[2,128]{1,0:T(2,128)S(1)} %get-tuple-element.71.refs_0_.index_in, bf16[8,64,256]{2,1,0:T(8,128)(2,1)S(1)} %all_to_all.68.hidden_ref, bf16[64,64,128]{2,1,0:T(8,128)(2,1)S(1)} %get-tuple-element.74.refs_3_.values_in, bf16[16,128]{1,0:T(8,128)(2,1)S(1)} %get-tuple-element.76.refs_0_), custom_call_target="tpu_custom_call" | custom-call | flops 1000000000 | bytes 2097152 | tf_op jit(solution)/shard_map/cond/branch_1_fun/pallas_call | solution.py:156
  71.9 21.9 %all_to_all.69 = bf16[32,48,128]{2,1,0:T(8,128)(2,1)S(1)} all-to-all(bf16[32,48,128]{2,1,0:T(8,128)(2,1)S(1)} %branch_1_fun.6), channel_id=1, replica_groups=mesh['section'=2,'row'=8,'col'=32] {'col'}, dimensions={0} | all-to-all | bytes 786432 | tf_op jit(solution)/shard_map/cond/branch_1_fun/all_to_all | solution.py:190
  94.0 0.0 copy-start.1
  94.0 0.8 broadcast_in_dim.34
  94.7 0.0 copy-done.1
  94.7 5.5 %all-to-all-start.10 = ((bf16[32,1,32,128]{3,2,1,0:T(8,128)(2,1)}), bf16[32,1,32,128]{3,2,1,0:T(8,128)(2,1)S(1)}, u32[]{:S(2)}, u32[]{:S(2)}) async-start(bf16[32,1,32,128]{3,2,1,0:T(8,128)(2,1)} %broadcast_in_dim.34), calls=%async_computation.10 | async-start | bytes 524288 | tf_op jit(solution)/shard_map/cond/branch_1_fun/all_to_all | solution.py:190
  100.3 2.2 %branch_1_fun.7.refs_3_ = bf16[8,1,64,256]{3,2,1,0:T(8,128)(2,1)S(1)} custom-call(s32[2,128]{1,0:T(2,128)S(1)} %get-tuple-element.68.refs_0_.index_in, bf16[32,1,32,128]{3,2,1,0:T(8,128)(2,1)S(1)} %maximum_bitcast_fusion.1.refs_1_, bf16[64,64,128]{2,1,0:T(8,128)(2,1)} %get-tuple-element.78.refs_2_.values_in), custom_call_target="tpu_custom_call" | custom-call | flops 1000000000 | bytes 2097152 | tf_op jit(solution)/shard_map/cond/branch_1_fun/pallas_call | solution.py:91
  102.4 7.4 %all-to-all-done.10.refs_1_ = bf16[32,1,32,128]{3,2,1,0:T(8,128)(2,1)S(1)} async-done(((bf16[32,1,32,128]{3,2,1,0:T(8,128)(2,1)}), bf16[32,1,32,128]{3,2,1,0:T(8,128)(2,1)S(1)}, u32[]{:S(2)}, u32[]{:S(2)}) %all-to-all-start.10) | async-done | bytes 262176 | tf_op jit(solution)/shard_map/cond/branch_1_fun/all_to_all | solution.py:190
  109.9 2.2 %branch_1_fun.8 = bf16[8,2,64,256]{3,2,1,0:T(8,128)(2,1)S(1)} custom-call(s32[2,128]{1,0:T(2,128)S(1)} %get-tuple-element.69.refs_0_, bf16[32,1,32,128]{3,2,1,0:T(8,128)(2,1)S(1)} %all-to-all-done.10.refs_1_, bf16[64,64,128]{2,1,0:T(8,128)(2,1)} %get-tuple-element.77.refs_2_, bf16[8,1,64,256]{3,2,1,0:T(8,128)(2,1)S(1)} %branch_1_fun.7.refs_3_), custom_call_target="tpu_custom_call" | custom-call | flops 1000000000 | bytes 2097152 | tf_op jit(solution)/shard_map/cond/branch_1_fun/pallas_call | solution.py:91
  112.0 14.7 %all_to_all.70 = bf16[8,2,64,256]{3,2,1,0:T(8,128)(2,1)S(1)} all-to-all(bf16[8,2,64,256]{3,2,1,0:T(8,128)(2,1)S(1)} %branch_1_fun.8), channel_id=1, replica_groups=mesh['section'=2,'row'=8,'col'=32] {'row'}, dimensions={0} | all-to-all | bytes 1048576 | tf_op jit(solution)/shard_map/cond/branch_1_fun/all_to_all | solution.py:190
  126.7 0.1 convert_reduce_fusion.4
  126.8 11.7 %all_to_all.71.hidden_ref = bf16[8,64,256]{2,1,0:T(8,128)(2,1)S(1)} all-to-all(bf16[8,64,256]{2,1,0:T(8,128)(2,1)S(1)} %broadcast_in_dim.37), channel_id=1, replica_groups=mesh['section'=2,'row'=8,'col'=32] {'row'}, dimensions={0} | all-to-all | bytes 524288 | tf_op jit(solution)/shard_map/cond/branch_1_fun/all_to_all | solution.py:190
  138.6 2.6 %branch_1_fun.9 = bf16[32,32,128]{2,1,0:T(8,128)(2,1)S(1)} custom-call(s32[2,128]{1,0:T(2,128)S(1)} %get-tuple-element.68.refs_0_.index_in, bf16[8,64,256]{2,1,0:T(8,128)(2,1)S(1)} %all_to_all.71.hidden_ref, bf16[64,64,128]{2,1,0:T(8,128)(2,1)} %get-tuple-element.78.refs_2_.values_in), custom_call_target="tpu_custom_call" | custom-call | flops 1000000000 | bytes 2097152 | tf_op jit(solution)/shard_map/cond/branch_1_fun/pallas_call | solution.py:156
  141.2 13.9 %all_to_all.72 = bf16[32,32,128]{2,1,0:T(8,128)(2,1)S(1)} all-to-all(bf16[32,32,128]{2,1,0:T(8,128)(2,1)S(1)} %branch_1_fun.9), channel_id=1, replica_groups=mesh['section'=2,'row'=8,'col'=32] {'col'}, dimensions={0} | all-to-all | bytes 524288 | tf_op jit(solution)/shard_map/cond/branch_1_fun/all_to_all | solution.py:190
  155.0 0.0 copy-start.2
  155.1 0.6 copy-done.2
  155.7 10.5 %collective-permute-start.3 = (bf16[32,128]{1,0:T(8,128)(2,1)S(1)}, bf16[32,128]{1,0:T(8,128)(2,1)S(1)}, u32[]{:S(2)}, u32[]{:S(2)}) collective-permute-start(bf16[32,128]{1,0:T(8,128)(2,1)S(1)} %get-tuple-element.93), channel_id=1, source_target_pairs={{0,256},{256,0},{1,257},{257,1},{2,258},{258,2},{3,259},{259,3},{4... | collective-permute-start | bytes 24584 | tf_op jit(solution)/shard_map/ppermute | solution.py:212
  166.3 0.8 collective-permute-done.3
  167.1 0.6 select_n.54
  (25 shorter events, 0.4 us)
Async XLA Ops:
  0.0 10.3 %copy-start = (bf16[1,4,2048]{2,1,0:T(4,128)(2,1)S(1)}, bf16[1,4,2048]{2,1,0:T(4,128)(2,1)}, u32[]{:S(2)}) copy-start(bf16[1,4,2048]{2,1,0:T(4,128)(2,1)} %param.9) | copy-start | bytes 49156
  0.0 0.7 copy-start.3
  0.8 0.7 copy-start.4
  0.8 0.7 copy-start.5
  1.5 9.6 %collective-permute-start = (bf16[48,128]{1,0:T(8,128)(2,1)S(1)}, bf16[48,128]{1,0:T(8,128)(2,1)S(1)}, u32[]{:S(2)}, u32[]{:S(2)}) collective-permute-start(bf16[48,128]{1,0:T(8,128)(2,1)S(1)} %pad_maximum_fusion.1), channel_id=1, source_target_pairs={{0,256},{256,0},{1,257},{257,1},{2,258},{258,2},{3,259},{259,3},{4... | collective-permute-start | bytes 36872 | tf_op jit(solution)/shard_map/ppermute | solution.py:212
  10.3 9.2 %copy-start.6 = (bf16[1,1,1,64,64,128]{5,4,3,2,1,0:T(8,128)(2,1)S(1)}, bf16[1,1,1,64,64,128]{5,4,3,2,1,0:T(8,128)(2,1)}, u32[]{:S(2)}) copy-start(bf16[1,1,1,64,64,128]{5,4,3,2,1,0:T(8,128)(2,1)} %param.10) | copy-start | bytes 3145732
  10.3 11.8 %copy-start.7 = (bf16[1,1,1,64,64,128]{5,4,3,2,1,0:T(8,128)(2,1)S(1)}, bf16[1,1,1,64,64,128]{5,4,3,2,1,0:T(8,128)(2,1)}, u32[]{:S(2)}) copy-start(bf16[1,1,1,64,64,128]{5,4,3,2,1,0:T(8,128)(2,1)} %param.12) | copy-start | bytes 3145732
  12.0 24.3 %all-to-all-start.14 = ((bf16[32,80,128]{2,1,0:T(8,128)(2,1)}), bf16[32,80,128]{2,1,0:T(8,128)(2,1)S(1)}, u32[]{:S(2)}, u32[]{:S(2)}) async-start(bf16[32,80,128]{2,1,0:T(8,128)(2,1)} %broadcast_in_dim.39), calls=%async_computation.14 | async-start | bytes 1310720 | tf_op jit(solution)/shard_map/all_to_all | solution.py:190
  19.6 4.9 %collective-permute-start.1 = (bf16[64,64,128]{2,1,0:T(8,128)(2,1)S(1)}, bf16[64,64,128]{2,1,0:T(8,128)(2,1)}, u32[]{:S(2)}, u32[]{:S(2)}) collective-permute-start(bf16[64,64,128]{2,1,0:T(8,128)(2,1)S(1)} %bitcast.30), channel_id=1, source_target_pairs={{0,256},{256,0},{1,257},{257,1},{2,258},{258,2},{3,259},{259,3},{4... | collective-permute-start | bytes 3145736 | tf_op jit(solution)/shard_map/ppermute | solution.py:212
  22.1 4.7 %collective-permute-start.2 = (bf16[64,64,128]{2,1,0:T(8,128)(2,1)S(1)}, bf16[64,64,128]{2,1,0:T(8,128)(2,1)}, u32[]{:S(2)}, u32[]{:S(2)}) collective-permute-start(bf16[64,64,128]{2,1,0:T(8,128)(2,1)S(1)} %bitcast.33), channel_id=1, source_target_pairs={{0,256},{256,0},{1,257},{257,1},{2,258},{258,2},{3,259},{259,3},{4... | collective-permute-start | bytes 3145736 | tf_op jit(solution)/shard_map/ppermute | solution.py:212
  94.0 0.8 copy-start.1
  94.7 15.1 %all-to-all-start.10 = ((bf16[32,1,32,128]{3,2,1,0:T(8,128)(2,1)}), bf16[32,1,32,128]{3,2,1,0:T(8,128)(2,1)S(1)}, u32[]{:S(2)}, u32[]{:S(2)}) async-start(bf16[32,1,32,128]{3,2,1,0:T(8,128)(2,1)} %broadcast_in_dim.34), calls=%async_computation.10 | async-start | bytes 524288 | tf_op jit(solution)/shard_map/cond/branch_1_fun/all_to_all | solution.py:190
  155.0 0.7 copy-start.2
  155.7 11.4 %collective-permute-start.3 = (bf16[32,128]{1,0:T(8,128)(2,1)S(1)}, bf16[32,128]{1,0:T(8,128)(2,1)S(1)}, u32[]{:S(2)}, u32[]{:S(2)}) collective-permute-start(bf16[32,128]{1,0:T(8,128)(2,1)S(1)} %get-tuple-element.93), channel_id=1, source_target_pairs={{0,256},{256,0},{1,257},{257,1},{2,258},{258,2},{3,259},{259,3},{4... | collective-permute-start | bytes 24584 | tf_op jit(solution)/shard_map/ppermute | solution.py:212
